TPU v7x, 32 devices: a whole 2x2x4 slice. The times are simulated.
32 devices in a mesh: dp: 4 (over y, x), wide: 8 (over z, core).
Axes of the slice: x: 2, y: 2, z: 4, core: 2. Of those that a mesh axis runs over, the one named last changes fastest.
Arguments:
- chars: bfloat16 [32, 8, 64, 16, 256], P(('dp', 'wide')), may hold values from -6 to 6
- char_counts: int32 [32, 8, 64], P(('dp', 'wide')), may hold values from 1 to 16
- buckets: int32 [32, 256, 1], P(('dp', 'wide')), may hold values from 0 to 7; in each aligned block of 256 rows (0 to 255, 256 to 511, ..., all dimensions but the last counted through in order) at most 64 rows name the same one
- assign: int32 [8], replicated, may hold values from 0 to 7, each once
- segments: int32 [32, 256], P(('dp', 'wide')), may hold values from 0 to 15, never falling along the last dimension, each value on 1 to 128 neighbouring positions
- char_gain: bfloat16 [256], P('wide'), may hold values from 0.5 to 1.5
- char_shift: bfloat16 [256], P('wide'), may hold values from -1 to 1
- char_inproj: bfloat16 [256, 768], P('wide'), may hold values from -0.375 to 0.375
- char_outproj: bfloat16 [256, 256], P('wide'), may hold values from -0.75 to 0.75
- char_gain_mid: bfloat16 [256], P('wide'), may hold values from 0.5 to 1.5
- char_shift_mid: bfloat16 [256], P('wide'), may hold values from -1 to 1
- char_up: bfloat16 [256, 1024], P('wide'), may hold values from -0.375 to 0.375
- char_up_bias: bfloat16 [1024], P('wide'), may hold values from -1.5 to 1.5
- char_down: bfloat16 [1024, 256], P('wide'), may hold values from -0.1875 to 0.1875
- char_down_bias: bfloat16 [256], P('wide'), may hold values from -1.5 to 1.5
- pool_query: bfloat16 [256], P('wide'), may hold values from -4 to 4
- char_proj: bfloat16 [256, 512], P('wide'), may hold values from -0.375 to 0.375
- char_proj_bias: bfloat16 [512], P('wide'), may hold values from -1.5 to 1.5
- word_gain: bfloat16 [512], P('wide'), may hold values from 0.5 to 1.5
- word_shift: bfloat16 [512], P('wide'), may hold values from -1 to 1
- word_inproj: bfloat16 [512, 1536], P('wide'), may hold values from -0.25 to 0.25
- word_outproj: bfloat16 [512, 512], P('wide'), may hold values from -0.75 to 0.75
- word_gain_mid: bfloat16 [512], P('wide'), may hold values from 0.5 to 1.5
- word_shift_mid: bfloat16 [512], P('wide'), may hold values from -1 to 1
- word_up: bfloat16 [512, 2048], P('wide'), may hold values from -0.25 to 0.25
- word_up_bias: bfloat16 [2048], P('wide'), may hold values from -1.5 to 1.5
- word_down: bfloat16 [2048, 512], P('wide'), may hold values from -0.125 to 0.125
- word_down_bias: bfloat16 [512], P('wide'), may hold values from -1.5 to 1.5
- out_grad: bfloat16 [32, 256, 512], P(('dp', 'wide')), may hold values from -6 to 6
Outputs:
- word_output: float32 [32, 256, 512], P(('dp', 'wide'))
- grad_chars: float32 [32, 8, 64, 16, 256], P(('dp', 'wide'))
- grad_char_gain: float32 [256], P('wide')
- grad_char_shift: float32 [256], P('wide')
- grad_char_inproj: float32 [256, 768], P('wide')
- grad_char_outproj: float32 [256, 256], P('wide')
- grad_char_gain_mid: float32 [256], P('wide')
- grad_char_shift_mid: float32 [256], P('wide')
- grad_char_up: float32 [256, 1024], P('wide')
- grad_char_up_bias: float32 [1024], P('wide')
- grad_char_down: float32 [1024, 256], P('wide')
- grad_char_down_bias: float32 [256], P('wide')
- grad_pool_query: float32 [256], P('wide')
- grad_char_proj: float32 [256, 512], P('wide')
- grad_char_proj_bias: float32 [512], P('wide')
- grad_word_gain: float32 [512], P('wide')
- grad_word_shift: float32 [512], P('wide')
- grad_word_inproj: float32 [512, 1536], P('wide')
- grad_word_outproj: float32 [512, 512], P('wide')
- grad_word_gain_mid: float32 [512], P('wide')
- grad_word_shift_mid: float32 [512], P('wide')
- grad_word_up: float32 [512, 2048], P('wide')
- grad_word_up_bias: float32 [2048], P('wide')
- grad_word_down: float32 [2048, 512], P('wide')
- grad_word_down_bias: float32 [512], P('wide')
Inputs may be any that keep to these rules, and one draw needn't show every extreme that they name: `buckets`: within one sequence at most 64 words name the same bucket, and in some sequence one bucket is named by exactly 64. `assign`: A permutation of the buckets over the wide indices. `segments`: never falling along a sequence; each document has 1 to 128 words, and one has exactly that many.
All inputs are finite; a program needn't handle non-finite values.
Results may differ from a plain program's by a relative error of at most 0.023.
Values may be sent and summed in bfloat16 or wider, within the bound.
A program may use at most 192 MiB of HBM per device.

v0:
```python
import jax
import jax.numpy as jnp
from jax import lax
from jax.sharding import PartitionSpec as P

HEADS = 8
HD = 64
CHEADS = 4
CHD = 64


EPS = 1e-05
NEG = -1e30
ROOT_HALF = 0.7071067811865476
INV_ROOT_TWO_PI = 0.3989422804014327


def split_up(shard, dim, size):
    before, after = (shard.shape[:dim], shard.shape[dim + 1 :])
    return jnp.moveaxis(shard.reshape(*before, size, -1, *after), dim, 0)


def sum_at_owner(shard, axis, dim):
    parts = split_up(shard, dim, lax.axis_size(axis))
    arrived = lax.all_to_all(parts, axis, split_axis=0, concat_axis=0, tiled=True)
    return arrived.astype(jnp.float32).sum(axis=0)


def sent_together(arrays, axis, dim, along):
    columns = [a.reshape(*a.shape[:along], -1) for a in arrays]
    both = jnp.concatenate(columns, axis=along)
    filled, at, outs = (sum_at_owner(both, axis, dim), 0, [])
    for a, column in zip(arrays, columns):
        slab = filled[..., at : at + column.shape[along]]
        outs.append(slab.reshape(*slab.shape[:along], *a.shape[along:]))
        at += column.shape[along]
    return tuple(outs)


def dense(left, right):
    return jnp.dot(left, right, preferred_element_type=jnp.float32)


def dense_left(left, right):
    return lax.dot_general(
        left, right, (((0,), (0,)), ((), ())), preferred_element_type=jnp.float32
    )


def dense_right(left, right):
    return lax.dot_general(
        left, right, (((1,), (1,)), ((), ())), preferred_element_type=jnp.float32
    )


def rounded(value):
    return lax.optimization_barrier(value.astype(jnp.bfloat16)).astype(jnp.float32)


def gelu_exact(value):
    return 0.5 * value * (1.0 + lax.erf(value * ROOT_HALF))


def gelu_slope(value):
    return (
        0.5 * (1.0 + lax.erf(value * ROOT_HALF))
        + value * jnp.exp(-0.5 * value * value) * INV_ROOT_TWO_PI
    )


def softmax_rows(scores):
    row_max = jnp.max(scores, -1, keepdims=True)
    exponent = jnp.exp(scores - row_max)
    return exponent / jnp.sum(exponent, -1, keepdims=True)


def norm_forward(values, gain, shift):
    center = values - jnp.mean(values, -1, keepdims=True)
    inv_scale = lax.rsqrt(jnp.mean(center * center, -1, keepdims=True) + EPS)
    normal = center * inv_scale
    return (normal * gain.astype(jnp.float32) + shift.astype(jnp.float32), normal, inv_scale)


def norm_backward(upstream, normal, inv_scale, gain):
    weighted = upstream * gain.astype(jnp.float32)
    inner = (
        weighted
        - jnp.mean(weighted, -1, keepdims=True)
        - normal * jnp.mean(weighted * normal, -1, keepdims=True)
    )
    return (inv_scale * inner, jnp.sum(upstream * normal, 0), jnp.sum(upstream, 0))


def char_core(params, char_block, count_block):
    (
        gain_a,
        shift_a,
        inproj,
        outproj,
        gain_b,
        shift_b,
        up_weight,
        up_bias,
        down_weight,
        down_bias,
        query_vec,
        proj_weight,
        proj_bias,
    ) = params
    word_count, char_slots, feature_width = char_block.shape
    flat_rows = char_block.astype(jnp.float32).reshape(word_count * char_slots, feature_width)
    valid_mask = lax.broadcasted_iota(jnp.int32, (word_count, char_slots), 1) < count_block[:, None]
    normed, normal_a, scale_a = norm_forward(flat_rows, gain_a, shift_a)
    normed_low = normed.astype(jnp.bfloat16)
    triple = (
        dense(normed_low, inproj)
        .astype(jnp.bfloat16)
        .reshape(word_count, char_slots, 3, CHEADS, CHD)
    )
    query_rows = triple[:, :, 0]
    key_rows = triple[:, :, 1]
    value_rows = triple[:, :, 2]
    scores = jnp.einsum(
        "wihd,wjhd->whij", query_rows, key_rows, preferred_element_type=jnp.float32
    ) * CHD ** (-0.5)
    scores = jnp.where(valid_mask[:, None, None, :], scores, NEG)
    soft_weights = softmax_rows(scores)
    mixed = jnp.einsum(
        "whij,wjhd->wihd",
        soft_weights.astype(jnp.bfloat16),
        value_rows,
        preferred_element_type=jnp.float32,
    )
    mixed = mixed.astype(jnp.bfloat16).reshape(word_count * char_slots, feature_width)
    inner_sum = flat_rows + dense(mixed, outproj)
    spread, normal_b, scale_b = norm_forward(inner_sum, gain_b, shift_b)
    spread_low = spread.astype(jnp.bfloat16)
    before = dense(spread_low, up_weight) + up_bias.astype(jnp.float32)
    active = gelu_exact(before).astype(jnp.bfloat16)
    outer_sum = inner_sum + dense(active, down_weight) + down_bias.astype(jnp.float32)
    char_grid = outer_sum.reshape(word_count, char_slots, feature_width)
    attend = jnp.sum(char_grid * query_vec.astype(jnp.float32), -1) * feature_width ** (-0.5)
    pool_weights = softmax_rows(jnp.where(valid_mask, attend, NEG))
    pooled = jnp.sum(pool_weights[:, :, None] * char_grid, 1).astype(jnp.bfloat16)
    return (
        normal_a,
        scale_a,
        normed_low,
        query_rows,
        key_rows,
        value_rows,
        soft_weights,
        mixed,
        normal_b,
        scale_b,
        spread_low,
        before,
        active,
        char_grid,
        pool_weights,
        pooled,
    )


def char_send(params, char_block, count_block):
    pooled = char_core(params, char_block, count_block)[15]
    return (dense(pooled, params[11]) + params[12].astype(jnp.float32)).astype(jnp.bfloat16)


def char_back(params, char_block, count_block, incoming):
    (
        gain_a,
        shift_a,
        inproj,
        outproj,
        gain_b,
        shift_b,
        up_weight,
        up_bias,
        down_weight,
        down_bias,
        query_vec,
        proj_weight,
        proj_bias,
    ) = params
    (
        normal_a,
        scale_a,
        normed_low,
        query_rows,
        key_rows,
        value_rows,
        soft_weights,
        mixed,
        normal_b,
        scale_b,
        spread_low,
        before,
        active,
        char_grid,
        pool_weights,
        pooled,
    ) = char_core(params, char_block, count_block)
    word_count, char_slots, feature_width = char_block.shape
    pool_grad = rounded(dense_right(incoming, proj_weight))
    proj_grad = dense_left(pooled, incoming)
    proj_bias_grad = jnp.sum(incoming.astype(jnp.float32), 0)
    pool_factor = feature_width ** (-0.5)
    weight_grad = jnp.sum(char_grid * pool_grad[:, None, :], -1)
    attend_grad = pool_weights * (
        weight_grad - jnp.sum(pool_weights * weight_grad, -1, keepdims=True)
    )
    grid_grad = pool_weights[:, :, None] * pool_grad[:, None, :] + attend_grad[:, :, None] * (
        query_vec.astype(jnp.float32) * pool_factor
    )
    query_grad = jnp.sum(attend_grad[:, :, None] * char_grid, (0, 1)) * pool_factor
    outer_grad = grid_grad.reshape(word_count * char_slots, feature_width)
    outer_low = outer_grad.astype(jnp.bfloat16)
    down_grad = dense_left(active, outer_low)
    down_bias_grad = jnp.sum(outer_low.astype(jnp.float32), 0)
    before_low = (dense_right(outer_low, down_weight) * gelu_slope(before)).astype(jnp.bfloat16)
    up_grad = dense_left(spread_low, before_low)
    up_bias_grad = jnp.sum(before_low.astype(jnp.float32), 0)
    inner_part, gain_b_grad, shift_b_grad = norm_backward(
        dense_right(before_low, up_weight), normal_b, scale_b, gain_b
    )
    inner_grad = outer_grad + inner_part
    inner_low = inner_grad.astype(jnp.bfloat16)
    outproj_grad = dense_left(mixed, inner_low)
    mixed_grad = (
        dense_right(inner_low, outproj)
        .astype(jnp.bfloat16)
        .reshape(word_count, char_slots, CHEADS, CHD)
    )
    soft_grad = jnp.einsum(
        "wihd,wjhd->whij", mixed_grad, value_rows, preferred_element_type=jnp.float32
    )
    value_grad = jnp.einsum(
        "whij,wihd->wjhd",
        soft_weights.astype(jnp.bfloat16),
        mixed_grad,
        preferred_element_type=jnp.float32,
    )
    score_grad = (
        soft_weights * (soft_grad - jnp.sum(soft_grad * soft_weights, -1, keepdims=True))
    ).astype(jnp.bfloat16)
    query_part = jnp.einsum(
        "whij,wjhd->wihd", score_grad, key_rows, preferred_element_type=jnp.float32
    ) * CHD ** (-0.5)
    key_part = jnp.einsum(
        "whij,wihd->wjhd", score_grad, query_rows, preferred_element_type=jnp.float32
    ) * CHD ** (-0.5)
    triple_grad = (
        jnp.stack((query_part, key_part, value_grad), 2)
        .reshape(word_count * char_slots, 3 * feature_width)
        .astype(jnp.bfloat16)
    )
    inproj_grad = dense_left(normed_low, triple_grad)
    input_part, gain_a_grad, shift_a_grad = norm_backward(
        dense_right(triple_grad, inproj), normal_a, scale_a, gain_a
    )
    char_grad = (inner_grad + input_part).reshape(word_count, char_slots, feature_width)
    return (
        char_grad,
        (
            gain_a_grad,
            shift_a_grad,
            inproj_grad,
            outproj_grad,
            gain_b_grad,
            shift_b_grad,
            up_grad,
            up_bias_grad,
            down_grad,
            down_bias_grad,
            query_grad,
            proj_grad,
            proj_bias_grad,
        ),
    )


def word_forward(params, word_in, segment_row):
    (
        gain_a,
        shift_a,
        inproj,
        outproj,
        gain_b,
        shift_b,
        up_weight,
        up_bias,
        down_weight,
        down_bias,
    ) = params
    length, feature_width = word_in.shape
    input_rows = word_in.astype(jnp.float32)
    normed, normal_a, scale_a = norm_forward(input_rows, gain_a, shift_a)
    normed_low = normed.astype(jnp.bfloat16)
    triple = dense(normed_low, inproj).astype(jnp.bfloat16).reshape(length, 3, HEADS, HD)
    query_rows = triple[:, 0]
    key_rows = triple[:, 1]
    value_rows = triple[:, 2]
    row_place = lax.broadcasted_iota(jnp.int32, (length, length), 0)
    col_place = lax.broadcasted_iota(jnp.int32, (length, length), 1)
    allowed = (segment_row[:, None] == segment_row[None, :]) & (col_place <= row_place)
    scores = jnp.einsum(
        "ihd,jhd->hij", query_rows, key_rows, preferred_element_type=jnp.float32
    ) * HD ** (-0.5)
    scores = jnp.where(allowed[None], scores, NEG)
    row_max = jnp.max(scores, -1, keepdims=True)
    exponent = jnp.exp(scores - row_max)
    total = jnp.sum(exponent, -1, keepdims=True)
    log_total = row_max + jnp.log(total)
    soft_low = (exponent / total).astype(jnp.bfloat16)
    mixed = (
        jnp.einsum("hij,jhd->ihd", soft_low, value_rows, preferred_element_type=jnp.float32)
        .astype(jnp.bfloat16)
        .reshape(length, feature_width)
    )
    inner_sum = input_rows + dense(mixed, outproj)
    spread, normal_b, scale_b = norm_forward(inner_sum, gain_b, shift_b)
    spread_low = spread.astype(jnp.bfloat16)
    before = dense(spread_low, up_weight) + up_bias.astype(jnp.float32)
    active = gelu_exact(before).astype(jnp.bfloat16)
    result = inner_sum + dense(active, down_weight) + down_bias.astype(jnp.float32)
    kept = (
        normed_low,
        normal_a,
        scale_a,
        query_rows,
        key_rows,
        value_rows,
        allowed,
        log_total,
        mixed,
        normal_b,
        scale_b,
        spread_low,
        before,
        active,
    )
    return (result, kept)


def word_back(params, kept, upstream):
    (
        gain_a,
        shift_a,
        inproj,
        outproj,
        gain_b,
        shift_b,
        up_weight,
        up_bias,
        down_weight,
        down_bias,
    ) = params
    (
        normed_low,
        normal_a,
        scale_a,
        query_rows,
        key_rows,
        value_rows,
        allowed,
        log_total,
        mixed,
        normal_b,
        scale_b,
        spread_low,
        before,
        active,
    ) = kept
    length, feature_width = upstream.shape
    outer_low = upstream.astype(jnp.bfloat16)
    down_grad = dense_left(active, outer_low)
    down_bias_grad = jnp.sum(outer_low.astype(jnp.float32), 0)
    before_low = (dense_right(outer_low, down_weight) * gelu_slope(before)).astype(jnp.bfloat16)
    up_grad = dense_left(spread_low, before_low)
    up_bias_grad = jnp.sum(before_low.astype(jnp.float32), 0)
    inner_part, gain_b_grad, shift_b_grad = norm_backward(
        dense_right(before_low, up_weight), normal_b, scale_b, gain_b
    )
    inner_grad = upstream + inner_part
    inner_low = inner_grad.astype(jnp.bfloat16)
    outproj_grad = dense_left(mixed, inner_low)
    mixed_grad = dense_right(inner_low, outproj).astype(jnp.bfloat16).reshape(length, HEADS, HD)
    scores = jnp.einsum(
        "ihd,jhd->hij", query_rows, key_rows, preferred_element_type=jnp.float32
    ) * HD ** (-0.5)
    soft_weights = jnp.exp(jnp.where(allowed[None], scores, NEG) - log_total)
    soft_grad = jnp.einsum(
        "ihd,jhd->hij", mixed_grad, value_rows, preferred_element_type=jnp.float32
    )
    value_grad = jnp.einsum(
        "hij,ihd->jhd",
        soft_weights.astype(jnp.bfloat16),
        mixed_grad,
        preferred_element_type=jnp.float32,
    )
    score_grad = (
        soft_weights * (soft_grad - jnp.sum(soft_grad * soft_weights, -1, keepdims=True))
    ).astype(jnp.bfloat16)
    query_part = jnp.einsum(
        "hij,jhd->ihd", score_grad, key_rows, preferred_element_type=jnp.float32
    ) * HD ** (-0.5)
    key_part = jnp.einsum(
        "hij,ihd->jhd", score_grad, query_rows, preferred_element_type=jnp.float32
    ) * HD ** (-0.5)
    triple_grad = (
        jnp.stack((query_part, key_part, value_grad), 1)
        .reshape(length, 3 * feature_width)
        .astype(jnp.bfloat16)
    )
    inproj_grad = dense_left(normed_low, triple_grad)
    input_part, gain_a_grad, shift_a_grad = norm_backward(
        dense_right(triple_grad, inproj), normal_a, scale_a, gain_a
    )
    return (
        inner_grad + input_part,
        (
            gain_a_grad,
            shift_a_grad,
            inproj_grad,
            outproj_grad,
            gain_b_grad,
            shift_b_grad,
            up_grad,
            up_bias_grad,
            down_grad,
            down_bias_grad,
        ),
    )


def shards(
    chars,
    char_counts,
    buckets,
    assign,
    segments,
    char_gain,
    char_shift,
    char_inproj,
    char_outproj,
    char_gain_mid,
    char_shift_mid,
    char_up,
    char_up_bias,
    char_down,
    char_down_bias,
    pool_query,
    char_proj,
    char_proj_bias,
    word_gain,
    word_shift,
    word_inproj,
    word_outproj,
    word_gain_mid,
    word_shift_mid,
    word_up,
    word_up_bias,
    word_down,
    word_down_bias,
    out_grad,
):
    owners = lax.axis_size("wide")
    slot_cap = chars.shape[2]
    char_slots = chars.shape[3]
    feature_width = chars.shape[4]
    slot_total = chars.shape[1] * slot_cap
    char_params = (
        lax.all_gather(char_gain, "wide", axis=0, tiled=True),
        lax.all_gather(char_shift, "wide", axis=0, tiled=True),
        lax.all_gather(char_inproj, "wide", axis=0, tiled=True),
        lax.all_gather(char_outproj, "wide", axis=0, tiled=True),
        lax.all_gather(char_gain_mid, "wide", axis=0, tiled=True),
        lax.all_gather(char_shift_mid, "wide", axis=0, tiled=True),
        lax.all_gather(char_up, "wide", axis=0, tiled=True),
        lax.all_gather(char_up_bias, "wide", axis=0, tiled=True),
        lax.all_gather(char_down, "wide", axis=0, tiled=True),
        lax.all_gather(char_down_bias, "wide", axis=0, tiled=True),
        lax.all_gather(pool_query, "wide", axis=0, tiled=True),
        lax.all_gather(char_proj, "wide", axis=0, tiled=True),
        lax.all_gather(char_proj_bias, "wide", axis=0, tiled=True),
    )
    word_params = (
        lax.all_gather(word_gain, "wide", axis=0, tiled=True),
        lax.all_gather(word_shift, "wide", axis=0, tiled=True),
        lax.all_gather(word_inproj, "wide", axis=0, tiled=True),
        lax.all_gather(word_outproj, "wide", axis=0, tiled=True),
        lax.all_gather(word_gain_mid, "wide", axis=0, tiled=True),
        lax.all_gather(word_shift_mid, "wide", axis=0, tiled=True),
        lax.all_gather(word_up, "wide", axis=0, tiled=True),
        lax.all_gather(word_up_bias, "wide", axis=0, tiled=True),
        lax.all_gather(word_down, "wide", axis=0, tiled=True),
        lax.all_gather(word_down_bias, "wide", axis=0, tiled=True),
    )
    block_words = min(slot_total, 256)
    block_count = slot_total // block_words
    char_blocks = chars.reshape(block_count, block_words, char_slots, feature_width)
    count_blocks = char_counts.reshape(block_count, block_words)

    def send_block(block_pair):
        return char_send(char_params, block_pair[0], block_pair[1])

    outgoing = lax.map(send_block, (char_blocks, count_blocks))
    outgoing = outgoing.reshape(owners, slot_cap, outgoing.shape[-1])
    bucket_row = buckets[0, :, 0]
    length = bucket_row.shape[0]
    onehot = bucket_row[:, None] == lax.broadcasted_iota(jnp.int32, (length, owners), 1)
    target = jnp.sum(jnp.where(onehot, assign[None, :], 0), 1)
    rank = jnp.sum(jnp.where(onehot, jnp.cumsum(onehot.astype(jnp.int32), 0) - 1, 0), 1)
    slot_index = target * slot_cap + rank
    arrived = lax.all_to_all(outgoing, "wide", split_axis=0, concat_axis=0, tiled=True)
    word_in = arrived.reshape(owners * slot_cap, arrived.shape[-1])[slot_index]
    result, kept = word_forward(word_params, word_in, segments[0])
    input_grad, word_grads = word_back(word_params, kept, out_grad[0].astype(jnp.float32))
    input_low = input_grad.astype(jnp.bfloat16)
    word_parts = (
        lax.psum_scatter(word_grads[0], "wide", scatter_dimension=0, tiled=True),
        lax.psum_scatter(word_grads[1], "wide", scatter_dimension=0, tiled=True),
        lax.psum_scatter(word_grads[2], "wide", scatter_dimension=0, tiled=True),
        lax.psum_scatter(word_grads[3], "wide", scatter_dimension=0, tiled=True),
        lax.psum_scatter(word_grads[4], "wide", scatter_dimension=0, tiled=True),
        lax.psum_scatter(word_grads[5], "wide", scatter_dimension=0, tiled=True),
        lax.psum_scatter(word_grads[6], "wide", scatter_dimension=0, tiled=True),
        lax.psum_scatter(word_grads[7], "wide", scatter_dimension=0, tiled=True),
        lax.psum_scatter(word_grads[8], "wide", scatter_dimension=0, tiled=True),
        lax.psum_scatter(word_grads[9], "wide", scatter_dimension=0, tiled=True),
    )
    word_total = (
        lax.psum(word_parts[0].astype(jnp.bfloat16), "dp").astype(jnp.float32),
        lax.psum(word_parts[1].astype(jnp.bfloat16), "dp").astype(jnp.float32),
        lax.psum(word_parts[2].astype(jnp.bfloat16), "dp").astype(jnp.float32),
        lax.psum(word_parts[3].astype(jnp.bfloat16), "dp").astype(jnp.float32),
        lax.psum(word_parts[4].astype(jnp.bfloat16), "dp").astype(jnp.float32),
        lax.psum(word_parts[5].astype(jnp.bfloat16), "dp").astype(jnp.float32),
        lax.psum(word_parts[6].astype(jnp.bfloat16), "dp").astype(jnp.float32),
        lax.psum(word_parts[7].astype(jnp.bfloat16), "dp").astype(jnp.float32),
        lax.psum(word_parts[8].astype(jnp.bfloat16), "dp").astype(jnp.float32),
        lax.psum(word_parts[9].astype(jnp.bfloat16), "dp").astype(jnp.float32),
    )
    back_rows = (
        jnp.zeros((owners * slot_cap, input_low.shape[1]), jnp.bfloat16)
        .at[slot_index]
        .set(input_low)
    )
    returned = lax.all_to_all(
        back_rows.reshape(owners, slot_cap, input_low.shape[1]),
        "wide",
        split_axis=0,
        concat_axis=0,
        tiled=True,
    )
    owner_proj = 0.0
    owner_bias = 0.0
    incoming_blocks = returned.reshape(block_count, block_words, returned.shape[-1])
    initial = tuple((jnp.zeros(weight.shape, jnp.float32) for weight in char_params))

    def back_step(running, block_items):
        char_grad, pieces = char_back(char_params, block_items[0], block_items[1], block_items[2])
        return (tuple((total + piece for total, piece in zip(running, pieces))), char_grad)

    totals, char_grads = lax.scan(back_step, initial, (char_blocks, count_blocks, incoming_blocks))
    char_parts = (
        sum_at_owner(totals[0].astype(jnp.bfloat16), "wide", 0),
        *sent_together(
            (
                totals[1].astype(jnp.bfloat16),
                totals[2].astype(jnp.bfloat16),
                totals[3].astype(jnp.bfloat16),
                totals[4].astype(jnp.bfloat16),
                totals[5].astype(jnp.bfloat16),
                totals[6].astype(jnp.bfloat16),
            ),
            "wide",
            0,
            1,
        ),
        *sent_together(
            (totals[7].astype(jnp.bfloat16), totals[8].astype(jnp.bfloat16)), "wide", 0, 1
        ),
        sum_at_owner(totals[9].astype(jnp.bfloat16), "wide", 0),
        *sent_together(
            (totals[10].astype(jnp.bfloat16), (totals[11] + owner_proj).astype(jnp.bfloat16)),
            "wide",
            0,
            1,
        ),
        sum_at_owner((totals[12] + owner_bias).astype(jnp.bfloat16), "wide", 0),
    )
    char_total = (
        lax.psum(char_parts[0].astype(jnp.bfloat16), "dp").astype(jnp.float32),
        lax.psum(char_parts[1].astype(jnp.bfloat16), "dp").astype(jnp.float32),
        lax.psum(char_parts[2].astype(jnp.bfloat16), "dp").astype(jnp.float32),
        lax.psum(char_parts[3].astype(jnp.bfloat16), "dp").astype(jnp.float32),
        lax.psum(char_parts[4].astype(jnp.bfloat16), "dp").astype(jnp.float32),
        lax.psum(char_parts[5].astype(jnp.bfloat16), "dp").astype(jnp.float32),
        lax.psum(char_parts[6].astype(jnp.bfloat16), "dp").astype(jnp.float32),
        lax.psum(char_parts[7].astype(jnp.bfloat16), "dp").astype(jnp.float32),
        lax.psum(char_parts[8].astype(jnp.bfloat16), "dp").astype(jnp.float32),
        lax.psum(char_parts[9].astype(jnp.bfloat16), "dp").astype(jnp.float32),
        lax.psum(char_parts[10].astype(jnp.bfloat16), "dp").astype(jnp.float32),
        lax.psum(char_parts[11].astype(jnp.bfloat16), "dp").astype(jnp.float32),
        lax.psum(char_parts[12].astype(jnp.bfloat16), "dp").astype(jnp.float32),
    )
    return (
        result[None],
        char_grads.reshape(chars.shape),
        char_total[0],
        char_total[1],
        char_total[2],
        char_total[3],
        char_total[4],
        char_total[5],
        char_total[6],
        char_total[7],
        char_total[8],
        char_total[9],
        char_total[10],
        char_total[11],
        char_total[12],
        word_total[0],
        word_total[1],
        word_total[2],
        word_total[3],
        word_total[4],
        word_total[5],
        word_total[6],
        word_total[7],
        word_total[8],
        word_total[9],
    )


def solution(mesh):
    placed = (
        P(("dp", "wide"), None, None, None, None),
        P(("dp", "wide"), None, None),
        P(("dp", "wide"), None, None),
        P(),
        P(("dp", "wide"), None),
        P("wide"),
        P("wide"),
        P("wide", None),
        P("wide", None),
        P("wide"),
        P("wide"),
        P("wide", None),
        P("wide"),
        P("wide", None),
        P("wide"),
        P("wide"),
        P("wide", None),
        P("wide"),
        P("wide"),
        P("wide"),
        P("wide", None),
        P("wide", None),
        P("wide"),
        P("wide"),
        P("wide", None),
        P("wide"),
        P("wide", None),
        P("wide"),
        P(("dp", "wide"), None, None),
    )
    return jax.shard_map(
        shards,
        mesh=mesh,
        in_specs=placed,
        out_specs=(
            P(("dp", "wide"), None, None),
            P(("dp", "wide"), None, None, None, None),
            P("wide"),
            P("wide"),
            P("wide", None),
            P("wide", None),
            P("wide"),
            P("wide"),
            P("wide", None),
            P("wide"),
            P("wide", None),
            P("wide"),
            P("wide"),
            P("wide", None),
            P("wide"),
            P("wide"),
            P("wide"),
            P("wide", None),
            P("wide", None),
            P("wide"),
            P("wide"),
            P("wide", None),
            P("wide"),
            P("wide", None),
            P("wide"),
        ),
        check_vma=False,
    )
```

profile of v0, /device:TPU:0, one launch (start us, length us, event | category | flops | bytes accessed | tf_op | source)
XLA Modules:
  0.0 1263.7 jit_solution(12761789074243394396)
XLA Ops:
  12.7 13.5 %all-gather = bf16[8,1,128]{2,1,0:T(2,128)(2,1)S(1)} all-gather(bf16[1,1,128]{2,1,0:T(2,128)(2,1)} %bitcast.401), channel_id=1, replica_groups=mesh['dp'=4,'wide'=8] {'wide'}, dimensions={0}, use_global_device_ids=true | all-gather | bytes 2304 | tf_op jit(solution)/shard_map/all_gather | solution.py:481
  26.2 14.4 %all_gather.72 = bf16[256,256]{1,0:T(8,128)(2,1)S(1)} all-gather(bf16[32,256]{1,0:T(8,128)(2,1)} %param.41), channel_id=1, replica_groups=mesh['dp'=4,'wide'=8] {'wide'}, dimensions={0}, use_global_device_ids=true | all-gather | bytes 147456 | tf_op jit(solution)/shard_map/all_gather | solution.py:477
  40.7 15.1 %all_gather.80 = bf16[256,512]{1,0:T(8,128)(2,1)S(1)} all-gather(bf16[32,512]{1,0:T(8,128)(2,1)} %param.49), channel_id=1, replica_groups=mesh['dp'=4,'wide'=8] {'wide'}, dimensions={0}, use_global_device_ids=true | all-gather | bytes 294912 | tf_op jit(solution)/shard_map/all_gather | solution.py:485
  55.7 16.4 %all_gather.71 = bf16[256,768]{1,0:T(8,128)(2,1)S(1)} all-gather(bf16[32,768]{1,0:T(8,128)(2,1)} %param.40), channel_id=1, replica_groups=mesh['dp'=4,'wide'=8] {'wide'}, dimensions={0}, use_global_device_ids=true | all-gather | bytes 442368 | tf_op jit(solution)/shard_map/all_gather | solution.py:476
  72.1 16.0 %all_gather.75 = bf16[256,1024]{1,0:T(8,128)(2,1)} all-gather(bf16[32,1024]{1,0:T(8,128)(2,1)} %param.44), channel_id=1, replica_groups=mesh['dp'=4,'wide'=8] {'wide'}, dimensions={0}, use_global_device_ids=true | all-gather | bytes 589824 | tf_op jit(solution)/shard_map/all_gather | solution.py:480
  88.2 15.2 %all_gather.77 = bf16[1024,256]{1,0:T(8,128)(2,1)S(1)} all-gather(bf16[128,256]{1,0:T(8,128)(2,1)} %param.46), channel_id=1, replica_groups=mesh['dp'=4,'wide'=8] {'wide'}, dimensions={0}, use_global_device_ids=true | all-gather | bytes 589824 | tf_op jit(solution)/shard_map/all_gather | solution.py:482
  113.5 15.1 %all-reduce.19 = (bf16[256]{0:T(256)(128)(2,1)}, bf16[256]{0:T(256)(128)(2,1)}, bf16[256]{0:T(256)(128)(2,1)}, bf16[256]{0:T(256)(128)(2,1)}, bf16[256]{0:T(256)...) all-reduce(bf16[256]{0:T(256)(128)(2,1)S(1)} %dynamic-update-slice,, ...), channel_id=1, replica_groups=mesh['dp'=4,'wide'=8] {'wide'}, use_global_device_ids=true, to_apply=%add | all-reduce | flops 4608 | bytes 18432
  128.7 217.4 %while.47 = (s32[]{:T(128)}, bf16[2,256,512]{2,1,0:T(8,128)(2,1)}, s32[2,256]{1,0:T(2,128)}, bf16[2,256,16,256]{3,2,1,0:T(8,128)(2,1)}, bf16[256]{0:T(256)(128)(...) while((s32[]{:T(128)}, bf16[2,256,512]{2,1,0:T(8,128)(2,1)}, ...), condition=%wide.region_11.12_spmd, body=%wide.region_0.11_spmd.sunk | while | flops 6638267392 | bytes 143615456 | solution.py:508
  152.0 18.6 %reshape.878 = bf16[256,16,3,4,64]{4,3,2,1,0:T(4,128)(2,1)} reshape(bf16[4096,768]{1,0:T(8,128)(2,1)} %convolution_convert_fusion.12) | data formatting | bytes 12582912 | tf_op jit(solution)/shard_map/while/body/eval_jaxpr/reshape | solution.py:118
  222.3 10.4 multiply_reduce_fusion.37
  260.4 18.6 %reshape.878 = bf16[256,16,3,4,64]{4,3,2,1,0:T(4,128)(2,1)} reshape(bf16[4096,768]{1,0:T(8,128)(2,1)} %convolution_convert_fusion.12) | data formatting | bytes 12582912 | tf_op jit(solution)/shard_map/while/body/eval_jaxpr/reshape | solution.py:118
  330.7 10.4 multiply_reduce_fusion.37
  356.1 12.2 all-gather.1
  369.2 18.3 %all_gather.85 = bf16[512,512]{1,0:T(8,128)(2,1)} all-gather(bf16[64,512]{1,0:T(8,128)(2,1)} %param.54), channel_id=1, replica_groups=mesh['dp'=4,'wide'=8] {'wide'}, dimensions={0}, use_global_device_ids=true | all-gather | bytes 589824 | tf_op jit(solution)/shard_map/all_gather | solution.py:492
  436.7 12.1 all-to-all-done.1
  448.8 568.5 %while.48 = (s32[]{:T(128)}, f32[256]{0:T(256)}, f32[256]{0:T(256)}, f32[256,768]{1,0:T(8,128)}, f32[256,256]{1,0:T(8,128)}, /*index=5*/f32[256]{0:T(256)}, f32[...) while((s32[]{:T(128)}, f32[256]{0:T(256)}, ...), condition=%wide.region_54.55_spmd.clone, body=%wide.region_28.54_spmd.clone.sunk | while | flops 19864637440 | bytes 748739776 | solution.py:566
  474.9 18.7 %reshape.880 = bf16[256,16,3,4,64]{4,3,2,1,0:T(4,128)(2,1)} reshape(bf16[4096,768]{1,0:T(8,128)(2,1)} %convolution_convert_fusion.14) | data formatting | bytes 12582912 | tf_op jit(solution)/shard_map/while/body/eval_jaxpr/reshape | solution.py:118
  509.3 10.3 fusion.302
  564.8 13.4 %convert_reduce_fusion.14 = (f32[1024]{0:T(1024)S(1)}, bf16[4096,1024]{1,0:T(8,128)(2,1)S(1)}) fusion(f32[4096,1024]{1,0:T(8,128)} %get-tuple-element.1009, f32[1024]{0:T(1024)S(1)} %copy-done.69, bf16[4096,256]{1,0:T(8,128)(2,1)S(1)} %fusion.307, bf16[1024,256]{1,0:T(8,128)(2,1)} %get-tuple-element.1181), kind=kOutput, calls=%fused_computation.68.clone.1 | convolution fusion | flops 2202008576 | bytes 27795456 | tf_op jit(solution)/shard_map/while/body/eval_jaxpr/dot_general | solution.py:51
  614.4 13.0 %multiply_reduce_fusion.44 = (f32[256,4,16]{2,1,0:T(4,128)}, f32[256,4,16,16]{2,3,1,0:T(8,128)}) fusion(f32[256,4,16,16]{2,3,1,0:T(8,128)} %copy-done.17, f32[256,4,16]{2,1,0:T(4,128)S(1)} %copy-done.31, bf16[256,16,1,4,64]{4,3,2,1,0:T(4,128)(2,1)} %get-tuple-element.996, bf16[256,16,4,64]{3,2,1,0:T(4,128)(2,1)} %reshape.882), kind=kOutput, calls=%fused_computation.73.clone.1 | convolution fusion | flops 34324480 | bytes 6422528 | tf_op jit(solution)/shard_map/while/body/eval_jaxpr/wihd,wjhd->whij/dot_general | solution.py:235
  674.9 20.1 %copy.300 = bf16[256,16,3,4,64]{4,3,2,1,0:T(4,128)(2,1)} copy(bf16[256,16,3,4,64]{0,4,3,2,1:T(8,128)(2,1)} %maximum_convert_fusion.2) | data formatting | bytes 12582912 | tf_op jit(solution)/shard_map/while/body/eval_jaxpr/convert_element_type | solution.py:256
  695.0 18.6 %convert_element_type.855 = bf16[4096,768]{1,0:T(8,128)(2,1)} reshape(bf16[256,16,3,4,64]{4,3,2,1,0:T(4,128)(2,1)} %copy.300) | data formatting | bytes 12582912 | tf_op jit(solution)/shard_map/while/body/eval_jaxpr/convert_element_type | solution.py:256
  756.4 18.6 %reshape.880 = bf16[256,16,3,4,64]{4,3,2,1,0:T(4,128)(2,1)} reshape(bf16[4096,768]{1,0:T(8,128)(2,1)} %convolution_convert_fusion.14) | data formatting | bytes 12582912 | tf_op jit(solution)/shard_map/while/body/eval_jaxpr/reshape | solution.py:118
  790.6 10.2 fusion.302
  846.9 13.3 %convert_reduce_fusion.14 = (f32[1024]{0:T(1024)S(1)}, bf16[4096,1024]{1,0:T(8,128)(2,1)S(1)}) fusion(f32[4096,1024]{1,0:T(8,128)} %get-tuple-element.1009, f32[1024]{0:T(1024)S(1)} %copy-done.69, bf16[4096,256]{1,0:T(8,128)(2,1)S(1)} %fusion.307, bf16[1024,256]{1,0:T(8,128)(2,1)} %get-tuple-element.1181), kind=kOutput, calls=%fused_computation.68.clone.1 | convolution fusion | flops 2202008576 | bytes 27795456 | tf_op jit(solution)/shard_map/while/body/eval_jaxpr/dot_general | solution.py:51
  896.3 13.0 %multiply_reduce_fusion.44 = (f32[256,4,16]{2,1,0:T(4,128)}, f32[256,4,16,16]{2,3,1,0:T(8,128)}) fusion(f32[256,4,16,16]{2,3,1,0:T(8,128)} %copy-done.17, f32[256,4,16]{2,1,0:T(4,128)S(1)} %copy-done.31, bf16[256,16,1,4,64]{4,3,2,1,0:T(4,128)(2,1)} %get-tuple-element.996, bf16[256,16,4,64]{3,2,1,0:T(4,128)(2,1)} %reshape.882), kind=kOutput, calls=%fused_computation.73.clone.1 | convolution fusion | flops 34324480 | bytes 6422528 | tf_op jit(solution)/shard_map/while/body/eval_jaxpr/wihd,wjhd->whij/dot_general | solution.py:235
  956.8 20.1 %copy.300 = bf16[256,16,3,4,64]{4,3,2,1,0:T(4,128)(2,1)} copy(bf16[256,16,3,4,64]{0,4,3,2,1:T(8,128)(2,1)} %maximum_convert_fusion.2) | data formatting | bytes 12582912 | tf_op jit(solution)/shard_map/while/body/eval_jaxpr/convert_element_type | solution.py:256
  976.9 18.6 %convert_element_type.855 = bf16[4096,768]{1,0:T(8,128)(2,1)} reshape(bf16[256,16,3,4,64]{4,3,2,1,0:T(4,128)(2,1)} %copy.300) | data formatting | bytes 12582912 | tf_op jit(solution)/shard_map/while/body/eval_jaxpr/convert_element_type | solution.py:256
  1067.7 11.0 all-to-all-done.4
  1083.6 41.8 %all-reduce.18 = (bf16[512]{0:T(512)(128)(2,1)}, bf16[512]{0:T(512)(128)(2,1)}, bf16[512]{0:T(512)(128)(2,1)}, bf16[512]{0:T(512)(128)(2,1)}, bf16[2048]{0:T(1024)(128)(2,1)}, /*index=5*/bf16[512]{0:T(512)(128)(2,1)}) all-reduce(f32[512]{0:T(512)} %get-tuple-element.449, ...), channel_id=2, replica_groups=mesh['dp'=4,'wide'=8] {'wide'}, use_global_device_ids=true, to_apply=%region_75.76.clone | all-reduce | flops 4608 | bytes 27648
  1154.3 33.7 %all-reduce.25.cloned.1.call-done = (bf16[32]{0:T(256)(128)(2,1)}, bf16[32]{0:T(256)(128)(2,1)}, bf16[32,768]{1,0:T(8,128)(2,1)}, bf16[32,256]{1,0:T(8,128)(2,1)...) async-done(((bf16[32]{0:T(256)(128)(2,1)}, ...) | async-done | bytes 100240 | tf_op jit(solution)/shard_map/psum | solution.py:595
  1208.3 38.8 %all-reduce.27.cloned.1.call-done = (bf16[128,256]{0,1:T(8,128)(2,1)}, bf16[32,1024]{1,0:T(8,128)(2,1)}, bf16[64,1536]{1,0:T(8,128)(2,1)}, bf16[64,512]{1,0:T(8,...) async-done(((bf16[128,256]{0,1:T(8,128)(2,1)}, bf16[32,1024]{1,0:T(8,128)(2,1)}, bf16[64,1536]{1,0:T(8,128)(2,1)}, bf16[64,512]{1,0:T(8,128)(2,1)}, ...) | async-done | bytes 917520 | tf_op jit(solution)/shard_map/psum | solution.py:603
  (817 shorter events, 717.7 us)
Async XLA Ops:
  7.2 381.8 %all-gather.6.cloned.1.call-start = ((), (), s32[]{:S(2)}) async-start(), calls=%async_computation.12 | async-start | bytes 1769472 | tf_op jit(solution)/shard_map/all_gather | solution.py:491
  7.9 388.7 %all-gather.8.cloned.1.call-start = ((), (), s32[]{:S(2)}) async-start(), calls=%async_computation.13 | async-start | bytes 2359296 | tf_op jit(solution)/shard_map/all_gather | solution.py:495
  346.1 46.2 %copy-start.28 = (bf16[1024,256]{1,0:T(8,128)(2,1)}, bf16[1024,256]{1,0:T(8,128)(2,1)S(1)}, u32[]{:S(2)}) copy-start(bf16[1024,256]{1,0:T(8,128)(2,1)S(1)} %get-tuple-element.1250) | copy-start | bytes 1572868
  346.1 41.4 %all-to-all-start = ((bf16[8,64,512]{2,1,0:T(8,128)(2,1)}), bf16[8,64,512]{2,1,0:T(8,128)(2,1)S(1)}, u32[]{:S(2)}, u32[]{:S(2)}) async-start(bf16[8,64,512]{2,1,0:T(8,128)(2,1)} %bitcast.392), calls=%async_computation | async-start | bytes 1048576 | tf_op jit(solution)/shard_map/all_to_all | solution.py:516
  349.6 51.2 %all-gather.10.cloned.1.call-start = ((), (), s32[]{:S(2)}) async-start(), calls=%async_computation.14 | async-start | bytes 2359296 | tf_op jit(solution)/shard_map/all_gather | solution.py:497
  350.3 793.3 %reduce-scatter.7.cloned.1.call-start = ((), (), s32[]{:S(2)}) async-start(), calls=%async_computation.16 | async-start | bytes 1179648 | tf_op jit(solution)/shard_map/reduce_scatter | solution.py:525
  396.4 23.3 %copy-start.32 = (f32[256,512]{1,0:T(8,128)}, f32[256,512]{1,0:T(8,128)S(1)}, u32[]{:S(2)}) copy-start(f32[256,512]{1,0:T(8,128)S(1)} %get-tuple-element.641) | copy-start | bytes 1572868
  409.4 736.5 %reduce-scatter.5.cloned.1.call-start = ((), (), s32[]{:S(2)}) async-start(), calls=%async_computation.15 | async-start | bytes 3538944 | tf_op jit(solution)/shard_map/reduce_scatter | solution.py:524
  419.5 728.2 %reduce-scatter.9.cloned.1.call-start = ((), (), s32[]{:S(2)}) async-start(), calls=%async_computation.17 | async-start | bytes 4718592 | tf_op jit(solution)/shard_map/reduce_scatter | solution.py:528
  429.3 19.5 %all-to-all-start.1 = ((bf16[8,64,512]{2,1,0:T(8,128)(2,1)}), bf16[8,64,512]{2,1,0:T(8,128)(2,1)S(1)}, u32[]{:S(2)}, u32[]{:S(2)}) async-start(bf16[8,64,512]{2,1,0:T(8,128)(2,1)} %bitcast.38), calls=%async_computation.1 | async-start | bytes 1048576 | tf_op jit(solution)/shard_map/all_to_all | solution.py:550
  432.8 716.6 %reduce-scatter.11.cloned.1.call-start = ((), (), s32[]{:S(2)}) async-start(), calls=%async_computation.18 | async-start | bytes 4718592 | tf_op jit(solution)/shard_map/reduce_scatter | solution.py:530
  449.2 18.7 %copy-start.19 = (bf16[256,768]{1,0:T(8,128)(2,1)}, bf16[256,768]{1,0:T(8,128)(2,1)S(1)}, u32[]{:S(2)}) copy-start(bf16[256,768]{1,0:T(8,128)(2,1)S(1)} %get-tuple-element.1174) | copy-start | bytes 1179652 | tf_op jit(solution)/shard_map/while
  695.0 18.6 %copy-start.16 = (bf16[1,256,16,256]{3,2,1,0:T(8,128)(2,1)S(1)}, bf16[1,256,16,256]{3,2,1,0:T(8,128)(2,1)}, u32[]{:S(2)}) copy-start(bf16[1,256,16,256]{3,2,1,0:T(8,128)(2,1)} %add_convert_fusion.22) | copy-start | bytes 6291460 | tf_op jit(solution)/shard_map/while
  730.8 18.6 %copy-start.19 = (bf16[256,768]{1,0:T(8,128)(2,1)}, bf16[256,768]{1,0:T(8,128)(2,1)S(1)}, u32[]{:S(2)}) copy-start(bf16[256,768]{1,0:T(8,128)(2,1)S(1)} %get-tuple-element.1174) | copy-start | bytes 1179652 | tf_op jit(solution)/shard_map/while
  1017.3 27.7 %copy-start.68 = (f32[1024]{0:T(1024)}, f32[1024]{0:T(1024)S(1)}, u32[]{:S(2)}) copy-start(f32[1024]{0:T(1024)S(1)} %get-tuple-element.286) | copy-start | bytes 12292
  1017.3 45.7 %copy-start.88 = (f32[256]{0:T(256)S(1)}, f32[256]{0:T(256)}, u32[]{:S(2)}) copy-start(f32[256]{0:T(256)} %get-tuple-element.280) | copy-start | bytes 3076
  1017.3 45.7 %copy-start.85 = (f32[256]{0:T(256)S(1)}, f32[256]{0:T(256)}, u32[]{:S(2)}) copy-start(f32[256]{0:T(256)} %get-tuple-element.283) | copy-start | bytes 3076
  1017.3 45.7 %copy-start.82 = (f32[256]{0:T(256)S(1)}, f32[256]{0:T(256)}, u32[]{:S(2)}) copy-start(f32[256]{0:T(256)} %get-tuple-element.284) | copy-start | bytes 3076
  1017.4 46.5 %copy-start.36 = (f32[256,256]{1,0:T(8,128)S(1)}, f32[256,256]{1,0:T(8,128)}, u32[]{:S(2)}) copy-start(f32[256,256]{1,0:T(8,128)} %get-tuple-element.282) | copy-start | bytes 786436
  1018.8 8.7 all-to-all-start.2
  1027.5 36.3 %copy-start.91 = (bf16[8,1,32]{2,1,0:T(2,128)(2,1)}, bf16[8,1,32]{2,1,0:T(2,128)(2,1)S(1)}, u32[]{:S(2)}) copy-start(bf16[8,1,32]{2,1,0:T(2,128)(2,1)S(1)} %all-to-all-done.2) | copy-start | bytes 1540
  1027.5 8.7 all-to-all-start.5
  1032.4 31.4 %copy-start.27 = (f32[256,768]{1,0:T(8,128)S(1)}, f32[256,768]{1,0:T(8,128)}, u32[]{:S(2)}) copy-start(f32[256,768]{1,0:T(8,128)} %get-tuple-element.281) | copy-start | bytes 2359300
  1036.2 27.7 %copy-start.92 = (bf16[8,1,32]{2,1,0:T(2,128)(2,1)}, bf16[8,1,32]{2,1,0:T(2,128)(2,1)S(1)}, u32[]{:S(2)}) copy-start(bf16[8,1,32]{2,1,0:T(2,128)(2,1)S(1)} %all-to-all-done.5) | copy-start | bytes 1540
  1036.2 8.7 all-to-all-start.7
  1045.0 14.5 %all-to-all-start.6 = ((bf16[8,32,513]{2,1,0:T(8,128)(2,1)}), bf16[8,32,513]{2,1,0:T(8,128)(2,1)S(1)}, u32[]{:S(2)}, u32[]{:S(2)}) async-start(bf16[8,32,513]{2,1,0:T(8,128)(2,1)} %pad_maximum_fusion.2), calls=%async_computation.6 | async-start | bytes 655360 | tf_op jit(solution)/shard_map/all_to_all | solution.py:25
  1059.5 19.2 %all-to-all-start.4 = ((bf16[8,128,257]{1,2,0:T(8,128)(2,1)}), bf16[8,128,257]{1,2,0:T(8,128)(2,1)S(1)}, u32[]{:S(2)}, u32[]{:S(2)}) async-start(bf16[8,128,257]{1,2,0:T(8,128)(2,1)} %copy.217), calls=%async_computation.4 | async-start | bytes 1081344 | tf_op jit(solution)/shard_map/all_to_all | solution.py:25
  1067.7 83.5 %copy-start.33 = (f32[256,512]{1,0:T(8,128)S(1)}, f32[256,512]{1,0:T(8,128)}, u32[]{:S(2)}) copy-start(f32[256,512]{1,0:T(8,128)} %copy-done.32) | copy-start | bytes 1572868
  1067.7 83.5 %copy-start.49 = (bf16[256,2048]{1,0:T(8,128)(2,1)S(1)}, bf16[256,2048]{1,0:T(8,128)(2,1)}, u32[]{:S(2)}) copy-start(bf16[256,2048]{1,0:T(8,128)(2,1)} %get-tuple-element.642) | copy-start | bytes 3145732
  1078.7 62.0 %all-to-all-start.3 = ((bf16[8,32,2051]{2,1,0:T(8,128)(2,1)}), bf16[8,32,2051]{2,1,0:T(8,128)(2,1)S(1)}, u32[]{:S(2)}, u32[]{:S(2)}) async-start(bf16[8,32,2051]{2,1,0:T(8,128)(2,1)} %concatenate.38), calls=%async_computation.3 | async-start | bytes 2228224 | tf_op jit(solution)/shard_map/all_to_all | solution.py:25
  1082.2 105.9 %all-reduce.25.cloned.1.call-start = ((), (), s32[]{:S(2)}) async-start(), calls=%async_computation.19 | async-start | bytes 210944 | tf_op jit(solution)/shard_map/psum | solution.py:595
  1143.0 104.1 %all-reduce.27.cloned.1.call-start = ((), (), s32[]{:S(2)}) async-start(), calls=%async_computation.20 | async-start | bytes 1835008 | tf_op jit(solution)/shard_map/psum | solution.py:603
  (167 other events, 851.7 us)
Sparse Core Ops, SparseCore 0:
  9.7 28.8 all-gather.5
  40.2 31.4 all-gather.7
  352.0 35.4 all-gather.9
  409.5 32.0 reduce-scatter.6
  443.8 38.7 reduce-scatter.4
  484.7 49.1 reduce-scatter.8
  536.1 48.1 reduce-scatter.10
  1143.1 44.9 all-reduce.24
  1193.5 53.5 all-reduce.26
where the time goes:
time: 1280 us; the launch traced here: 1260 us
  local copies, waits for them, and re-layouts  377 us (29%)
  matrix products  305 us (24%)
  other arithmetic  232 us (18%)
  blocking collectives  178 us (14%)
  waiting for transfers between devices  116 us (9%)
  starting transfers between devices  28 us (2%)
  between operations  17.5 us (1%)
    dot_general x20, matrix products, dense(): return jnp.dot(left, right, preferred_element_type=jnp.float32)  91.6 us
    convert_element_type x4, local copies, waits for them, and re-layouts, char_back(): triple_grad = jnp.stack((query_part, key_part, value_grad), 2).reshape(wo...  77.3 us
    reshape x4, local copies, waits for them, and re-layouts, char_core(): triple = dense(normed_low, inproj).astype(jnp.bfloat16).reshape(word_coun...  74.5 us
    unnamed x2, blocking collectives  56.9 us
    dot_general x14, matrix products, dense_right(): lax.dot_general(left, right, (((1,), (1,)), ((), ())), preferred_element_...  53.4 us
    dot_general x14, matrix products, dense_left(): lax.dot_general(left, right, (((0,), (0,)), ((), ())), preferred_element_...  39.2 us
    psum x1, waiting for transfers between devices, shards(): lax.psum(char_parts[8].astype(jnp.bfloat16), 'dp').astype(jnp.float32)  38.8 us
    psum x1, waiting for transfers between devices, shards(): lax.psum(char_parts[0].astype(jnp.bfloat16), 'dp').astype(jnp.float32)  33.7 us
  transfers between devices with their start and end apart: 17, of which 8 were waited for; matrix products, arithmetic and copies ran while one was open for 69% of the time, Pallas kernels for 0%

commit v1 on v0

--- a/solution.py
+++ b/solution.py
@@ -1,18 +1,16 @@
+import functools
+
 import jax
 import jax.numpy as jnp
 from jax import lax
+from jax.experimental import pallas as pl
+from jax.experimental.pallas import tpu as pltpu
 from jax.sharding import PartitionSpec as P
 
 HEADS = 8
 HD = 64
 CHEADS = 4
 CHD = 64
-
-
-EPS = 1e-05
-NEG = -1e30
-ROOT_HALF = 0.7071067811865476
-INV_ROOT_TWO_PI = 0.3989422804014327
 
 
 def split_up(shard, dim, size):
@@ -91,193 +89,237 @@
     return (inv_scale * inner, jnp.sum(upstream * normal, 0), jnp.sum(upstream, 0))
 
 
-def char_core(params, char_block, count_block):
-    (
-        gain_a,
-        shift_a,
-        inproj,
-        outproj,
-        gain_b,
-        shift_b,
-        up_weight,
-        up_bias,
-        down_weight,
-        down_bias,
-        query_vec,
-        proj_weight,
-        proj_bias,
-    ) = params
-    word_count, char_slots, feature_width = char_block.shape
-    flat_rows = char_block.astype(jnp.float32).reshape(word_count * char_slots, feature_width)
-    valid_mask = lax.broadcasted_iota(jnp.int32, (word_count, char_slots), 1) < count_block[:, None]
-    normed, normal_a, scale_a = norm_forward(flat_rows, gain_a, shift_a)
-    normed_low = normed.astype(jnp.bfloat16)
-    triple = (
-        dense(normed_low, inproj)
-        .astype(jnp.bfloat16)
-        .reshape(word_count, char_slots, 3, CHEADS, CHD)
-    )
-    query_rows = triple[:, :, 0]
-    key_rows = triple[:, :, 1]
-    value_rows = triple[:, :, 2]
-    scores = jnp.einsum(
-        "wihd,wjhd->whij", query_rows, key_rows, preferred_element_type=jnp.float32
-    ) * CHD ** (-0.5)
-    scores = jnp.where(valid_mask[:, None, None, :], scores, NEG)
-    soft_weights = softmax_rows(scores)
-    mixed = jnp.einsum(
-        "whij,wjhd->wihd",
-        soft_weights.astype(jnp.bfloat16),
-        value_rows,
-        preferred_element_type=jnp.float32,
-    )
-    mixed = mixed.astype(jnp.bfloat16).reshape(word_count * char_slots, feature_width)
-    inner_sum = flat_rows + dense(mixed, outproj)
-    spread, normal_b, scale_b = norm_forward(inner_sum, gain_b, shift_b)
-    spread_low = spread.astype(jnp.bfloat16)
-    before = dense(spread_low, up_weight) + up_bias.astype(jnp.float32)
-    active = gelu_exact(before).astype(jnp.bfloat16)
-    outer_sum = inner_sum + dense(active, down_weight) + down_bias.astype(jnp.float32)
-    char_grid = outer_sum.reshape(word_count, char_slots, feature_width)
-    attend = jnp.sum(char_grid * query_vec.astype(jnp.float32), -1) * feature_width ** (-0.5)
-    pool_weights = softmax_rows(jnp.where(valid_mask, attend, NEG))
-    pooled = jnp.sum(pool_weights[:, :, None] * char_grid, 1).astype(jnp.bfloat16)
-    return (
-        normal_a,
-        scale_a,
-        normed_low,
-        query_rows,
-        key_rows,
-        value_rows,
-        soft_weights,
-        mixed,
-        normal_b,
-        scale_b,
-        spread_low,
-        before,
-        active,
-        char_grid,
-        pool_weights,
-        pooled,
-    )
-
-
-def char_send(params, char_block, count_block):
-    pooled = char_core(params, char_block, count_block)[15]
-    return (dense(pooled, params[11]) + params[12].astype(jnp.float32)).astype(jnp.bfloat16)
-
-
-def char_back(params, char_block, count_block, incoming):
-    (
-        gain_a,
-        shift_a,
-        inproj,
-        outproj,
-        gain_b,
-        shift_b,
-        up_weight,
-        up_bias,
-        down_weight,
-        down_bias,
-        query_vec,
-        proj_weight,
-        proj_bias,
-    ) = params
-    (
-        normal_a,
-        scale_a,
-        normed_low,
-        query_rows,
-        key_rows,
-        value_rows,
-        soft_weights,
-        mixed,
-        normal_b,
-        scale_b,
-        spread_low,
-        before,
-        active,
-        char_grid,
-        pool_weights,
-        pooled,
-    ) = char_core(params, char_block, count_block)
-    word_count, char_slots, feature_width = char_block.shape
-    pool_grad = rounded(dense_right(incoming, proj_weight))
-    proj_grad = dense_left(pooled, incoming)
-    proj_bias_grad = jnp.sum(incoming.astype(jnp.float32), 0)
-    pool_factor = feature_width ** (-0.5)
-    weight_grad = jnp.sum(char_grid * pool_grad[:, None, :], -1)
-    attend_grad = pool_weights * (
-        weight_grad - jnp.sum(pool_weights * weight_grad, -1, keepdims=True)
-    )
-    grid_grad = pool_weights[:, :, None] * pool_grad[:, None, :] + attend_grad[:, :, None] * (
-        query_vec.astype(jnp.float32) * pool_factor
-    )
-    query_grad = jnp.sum(attend_grad[:, :, None] * char_grid, (0, 1)) * pool_factor
-    outer_grad = grid_grad.reshape(word_count * char_slots, feature_width)
-    outer_low = outer_grad.astype(jnp.bfloat16)
-    down_grad = dense_left(active, outer_low)
-    down_bias_grad = jnp.sum(outer_low.astype(jnp.float32), 0)
-    before_low = (dense_right(outer_low, down_weight) * gelu_slope(before)).astype(jnp.bfloat16)
-    up_grad = dense_left(spread_low, before_low)
-    up_bias_grad = jnp.sum(before_low.astype(jnp.float32), 0)
-    inner_part, gain_b_grad, shift_b_grad = norm_backward(
-        dense_right(before_low, up_weight), normal_b, scale_b, gain_b
-    )
-    inner_grad = outer_grad + inner_part
-    inner_low = inner_grad.astype(jnp.bfloat16)
-    outproj_grad = dense_left(mixed, inner_low)
-    mixed_grad = (
-        dense_right(inner_low, outproj)
-        .astype(jnp.bfloat16)
-        .reshape(word_count, char_slots, CHEADS, CHD)
-    )
-    soft_grad = jnp.einsum(
-        "wihd,wjhd->whij", mixed_grad, value_rows, preferred_element_type=jnp.float32
-    )
-    value_grad = jnp.einsum(
-        "whij,wihd->wjhd",
-        soft_weights.astype(jnp.bfloat16),
-        mixed_grad,
-        preferred_element_type=jnp.float32,
-    )
-    score_grad = (
-        soft_weights * (soft_grad - jnp.sum(soft_grad * soft_weights, -1, keepdims=True))
-    ).astype(jnp.bfloat16)
-    query_part = jnp.einsum(
-        "whij,wjhd->wihd", score_grad, key_rows, preferred_element_type=jnp.float32
-    ) * CHD ** (-0.5)
-    key_part = jnp.einsum(
-        "whij,wihd->wjhd", score_grad, query_rows, preferred_element_type=jnp.float32
-    ) * CHD ** (-0.5)
-    triple_grad = (
-        jnp.stack((query_part, key_part, value_grad), 2)
-        .reshape(word_count * char_slots, 3 * feature_width)
-        .astype(jnp.bfloat16)
-    )
-    inproj_grad = dense_left(normed_low, triple_grad)
-    input_part, gain_a_grad, shift_a_grad = norm_backward(
-        dense_right(triple_grad, inproj), normal_a, scale_a, gain_a
-    )
-    char_grad = (inner_grad + input_part).reshape(word_count, char_slots, feature_width)
-    return (
-        char_grad,
-        (
-            gain_a_grad,
-            shift_a_grad,
-            inproj_grad,
-            outproj_grad,
-            gain_b_grad,
-            shift_b_grad,
-            up_grad,
-            up_bias_grad,
-            down_grad,
-            down_bias_grad,
-            query_grad,
-            proj_grad,
-            proj_bias_grad,
-        ),
-    )
+EPS = 1e-05
+NEG = -1e30
+ROOT_HALF = 0.7071067811865476
+INV_ROOT_TWO_PI = 0.3989422804014327
+CHD = 64
+GROUP = 128
+F32 = jnp.float32
+BF = jnp.bfloat16
+
+
+def nn(a, b):
+    return lax.dot_general(a, b, (((1,), (0,)), ((), ())), preferred_element_type=F32)
+
+
+def nt(a, b):
+    return lax.dot_general(a, b, (((1,), (1,)), ((), ())), preferred_element_type=F32)
+
+
+def tn(a, b):
+    return lax.dot_general(a, b, (((0,), (0,)), ((), ())), preferred_element_type=F32)
+
+
+def normal_of(x):
+    c = x - jnp.mean(x, -1, keepdims=True)
+    r = lax.rsqrt(jnp.mean(c * c, -1, keepdims=True) + EPS)
+    return c * r, r
+
+
+def norm_back(d, n, r, g):
+    dg = d * g
+    return r * (dg - jnp.mean(dg, -1, keepdims=True) - n * jnp.mean(dg * n, -1, keepdims=True))
+
+
+def two_heads(t):
+    left = lax.broadcasted_iota(jnp.int32, t.shape, 1) < CHD
+    zero = jnp.zeros_like(t)
+    return jnp.concatenate([jnp.where(left, t, zero), jnp.where(left, zero, t)], 0)
+
+
+def pool_weights(h2, query, counts, chars_per):
+    rows = h2.shape[0]
+    words = rows // chars_per
+    e = jnp.sum(h2 * query, -1, keepdims=True) * (h2.shape[1] ** -0.5)
+    e = e.reshape(words, chars_per, 1)
+    place = lax.broadcasted_iota(jnp.int32, (words, chars_per, 1), 1)
+    e = jnp.where(place < counts.reshape(words, 1, 1), e, NEG)
+    top = jnp.max(e, 1, keepdims=True)
+    ex = jnp.exp(e - top)
+    return ex / jnp.sum(ex, 1, keepdims=True)
+
+
+def char_forward(chars_per, c_ref, vb_ref, cnt_ref, win, wout, wup, wdn, wpj, ga, sa, gb, sb, ub, db, qv, pb,
+                 x_ref, pooled_ref, qkv_ref, p_ref, o_ref, h1_ref, h2_ref, m_ref, s_ref):
+    rows, width = c_ref.shape
+    x = c_ref[...].astype(F32)
+    n, _ = normal_of(x)
+    a = (n * ga[...] + sa[...]).astype(BF)
+    qkv = nn(a, win[...])
+    qkv_ref[:, :width] = (qkv[:, :width] * CHD ** -0.5).astype(BF)
+    qkv_ref[:, width:] = qkv[:, width:].astype(BF)
+    ri = lax.broadcasted_iota(jnp.int32, (GROUP, GROUP), 0) // chars_per
+    ci = lax.broadcasted_iota(jnp.int32, (GROUP, GROUP), 1) // chars_per
+    same = ri == ci
+    for g in range(rows // GROUP):
+        at = slice(g * GROUP, (g + 1) * GROUP)
+        bias = jnp.where(same, jnp.broadcast_to(vb_ref[g:g + 1, :], (GROUP, GROUP)), NEG)
+        for p in range(width // GROUP):
+            lanes = slice(p * GROUP, (p + 1) * GROUP)
+            q = qkv_ref[at, p * GROUP:(p + 1) * GROUP]
+            k = qkv_ref[at, width + p * GROUP:width + (p + 1) * GROUP]
+            v = qkv_ref[at, 2 * width + p * GROUP:2 * width + (p + 1) * GROUP]
+            s = nt(q, two_heads(k))
+            parts = []
+            for h in range(2):
+                sh = s[:, h * GROUP:(h + 1) * GROUP] + bias
+                ex = jnp.exp(sh - jnp.max(sh, -1, keepdims=True))
+                parts.append((ex * (1.0 / jnp.sum(ex, -1, keepdims=True))).astype(BF))
+            soft = jnp.concatenate(parts, 1)
+            p_ref[at, p * 2 * GROUP:(p + 1) * 2 * GROUP] = soft
+            o_ref[at, lanes] = nn(soft, two_heads(v)).astype(BF)
+    chunk = min(rows, 256)
+    for t in range(rows // chunk):
+        at = slice(t * chunk, (t + 1) * chunk)
+        h1 = c_ref[at, :].astype(F32) + nn(o_ref[at, :], wout[...])
+        h1_ref[at, :] = h1
+        n, _ = normal_of(h1)
+        u = (n * gb[...] + sb[...]).astype(BF)
+        z = nn(u, wup[...]) + ub[...]
+        cdf = 0.5 * (1.0 + lax.erf(z * ROOT_HALF))
+        m = (z * cdf).astype(BF)
+        m_ref[at, :] = m
+        s_ref[at, :] = (cdf + z * jnp.exp(-0.5 * z * z) * INV_ROOT_TWO_PI).astype(BF)
+        h2 = h1 + (nn(m, wdn[...]) + db[...])
+        h2_ref[at, :] = h2
+        words = chunk // chars_per
+        wat = slice(t * words, (t + 1) * words)
+        om = pool_weights(h2, qv[...], cnt_ref[wat, :], chars_per)
+        pooled = jnp.sum(om * h2.reshape(words, chars_per, width), 1).astype(BF)
+        pooled_ref[wat, :] = pooled
+    x_ref[...] = (nn(pooled_ref[...], wpj[...]) + pb[...]).astype(BF)
+
+
+def char_backward(chars_per, gx_ref, c_ref, cnt_ref, qkv_ref, p_ref, o_ref, h1_ref, h2_ref, m_ref, s_ref,
+                  pooled_all, gx_all, win, wout, wup, wdn, wpj, ga, sa, gb, sb, qv,
+                  gc_ref, dga, dsa, dwin, dwout, dgb, dsb, dwup, dub, dwdn, ddb, dqv, dwpj, dpb, gq_ref, gh1_ref, gm_ref, gz_ref):
+    rows, width = c_ref.shape
+    words = rows // chars_per
+    accs = (dga, dsa, dwin, dwout, dgb, dsb, dwup, dub, dwdn, ddb, dqv)
+
+    @pl.when(pl.program_id(0) == 0)
+    def _():
+        for acc in accs:
+            acc[...] = jnp.zeros_like(acc)
+        dwpj[...] = tn(pooled_all[...], gx_all[...])
+        dpb[...] = jnp.sum(gx_all[...].astype(F32), 0, keepdims=True)
+
+    gp = nt(gx_ref[...], wpj[...]).astype(BF).astype(F32)
+    factor = width ** -0.5
+    chunk = min(rows, 256)
+    cw = chunk // chars_per
+    for t in range(rows // chunk):
+        at = slice(t * chunk, (t + 1) * chunk)
+        wat = slice(t * cw, (t + 1) * cw)
+        h2 = h2_ref[at, :]
+        om = pool_weights(h2, qv[...], cnt_ref[wat, :], chars_per)
+        gpb = jnp.broadcast_to(gp[wat, :].reshape(cw, 1, width), (cw, chars_per, width)).reshape(chunk, width)
+        w = jnp.sum(h2 * gpb, -1, keepdims=True).reshape(cw, chars_per, 1)
+        de = om * (w - jnp.sum(om * w, 1, keepdims=True))
+        de = de.reshape(chunk, 1) * factor
+        gh2 = om.reshape(chunk, 1) * gpb + de * qv[...]
+        dqv[...] += jnp.sum(de * h2, 0, keepdims=True)
+        gy = gh2.astype(BF)
+        ddb[...] += jnp.sum(gy.astype(F32), 0, keepdims=True)
+        gm_ref[at, :] = gy
+        gz = (nt(gy, wdn[...]) * s_ref[at, :].astype(F32)).astype(BF)
+        gz_ref[at, :] = gz
+        dub[...] += jnp.sum(gz.astype(F32), 0, keepdims=True)
+        du = nt(gz, wup[...])
+        n, r = normal_of(h1_ref[at, :])
+        dgb[...] += jnp.sum(du * n, 0, keepdims=True)
+        dsb[...] += jnp.sum(du, 0, keepdims=True)
+        gh1_ref[at, :] = gh2 + norm_back(du, n, r, gb[...])
+        o_u = (n * gb[...] + sb[...]).astype(BF)
+        dwup[...] += tn(o_u, gz)
+    dwdn[...] += tn(gm_ref[...], m_ref[...])
+    gh1 = gh1_ref[...]
+    g1 = gh1.astype(BF)
+    dwout[...] += tn(o_ref[...], g1)
+    gm_ref[...] = nt(g1, wout[...]).astype(BF)
+    for g in range(rows // GROUP):
+        at = slice(g * GROUP, (g + 1) * GROUP)
+        for p in range(width // GROUP):
+            q = qkv_ref[at, p * GROUP:(p + 1) * GROUP]
+            k = qkv_ref[at, width + p * GROUP:width + (p + 1) * GROUP]
+            v = qkv_ref[at, 2 * width + p * GROUP:2 * width + (p + 1) * GROUP]
+            soft = p_ref[at, p * 2 * GROUP:(p + 1) * 2 * GROUP]
+            gm = gm_ref[at, p * GROUP:(p + 1) * GROUP]
+            dp = nt(gm, two_heads(v))
+            parts = []
+            for h in range(2):
+                ph = soft[:, h * GROUP:(h + 1) * GROUP].astype(F32)
+                dh = dp[:, h * GROUP:(h + 1) * GROUP]
+                parts.append((ph * (dh - jnp.sum(dh * ph, -1, keepdims=True))).astype(BF))
+            gs = jnp.concatenate(parts, 1)
+            left = lax.broadcasted_iota(jnp.int32, (GROUP, GROUP), 1) < CHD
+            gv = tn(soft, gm)
+            gk = tn(gs, q)
+            gq = nn(gs, two_heads(k)) * CHD ** -0.5
+            gq_ref[at, p * GROUP:(p + 1) * GROUP] = gq.astype(BF)
+            gq_ref[at, width + p * GROUP:width + (p + 1) * GROUP] = jnp.where(left, gk[:GROUP], gk[GROUP:]).astype(BF)
+            gq_ref[at, 2 * width + p * GROUP:2 * width + (p + 1) * GROUP] = jnp.where(left, gv[:GROUP], gv[GROUP:]).astype(BF)
+    for t in range(rows // chunk):
+        at = slice(t * chunk, (t + 1) * chunk)
+        n, r = normal_of(c_ref[at, :].astype(F32))
+        a = (n * ga[...] + sa[...]).astype(BF)
+        gqkv = gq_ref[at, :]
+        dwin[...] += tn(a, gqkv)
+        da = nt(gqkv, win[...])
+        dga[...] += jnp.sum(da * n, 0, keepdims=True)
+        dsa[...] += jnp.sum(da, 0, keepdims=True)
+        gc_ref[at, :] = gh1_ref[at, :] + norm_back(da, n, r, ga[...])
+
+
+def full(shape):
+    return pl.BlockSpec(shape, lambda i: (0,) * len(shape))
+
+
+def by_row(rows, width):
+    return pl.BlockSpec((rows, width), lambda i: (i, 0))
+
+
+def run_forward(chars, vb, cnt, weights, chars_per, rows):
+    total, width = chars.shape
+    win, wout, wup, wdn, wpj, ga, sa, gb, sb, ub, db, qv, pb = weights
+    words, cw = total // chars_per, rows // chars_per
+    ff, out = wup.shape[1], wpj.shape[1]
+    outs = [((words, out), BF, cw), ((words, width), BF, cw), ((total, 3 * width), BF, rows), ((total, 2 * width), BF, rows),
+            ((total, width), BF, rows), ((total, width), F32, rows), ((total, width), F32, rows),
+            ((total, ff), BF, rows), ((total, ff), BF, rows)]
+    return pl.pallas_call(
+        functools.partial(char_forward, chars_per),
+        grid=(total // rows,),
+        in_specs=[by_row(rows, width), by_row(rows // GROUP, GROUP), by_row(cw, 1)] + [full(w.shape) for w in weights],
+        out_specs=[by_row(b, s[1]) for s, _, b in outs],
+        out_shape=[jax.ShapeDtypeStruct(s, d) for s, d, _ in outs],
+        compiler_params=pltpu.CompilerParams(vmem_limit_bytes=60 << 20),
+    )(chars, vb, cnt, *weights)
+
+
+def run_backward(gx, chars, cnt, saved, weights, chars_per, rows):
+    total, width = chars.shape
+    win, wout, wup, wdn, wpj, ga, sa, gb, sb, ub, db, qv, pb = weights
+    pooled, qkv, soft, mixed, h1, h2, m, s = saved
+    words, cw = total // chars_per, rows // chars_per
+    ff, out = wup.shape[1], wpj.shape[1]
+    ws = (win, wout, wup, wdn, wpj, ga, sa, gb, sb, qv)
+    row = [((total, width), F32)]
+    accs = [(1, width), (1, width), (width, 3 * width), (width, width), (1, width), (1, width), (width, ff), (1, ff),
+            (width, ff), (1, width), (1, width), (width, out), (1, out)]
+    return pl.pallas_call(
+        functools.partial(char_backward, chars_per),
+        grid=(total // rows,),
+        in_specs=[by_row(cw, out), by_row(rows, width), by_row(cw, 1), by_row(rows, 3 * width), by_row(rows, 2 * width),
+                  by_row(rows, width), by_row(rows, width), by_row(rows, width), by_row(rows, ff), by_row(rows, ff),
+                  full(pooled.shape), full(gx.shape)] + [full(w.shape) for w in ws],
+        out_specs=[by_row(rows, width)] + [full(a) for a in accs],
+        out_shape=[jax.ShapeDtypeStruct((total, width), F32)] + [jax.ShapeDtypeStruct(a, F32) for a in accs],
+        scratch_shapes=[pltpu.VMEM((rows, 3 * width), BF), pltpu.VMEM((rows, width), F32), pltpu.VMEM((rows, width), BF),
+                        pltpu.VMEM((rows, ff), BF)],
+        compiler_params=pltpu.CompilerParams(vmem_limit_bytes=60 << 20),
+    )(gx, chars, cnt, qkv, soft, mixed, h1, h2, m, s, pooled, gx, *ws)
 
 
 def word_forward(params, word_in, segment_row):
@@ -497,15 +539,20 @@
         lax.all_gather(word_down, "wide", axis=0, tiled=True),
         lax.all_gather(word_down_bias, "wide", axis=0, tiled=True),
     )
-    block_words = min(slot_total, 256)
-    block_count = slot_total // block_words
-    char_blocks = chars.reshape(block_count, block_words, char_slots, feature_width)
-    count_blocks = char_counts.reshape(block_count, block_words)
-
-    def send_block(block_pair):
-        return char_send(char_params, block_pair[0], block_pair[1])
-
-    outgoing = lax.map(send_block, (char_blocks, count_blocks))
+    rows = chars.reshape(-1, feature_width)
+    counts = char_counts.reshape(slot_total, 1)
+    places = lax.broadcasted_iota(jnp.int32, (slot_total, char_slots), 1)
+    key_bias = jnp.where(places < counts, 0.0, NEG).reshape(-1, GROUP)
+    as_row = lambda v: v.astype(F32)[None]
+    weights = (
+        char_params[2],
+        char_params[3],
+        char_params[6],
+        char_params[8],
+        char_params[11],
+        *(as_row(char_params[i]) for i in (0, 1, 4, 5, 7, 9, 10, 12)),
+    )
+    outgoing, *saved = run_forward(rows, key_bias, counts, weights, char_slots, 1024)
     outgoing = outgoing.reshape(owners, slot_cap, outgoing.shape[-1])
     bucket_row = buckets[0, :, 0]
     length = bucket_row.shape[0]
@@ -554,16 +601,10 @@
         concat_axis=0,
         tiled=True,
     )
-    owner_proj = 0.0
-    owner_bias = 0.0
-    incoming_blocks = returned.reshape(block_count, block_words, returned.shape[-1])
-    initial = tuple((jnp.zeros(weight.shape, jnp.float32) for weight in char_params))
-
-    def back_step(running, block_items):
-        char_grad, pieces = char_back(char_params, block_items[0], block_items[1], block_items[2])
-        return (tuple((total + piece for total, piece in zip(running, pieces))), char_grad)
-
-    totals, char_grads = lax.scan(back_step, initial, (char_blocks, count_blocks, incoming_blocks))
+    incoming = returned.reshape(slot_total, returned.shape[-1])
+    char_grads, *pieces = run_backward(incoming, rows, counts, saved, weights, char_slots, 1024)
+    dga, dsa, dwin, dwout, dgb, dsb, dwup, dub, dwdn, ddb, dqv, dwpj, dpb = pieces
+    totals = (dga[0], dsa[0], dwin, dwout, dgb[0], dsb[0], dwup, dub[0], dwdn.T, ddb[0], dqv[0], dwpj, dpb[0])
     char_parts = (
         sum_at_owner(totals[0].astype(jnp.bfloat16), "wide", 0),
         *sent_together(
@@ -584,12 +625,12 @@
         ),
         sum_at_owner(totals[9].astype(jnp.bfloat16), "wide", 0),
         *sent_together(
-            (totals[10].astype(jnp.bfloat16), (totals[11] + owner_proj).astype(jnp.bfloat16)),
+            (totals[10].astype(jnp.bfloat16), (totals[11]).astype(jnp.bfloat16)),
             "wide",
             0,
             1,
         ),
-        sum_at_owner((totals[12] + owner_bias).astype(jnp.bfloat16), "wide", 0),
+        sum_at_owner((totals[12]).astype(jnp.bfloat16), "wide", 0),
     )
     char_total = (
         lax.psum(char_parts[0].astype(jnp.bfloat16), "dp").astype(jnp.float32),

time: 1280 us -> 645 us (0.50)
  local copies, waits for them, and re-layouts: 377 us -> 45.1 us
  matrix products: 305 us -> 36.3 us
  other arithmetic: 232 us -> 59 us
  Pallas kernels: 0 us -> 142 us
  blocking collectives: 178 us -> 201 us
    pallas_call x0 -> x2, Pallas kernels: none -> 142 us  [the longest x1 88.4 us: run_backward(): pl.pallas_call(functools.partial(char_backward, chars_per), grid=(total /...]
    dot_general x16 -> x0, matrix products: 115 us -> none  [the longest x2 26 us: char_back(): jnp.einsum('wihd,wjhd->whij', mixed_grad, value_rows, preferred_element_t...]
    reshape x11 -> x1, local copies, waits for them, and re-layouts: 107 us -> 1.59 us  [shards(): counts = char_counts.reshape(slot_total, 1)]
    convert_element_type x10 -> x7, local copies, waits for them, and re-layouts: 107 us -> 4.24 us  [the longest x1 0.87 us: shards(): totals[4].astype(jnp.bfloat16)]
    dot_general x20 -> x4, matrix products: 91.6 us -> 9.84 us  [dense(): return jnp.dot(left, right, preferred_element_type=jnp.float32)]
    convert_element_type x37 -> x3, other arithmetic: 65 us -> 1.8 us  [the longest x1 1.09 us: shards(): totals[11].astype(jnp.bfloat16)]
    dot_general x8 -> x0, local copies, waits for them, and re-layouts: 54.7 us -> none  [the longest x2 15.9 us: char_back(): jnp.einsum('whij,wjhd->wihd', score_grad, key_rows, preferred_element_typ...]
    dot_general x14 -> x4, matrix products: 53.4 us -> 11.4 us  [dense_right(): lax.dot_general(left, right, (((1,), (1,)), ((), ())), preferred_element_...]
  transfers between devices with their start and end apart: 17 -> 16, of which waited for: 8 -> 7; matrix products, arithmetic and copies ran while one was open for 69% -> 19% of each run, Pallas kernels for 0% -> 22%
where the time goes in v1:
time: 645 us; the launch traced here: 635 us
  blocking collectives  201 us (31%)
  Pallas kernels  142 us (22%)
  waiting for transfers between devices  109 us (17%)
  other arithmetic  59 us (9%)
  local copies, waits for them, and re-layouts  45.1 us (7%)
  matrix products  36.3 us (6%)
  starting transfers between devices  25 us (4%)
  between operations  17.5 us (3%)
    pallas_call x1, Pallas kernels, run_backward(): pl.pallas_call(functools.partial(char_backward, chars_per), grid=(total /...  88.4 us
    unnamed x2, blocking collectives  61.2 us
    pallas_call x1, Pallas kernels, run_forward(): pl.pallas_call(functools.partial(char_forward, chars_per), grid=(total //...  53.6 us
    psum x1, waiting for transfers between devices, shards(): lax.psum(char_parts[8].astype(jnp.bfloat16), 'dp').astype(jnp.float32)  39 us
    psum x1, waiting for transfers between devices, shards(): lax.psum(char_parts[0].astype(jnp.bfloat16), 'dp').astype(jnp.float32)  34.5 us
    all_to_all x6, waiting for transfers between devices, sum_at_owner(): lax.all_to_all(parts, axis, split_axis=0, concat_axis=0, tiled=True)  32.9 us
    unnamed x91, local copies, waits for them, and re-layouts  24.1 us
    all_to_all x6, starting transfers between devices, sum_at_owner(): lax.all_to_all(parts, axis, split_axis=0, concat_axis=0, tiled=True)  20.7 us
  transfers between devices with their start and end apart: 16, of which 7 were waited for; matrix products, arithmetic and copies ran while one was open for 19% of the time, Pallas kernels for 22%

profile of v1, /device:TPU:0, one launch (start us, length us, event | category | flops | bytes accessed | tf_op | source)
XLA Modules:
  0.0 634.5 jit_solution(13139270912026349309)
XLA Ops:
  23.9 19.4 %all-reduce.19 = (bf16[256]{0:T(256)(128)(2,1)S(1)}, bf16[256]{0:T(256)(128)(2,1)S(1)}, bf16[256]{0:T(256)(128)(2,1)S(1)}, bf16[256]{0:T(256)(128)(2,1)S(1)}, bf...) all-reduce(bf16[256]{0:T(256)(128)(2,1)S(1)} %dynamic-update-slice,, ...), channel_id=1, replica_groups=mesh['dp'=4,'wide'=8] {'wide'}, use_global_device_ids=true, to_apply=%add | all-reduce | flops 4608 | bytes 18432
  47.5 8.7 %all-gather = bf16[8,1,128]{2,1,0:T(2,128)(2,1)S(1)} all-gather(bf16[1,1,128]{2,1,0:T(2,128)(2,1)} %bitcast.157), channel_id=1, replica_groups=mesh['dp'=4,'wide'=8] {'wide'}, dimensions={0}, use_global_device_ids=true | all-gather | bytes 2304 | tf_op jit(solution)/shard_map/all_gather | solution.py:523
  56.3 15.6 %all_gather.70.wout = bf16[256,256]{1,0:T(8,128)(2,1)} all-gather(bf16[32,256]{1,0:T(8,128)(2,1)} %param.37), channel_id=1, replica_groups=mesh['dp'=4,'wide'=8] {'wide'}, dimensions={0}, use_global_device_ids=true | all-gather | bytes 147456 | tf_op jit(solution)/shard_map/all_gather | solution.py:519
  71.9 15.5 %all_gather.73.wpj = bf16[256,512]{1,0:T(8,128)(2,1)} all-gather(bf16[32,512]{1,0:T(8,128)(2,1)} %param.45), channel_id=1, replica_groups=mesh['dp'=4,'wide'=8] {'wide'}, dimensions={0}, use_global_device_ids=true | all-gather | bytes 294912 | tf_op jit(solution)/shard_map/all_gather | solution.py:527
  87.4 15.7 %all_gather.69.win = bf16[256,768]{1,0:T(8,128)(2,1)} all-gather(bf16[32,768]{1,0:T(8,128)(2,1)} %param.36), channel_id=1, replica_groups=mesh['dp'=4,'wide'=8] {'wide'}, dimensions={0}, use_global_device_ids=true | all-gather | bytes 442368 | tf_op jit(solution)/shard_map/all_gather | solution.py:518
  104.3 15.8 %all_gather.71.wup = bf16[256,1024]{1,0:T(8,128)(2,1)} all-gather(bf16[32,1024]{1,0:T(8,128)(2,1)S(1)} %copy-done.13), channel_id=1, replica_groups=mesh['dp'=4,'wide'=8] {'wide'}, dimensions={0}, use_global_device_ids=true | all-gather | bytes 589824 | tf_op jit(solution)/shard_map/all_gather | solution.py:522
  120.1 15.8 %all_gather.72.wdn = bf16[1024,256]{1,0:T(8,128)(2,1)} all-gather(bf16[128,256]{1,0:T(8,128)(2,1)S(1)} %copy-done.14), channel_id=1, replica_groups=mesh['dp'=4,'wide'=8] {'wide'}, dimensions={0}, use_global_device_ids=true | all-gather | bytes 589824 | tf_op jit(solution)/shard_map/all_gather | solution.py:524
  135.9 53.6 %shard_map.468 = (bf16[512,512]{1,0:T(8,128)(2,1)}, bf16[512,256]{1,0:T(8,128)(2,1)}, bf16[8192,768]{1,0:T(8,128)(2,1)}, bf16[8192,512]{1,0:T(8,128)(2,1)}, bf16...) custom-call(bf16[8192,256]{1,0:T(8,128)(2,1)} %bitcast.115, ...), custom_call_target="tpu_custom_call" | custom-call | tf_op jit(solution)/shard_map/pallas_call | solution.py:291
  189.4 3.5 all-to-all-start
  194.9 14.3 %all-gather.1 = bf16[8,1,256]{2,1,0:T(2,128)(2,1)S(1)} all-gather(bf16[1,1,256]{2,1,0:T(2,128)(2,1)S(1)} %reshape.433), channel_id=1, replica_groups=mesh['dp'=4,'wide'=8] {'wide'}, dimensions={0}, use_global_device_ids=true | all-gather | bytes 4608 | tf_op jit(solution)/shard_map/all_gather | solution.py:538
  209.4 18.1 %all_gather.85 = bf16[512,512]{1,0:T(8,128)(2,1)S(1)} all-gather(bf16[64,512]{1,0:T(8,128)(2,1)S(1)} %copy-done.15), channel_id=1, replica_groups=mesh['dp'=4,'wide'=8] {'wide'}, dimensions={0}, use_global_device_ids=true | all-gather | bytes 589824 | tf_op jit(solution)/shard_map/all_gather | solution.py:534
  236.5 4.3 multiply_convert_fusion.1
  240.8 4.4 convert_reduce_fusion
  267.5 3.5 fusion.29
  273.4 20.6 %all_to_all.43 = bf16[8,64,512]{2,1,0:T(8,128)(2,1)} all-to-all(bf16[8,64,512]{2,1,0:T(8,128)(2,1)S(1)} %bitcast.129), channel_id=1, replica_groups=mesh['dp'=4,'wide'=8] {'wide'}, dimensions={0} | all-to-all | bytes 1048576 | tf_op jit(solution)/shard_map/all_to_all | solution.py:597
  294.0 88.4 %shard_map.469 = (f32[8192,256]{1,0:T(8,128)}, f32[1,256]{1,0:T(1,128)}, f32[1,256]{1,0:T(1,128)}, f32[256,768]{1,0:T(8,128)}, f32[256,256]{1,0:T(8,128)}, /*ind...) custom-call(bf16[512,512]{1,0:T(8,128)(2,1)} %bitcast.118, ...), custom_call_target="tpu_custom_call" | custom-call | tf_op jit(solution)/shard_map/pallas_call | solution.py:311
  383.7 3.3 all-to-all-start.2
  389.1 3.6 all-to-all-done.2
  392.7 3.6 all-to-all-start.5
  398.9 2.9 all-to-all-done.5
  401.9 3.3 all-to-all-start.7
  406.1 4.7 all-to-all-done.7
  410.8 3.4 all-to-all-start.6
  416.6 13.6 %all-to-all-done.6 = bf16[8,32,513]{2,1,0:T(8,128)(2,1)S(1)} async-done(((bf16[8,32,513]{2,1,0:T(8,128)(2,1)}), bf16[8,32,513]{2,1,0:T(8,128)(2,1)S(1)}, u32[]{:S(2)}, u32[]{:S(2)}) %all-to-all-start.6) | async-done | bytes 262688 | tf_op jit(solution)/shard_map/all_to_all | solution.py:23
  430.2 3.5 all-to-all-start.4
  438.3 3.1 concatenate.25
  441.4 8.0 %all-to-all-done.4 = bf16[8,128,257]{1,2,0:T(8,128)(2,1)S(1)} async-done(((bf16[8,128,257]{1,2,0:T(8,128)(2,1)}), bf16[8,128,257]{1,2,0:T(8,128)(2,1)S(1)}, u32[]{:S(2)}, u32[]{:S(2)}) %all-to-all-start.4) | async-done | bytes 526368 | tf_op jit(solution)/shard_map/all_to_all | solution.py:23
  449.4 3.6 all-to-all-start.3
  454.3 41.8 %all-reduce.18 = (bf16[512]{0:T(512)(128)(2,1)}, bf16[512]{0:T(512)(128)(2,1)}, bf16[512]{0:T(512)(128)(2,1)}, bf16[512]{0:T(512)(128)(2,1)}, bf16[2048]{0:T(1024)(128)(2,1)}, /*index=5*/bf16[512]{0:T(512)(128)(2,1)}) all-reduce(f32[512]{0:T(512)} %get-tuple-element.98, ...), channel_id=2, replica_groups=mesh['dp'=4,'wide'=8] {'wide'}, use_global_device_ids=true, to_apply=%region_36.37.clone | all-reduce | flops 4608 | bytes 27648
  521.9 3.1 fusion.8
  525.1 34.5 %all-reduce.25.cloned.1.call-done = (bf16[32]{0:T(256)(128)(2,1)}, bf16[32]{0:T(256)(128)(2,1)}, bf16[32,768]{1,0:T(8,128)(2,1)}, bf16[32,256]{1,0:T(8,128)(2,1)...) async-done(((bf16[32]{0:T(256)(128)(2,1)}, ...) | async-done | bytes 100240 | tf_op jit(solution)/shard_map/psum | solution.py:636
  579.6 39.0 %all-reduce.27.cloned.1.call-done = (bf16[128,256]{0,1:T(8,128)(2,1)}, bf16[32,1024]{1,0:T(8,128)(2,1)}, bf16[64,1536]{1,0:T(8,128)(2,1)}, bf16[64,512]{1,0:T(8,...) async-done(((bf16[128,256]{0,1:T(8,128)(2,1)}, bf16[32,1024]{1,0:T(8,128)(2,1)}, bf16[64,1536]{1,0:T(8,128)(2,1)}, bf16[64,512]{1,0:T(8,128)(2,1)}, ...) | async-done | bytes 917520 | tf_op jit(solution)/shard_map/psum | solution.py:644
  (245 shorter events, 124.9 us)
Async XLA Ops:
  7.2 97.1 %copy-start.13 = (bf16[32,1024]{1,0:T(8,128)(2,1)S(1)}, bf16[32,1024]{1,0:T(8,128)(2,1)}, u32[]{:S(2)}) copy-start(bf16[32,1024]{1,0:T(8,128)(2,1)} %param.40) | copy-start | bytes 196612
  7.2 112.8 %copy-start.14 = (bf16[128,256]{1,0:T(8,128)(2,1)S(1)}, bf16[128,256]{1,0:T(8,128)(2,1)}, u32[]{:S(2)}) copy-start(bf16[128,256]{1,0:T(8,128)(2,1)} %param.42) | copy-start | bytes 196612
  7.2 221.8 %all-gather.6.cloned.1.call-start = ((), (), s32[]{:S(2)}) async-start(), calls=%async_computation.12 | async-start | bytes 1769472 | tf_op jit(solution)/shard_map/all_gather | solution.py:533
  8.0 228.5 %all-gather.8.cloned.1.call-start = ((), (), s32[]{:S(2)}) async-start(), calls=%async_computation.13 | async-start | bytes 2359296 | tf_op jit(solution)/shard_map/all_gather | solution.py:537
  135.8 58.1 %copy-start.19 = (s32[1,256,1]{1,2,0:T(1,128)S(1)}, s32[1,256,1]{1,2,0:T(1,128)}, u32[]{:S(2)}) copy-start(s32[1,256,1]{1,2,0:T(1,128)} %param.31) | copy-start | bytes 3076
  135.8 58.9 %copy-start.23 = (s32[8]{0:T(128)S(1)}, s32[8]{0:T(128)}, u32[]{:S(2)}) copy-start(s32[8]{0:T(128)} %param.32) | copy-start | bytes 100
  135.8 59.0 %copy-start.28 = (bf16[256]{0:T(256)(128)(2,1)S(1)}, bf16[256]{0:T(256)(128)(2,1)}, u32[]{:S(2)}) copy-start(bf16[256]{0:T(256)(128)(2,1)} %param.54) | copy-start | bytes 1540
  135.9 73.4 %copy-start.20 = (s32[1,256]{1,0:T(1,128)S(1)}, s32[1,256]{1,0:T(1,128)}, u32[]{:S(2)}) copy-start(s32[1,256]{1,0:T(1,128)} %param.33) | copy-start | bytes 3076
  135.9 73.5 %copy-start.15 = (bf16[64,512]{1,0:T(8,128)(2,1)S(1)}, bf16[64,512]{1,0:T(8,128)(2,1)}, u32[]{:S(2)}) copy-start(bf16[64,512]{1,0:T(8,128)(2,1)} %param.50) | copy-start | bytes 196612
  189.4 38.1 %all-to-all-start = ((bf16[8,64,512]{2,1,0:T(8,128)(2,1)}), bf16[8,64,512]{2,1,0:T(8,128)(2,1)S(1)}, u32[]{:S(2)}, u32[]{:S(2)}) async-start(bf16[8,64,512]{2,1,0:T(8,128)(2,1)} %bitcast.136), calls=%async_computation | async-start | bytes 1048576 | tf_op jit(solution)/shard_map/all_to_all | solution.py:563
  192.9 47.9 %all-gather.10.cloned.1.call-start = ((), (), s32[]{:S(2)}) async-start(), calls=%async_computation.14 | async-start | bytes 2359296 | tf_op jit(solution)/shard_map/all_gather | solution.py:539
  193.7 320.7 %reduce-scatter.7.cloned.1.call-start = ((), (), s32[]{:S(2)}) async-start(), calls=%async_computation.16 | async-start | bytes 1179648 | tf_op jit(solution)/shard_map/reduce_scatter | solution.py:572
  227.5 8.1 %copy-start = (bf16[512,512]{1,0:T(8,128)(2,1)}, bf16[512,512]{1,0:T(8,128)(2,1)S(1)}, u32[]{:S(2)}) copy-start(bf16[512,512]{1,0:T(8,128)(2,1)S(1)} %all_gather.85) | copy-start | bytes 1572868
  248.9 267.8 %reduce-scatter.5.cloned.1.call-start = ((), (), s32[]{:S(2)}) async-start(), calls=%async_computation.15 | async-start | bytes 3538944 | tf_op jit(solution)/shard_map/reduce_scatter | solution.py:571
  259.5 258.8 %reduce-scatter.9.cloned.1.call-start = ((), (), s32[]{:S(2)}) async-start(), calls=%async_computation.17 | async-start | bytes 4718592 | tf_op jit(solution)/shard_map/reduce_scatter | solution.py:575
  263.5 256.6 %reduce-scatter.11.cloned.1.call-start = ((), (), s32[]{:S(2)}) async-start(), calls=%async_computation.18 | async-start | bytes 4718592 | tf_op jit(solution)/shard_map/reduce_scatter | solution.py:577
  382.4 31.9 %copy-start.21 = (f32[1,1024]{1,0:T(1,128)S(1)}, f32[1,1024]{1,0:T(1,128)}, u32[]{:S(2)}) copy-start(f32[1,1024]{1,0:T(1,128)} %get-tuple-element.65) | copy-start | bytes 12292
  383.7 8.9 %all-to-all-start.2 = ((bf16[8,1,32]{2,1,0:T(2,128)(2,1)}), bf16[8,1,32]{2,1,0:T(2,128)(2,1)S(1)}, u32[]{:S(2)}, u32[]{:S(2)}) async-start(bf16[8,1,32]{2,1,0:T(2,128)(2,1)} %convert_element_type.444), calls=%async_computation.2 | async-start | bytes 8192 | tf_op jit(solution)/shard_map/all_to_all | solution.py:23
  392.7 9.2 %all-to-all-start.5 = ((bf16[8,1,32]{2,1,0:T(2,128)(2,1)}), bf16[8,1,32]{2,1,0:T(2,128)(2,1)S(1)}, u32[]{:S(2)}, u32[]{:S(2)}) async-start(bf16[8,1,32]{2,1,0:T(2,128)(2,1)} %convert_element_type.448), calls=%async_computation.5 | async-start | bytes 8192 | tf_op jit(solution)/shard_map/all_to_all | solution.py:23
  401.9 12.4 %copy-start.17 = (bf16[8,1,32]{2,1,0:T(2,128)(2,1)}, bf16[8,1,32]{2,1,0:T(2,128)(2,1)S(1)}, u32[]{:S(2)}) copy-start(bf16[8,1,32]{2,1,0:T(2,128)(2,1)S(1)} %all-to-all-done.5) | copy-start | bytes 1540
  401.9 8.9 %all-to-all-start.7 = ((bf16[8,1,64]{2,1,0:T(2,128)(2,1)}), bf16[8,1,64]{2,1,0:T(2,128)(2,1)S(1)}, u32[]{:S(2)}, u32[]{:S(2)}) async-start(bf16[8,1,64]{2,1,0:T(2,128)(2,1)} %convert_element_type.450), calls=%async_computation.7 | async-start | bytes 8192 | tf_op jit(solution)/shard_map/all_to_all | solution.py:23
  406.1 27.7 %copy-start.27 = (f32[1,256]{1,0:T(1,128)S(1)}, f32[1,256]{1,0:T(1,128)}, u32[]{:S(2)}) copy-start(f32[1,256]{1,0:T(1,128)} %get-tuple-element.63) | copy-start | bytes 3076
  406.1 28.0 %copy-start.26 = (f32[1,256]{1,0:T(1,128)S(1)}, f32[1,256]{1,0:T(1,128)}, u32[]{:S(2)}) copy-start(f32[1,256]{1,0:T(1,128)} %get-tuple-element.62) | copy-start | bytes 3076
  410.8 19.4 %all-to-all-start.6 = ((bf16[8,32,513]{2,1,0:T(8,128)(2,1)}), bf16[8,32,513]{2,1,0:T(8,128)(2,1)S(1)}, u32[]{:S(2)}, u32[]{:S(2)}) async-start(bf16[8,32,513]{2,1,0:T(8,128)(2,1)} %pad_maximum_fusion.2), calls=%async_computation.6 | async-start | bytes 655360 | tf_op jit(solution)/shard_map/all_to_all | solution.py:23
  414.3 20.7 %copy-start.25 = (f32[1,256]{1,0:T(1,128)S(1)}, f32[1,256]{1,0:T(1,128)}, u32[]{:S(2)}) copy-start(f32[1,256]{1,0:T(1,128)} %get-tuple-element.59) | copy-start | bytes 3076
  414.3 21.6 %copy-start.12 = (f32[256,256]{1,0:T(8,128)S(1)}, f32[256,256]{1,0:T(8,128)}, u32[]{:S(2)}) copy-start(f32[256,256]{1,0:T(8,128)} %get-tuple-element.61) | copy-start | bytes 786436
  430.2 19.2 %all-to-all-start.4 = ((bf16[8,128,257]{1,2,0:T(8,128)(2,1)}), bf16[8,128,257]{1,2,0:T(8,128)(2,1)S(1)}, u32[]{:S(2)}, u32[]{:S(2)}) async-start(bf16[8,128,257]{1,2,0:T(8,128)(2,1)} %pad_maximum_fusion.1), calls=%async_computation.4 | async-start | bytes 1081344 | tf_op jit(solution)/shard_map/all_to_all | solution.py:23
  449.4 62.0 %all-to-all-start.3 = ((bf16[8,32,2051]{2,1,0:T(8,128)(2,1)}), bf16[8,32,2051]{2,1,0:T(8,128)(2,1)S(1)}, u32[]{:S(2)}, u32[]{:S(2)}) async-start(bf16[8,32,2051]{2,1,0:T(8,128)(2,1)} %concatenate.25), calls=%async_computation.3 | async-start | bytes 2228224 | tf_op jit(solution)/shard_map/all_to_all | solution.py:23
  453.0 106.6 %all-reduce.25.cloned.1.call-start = ((), (), s32[]{:S(2)}) async-start(), calls=%async_computation.19 | async-start | bytes 210944 | tf_op jit(solution)/shard_map/psum | solution.py:636
  511.6 10.4 %copy-start.22 = (bf16[512]{0:T(512)(128)(2,1)S(1)}, bf16[512]{0:T(512)(128)(2,1)}, u32[]{:S(2)}) copy-start(bf16[512]{0:T(512)(128)(2,1)} %get-tuple-element.126) | copy-start | bytes 3076
  513.7 104.9 %all-reduce.27.cloned.1.call-start = ((), (), s32[]{:S(2)}) async-start(), calls=%async_computation.20 | async-start | bytes 1835008 | tf_op jit(solution)/shard_map/psum | solution.py:644
  618.5 8.1 %copy-start.11 = (bf16[256,512]{1,0:T(8,128)(2,1)S(1)}, bf16[256,512]{1,0:T(8,128)(2,1)}, u32[]{:S(2)}) copy-start(bf16[256,512]{1,0:T(8,128)(2,1)} %get-tuple-element.149) | copy-start | bytes 786436
  (13 other events, 29.1 us)
Sparse Core Ops, SparseCore 0:
  9.7 28.5 all-gather.5
  39.9 29.1 all-gather.7
  195.4 35.5 all-gather.9
  249.0 33.2 reduce-scatter.6
  284.4 38.6 reduce-scatter.4
  325.3 49.3 reduce-scatter.8
  376.9 53.0 reduce-scatter.10
  513.8 45.6 all-reduce.24
  564.9 53.6 all-reduce.26

commit v2 on v1

v2 whole, which is shorter than its diff:
```python
import functools

import jax
import jax.numpy as jnp
from jax import lax
from jax.experimental import pallas as pl
from jax.experimental.pallas import tpu as pltpu
from jax.sharding import PartitionSpec as P

EPS = 1e-05
NEG = -1e30
ROOT_HALF = 0.7071067811865476
INV_ROOT_TWO_PI = 0.3989422804014327
HD = 64
GROUP = 128
F32 = jnp.float32
BF = jnp.bfloat16
MESH = pl.DeviceIdType.MESH
VMEM_LIMIT = 60 << 20


def nn(a, b):
    return lax.dot_general(a, b, (((1,), (0,)), ((), ())), preferred_element_type=F32)


def nt(a, b):
    return lax.dot_general(a, b, (((1,), (1,)), ((), ())), preferred_element_type=F32)


def tn(a, b):
    return lax.dot_general(a, b, (((0,), (0,)), ((), ())), preferred_element_type=F32)


def column_sum(x):
    return jnp.sum(x, 0, keepdims=True)


def normal_of(x):
    c = x - jnp.mean(x, -1, keepdims=True)
    r = lax.rsqrt(jnp.mean(c * c, -1, keepdims=True) + EPS)
    return c * r, r


def norm_back(d, n, r, g):
    dg = d * g
    return r * (dg - jnp.mean(dg, -1, keepdims=True) - n * jnp.mean(dg * n, -1, keepdims=True))


def gelu_and_slope(z):
    cdf = 0.5 * (1.0 + lax.erf(z * ROOT_HALF))
    return z * cdf, cdf + z * jnp.exp(-0.5 * z * z) * INV_ROOT_TWO_PI


def softmax_low(s):
    ex = jnp.exp(s - jnp.max(s, -1, keepdims=True))
    return (ex * (1.0 / jnp.sum(ex, -1, keepdims=True))).astype(BF)


def softmax_back(soft, d):
    soft = soft.astype(F32)
    return (soft * (d - jnp.sum(d * soft, -1, keepdims=True))).astype(BF)


def two_heads(t):
    left = lax.broadcasted_iota(jnp.int32, t.shape, 1) < HD
    zero = jnp.zeros_like(t)
    return jnp.concatenate([jnp.where(left, t, zero), jnp.where(left, zero, t)], 0)


def one_of_two(t):
    half = t.shape[0] // 2
    left = lax.broadcasted_iota(jnp.int32, (half, t.shape[1]), 1) < HD
    return jnp.where(left, t[:half], t[half:])


def pool_weights(h2, query, counts, chars_per):
    rows = h2.shape[0]
    words = rows // chars_per
    e = jnp.sum(h2 * query, -1, keepdims=True) * (h2.shape[1] ** -0.5)
    e = e.reshape(words, chars_per, 1)
    place = lax.broadcasted_iota(jnp.int32, (words, chars_per, 1), 1)
    e = jnp.where(place < counts.reshape(words, 1, 1), e, NEG)
    ex = jnp.exp(e - jnp.max(e, 1, keepdims=True))
    return ex / jnp.sum(ex, 1, keepdims=True)


class Net:
    def __init__(self, n_dp, n_wide):
        self.n_dp, self.n_wide, self.n_z = n_dp, n_wide, n_wide // 2
        self.dp, self.wide = lax.axis_index("dp"), lax.axis_index("wide")
        self.z, self.core = self.wide // 2, lax.rem(self.wide, 2)
        self.sibling = (self.dp, self.wide + 1 - 2 * self.core)

    def z_peer(self, j):
        z = lax.rem(self.z + j, self.n_z)
        return z, (self.dp, 2 * z + self.core)

    def dp_peer(self, j):
        q = lax.rem(self.dp + j, self.n_dp)
        return q, (q, self.wide)

    def wide_peer(self, j):
        w = lax.rem(self.wide + j, self.n_wide)
        return w, (self.dp, w)

    def greet(self, peers):
        barrier = pltpu.get_barrier_semaphore()
        for peer in peers:
            pl.semaphore_signal(barrier, inc=1, device_id=peer, device_id_type=MESH)

    def met(self, peers):
        pl.semaphore_wait(pltpu.get_barrier_semaphore(), len(peers))


def remote(src, dst, send, recv, peer):
    return pltpu.make_async_remote_copy(src_ref=src, dst_ref=dst, send_sem=send, recv_sem=recv, device_id=peer, device_id_type=MESH)


class Reduce:
    def __init__(self, net, grads, kept, from_core, part, from_dp, from_z, done, sems):
        self.net, self.grads = net, grads
        self.kept, self.from_core, self.part = kept, from_core, part
        self.from_dp, self.from_z, self.done = from_dp, from_z, done
        self.send, self.recv = sems
        self.span = part.shape[-1]

    @staticmethod
    def scratch(n_dp, n_z, rows, width):
        span = width // n_dp
        count = 2 + 2 * n_dp + n_z
        return [
            pltpu.VMEM((n_z, rows, width), BF),
            pltpu.VMEM((n_z, rows, width), BF),
            pltpu.VMEM((n_z, rows, span), BF),
            pltpu.VMEM((n_dp - 1, n_z, rows, span), BF),
            pltpu.VMEM((n_z - 1, rows, span), BF),
            pltpu.VMEM((n_dp, rows, span), BF),
            pltpu.SemaphoreType.DMA((count,)),
            pltpu.SemaphoreType.DMA((count,)),
        ]

    def lanes(self, q):
        return pl.ds(pl.multiple_of(q * self.span, GROUP), self.span)

    def to_core(self):
        net = self.net
        return remote(self.grads.at[:, 1 - net.core], self.from_core, self.send.at[0], self.recv.at[0], net.sibling)

    def own(self):
        return pltpu.make_async_copy(self.grads.at[:, self.net.core], self.kept, self.recv.at[1])

    def to_dp(self, j):
        q, peer = self.net.dp_peer(j)
        return remote(self.kept.at[:, :, self.lanes(q)], self.from_dp.at[j - 1], self.send.at[1 + j], self.recv.at[1 + j], peer)

    def to_z(self, j):
        z, peer = self.net.z_peer(j)
        at = 1 + self.net.n_dp + j
        return remote(self.part.at[z], self.from_z.at[j - 1], self.send.at[at], self.recv.at[at], peer)

    def to_all(self, j):
        net = self.net
        _, peer = net.dp_peer(j)
        at = 1 + net.n_dp + net.n_z + j
        mine = self.done.at[net.dp]
        return remote(mine, mine, self.send.at[at], self.recv.at[at], peer)

    def start(self):
        self.to_core().start()
        self.own().start()

    def over_dp(self):
        net = self.net
        self.own().wait()
        self.to_core().wait()

        @pl.loop(0, net.n_z)
        def _(z):
            self.kept[z] = (self.kept[z].astype(F32) + self.from_core[z].astype(F32)).astype(BF)

        for j in range(1, net.n_dp):
            self.to_dp(j).start()

    def over_z(self):
        net = self.net
        for j in range(1, net.n_dp):
            self.to_dp(j).wait()

        @pl.loop(0, net.n_z)
        def _(z):
            total = self.kept[z, :, self.lanes(net.dp)].astype(F32)
            for j in range(net.n_dp - 1):
                total = total + self.from_dp[j, z].astype(F32)
            self.part[z] = total.astype(BF)

        for j in range(1, net.n_z):
            self.to_z(j).start()

    def back_over_dp(self):
        net = self.net
        for j in range(1, net.n_z):
            self.to_z(j).wait()
        total = self.part[net.z].astype(F32)
        for j in range(net.n_z - 1):
            total = total + self.from_z[j].astype(F32)
        self.done[net.dp] = total.astype(BF)
        for j in range(1, net.n_dp):
            self.to_all(j).start()

    def finish(self, outs):
        net = self.net
        for j in range(1, net.n_dp):
            self.to_all(j).wait()
        rows = self.part.shape[1]
        for ref, first, columns, side in outs:
            for k in range(side):
                for at in range(0, columns, GROUP):
                    column = first + k * columns + at
                    q, lane = column // self.span, column % self.span
                    ref[k * rows : (k + 1) * rows, at : at + GROUP] = self.done[q, :, lane : lane + GROUP].astype(F32)


class ReduceRows:
    def __init__(self, net, row, from_core, of_dp, of_z, sems):
        self.net, self.row, self.from_core, self.of_dp, self.of_z = net, row, from_core, of_dp, of_z
        self.send, self.recv = sems

    @staticmethod
    def scratch(n_dp, n_z, width):
        count = 1 + n_dp + n_z
        return [
            pltpu.VMEM((1, width), F32),
            pltpu.VMEM((1, width), F32),
            pltpu.VMEM((n_dp, 1, width), F32),
            pltpu.VMEM((n_z, 1, width), F32),
            pltpu.SemaphoreType.DMA((count,)),
            pltpu.SemaphoreType.DMA((count,)),
        ]

    def to_core(self):
        return remote(self.row, self.from_core, self.send.at[0], self.recv.at[0], self.net.sibling)

    def to_dp(self, j):
        mine = self.of_dp.at[self.net.dp]
        return remote(mine, mine, self.send.at[j], self.recv.at[j], self.net.dp_peer(j)[1])

    def to_z(self, j):
        mine = self.of_z.at[self.net.z]
        at = self.net.n_dp + j
        return remote(mine, mine, self.send.at[at], self.recv.at[at], self.net.z_peer(j)[1])

    def start(self):
        self.to_core().start()

    def over_dp(self):
        self.to_core().wait()
        self.of_dp[self.net.dp] = self.row[...] + self.from_core[...]
        for j in range(1, self.net.n_dp):
            self.to_dp(j).start()

    def over_z(self):
        net = self.net
        for j in range(1, net.n_dp):
            self.to_dp(j).wait()
        total = self.of_dp[0]
        for q in range(1, net.n_dp):
            total = total + self.of_dp[q]
        self.of_z[net.z] = total
        for j in range(1, net.n_z):
            self.to_z(j).start()

    def finish(self, outs):
        net = self.net
        for j in range(1, net.n_z):
            self.to_z(j).wait()
        total = self.of_z[0]
        for z in range(1, net.n_z):
            total = total + self.of_z[z]
        for ref, first, length in outs:
            piece = ref.shape[1]
            vector = jnp.broadcast_to(total[:, first : first + length], (8, length))
            turned = pltpu.roll(vector, lax.rem(length - net.wide * piece, length), 1)
            ref[...] = turned[:1, :piece]


class Gather:
    def __init__(self, net, shards, wholes, send, recv, near):
        self.net, self.shards, self.wholes = net, shards, wholes
        self.send, self.recv, self.near = send, recv, near

    @staticmethod
    def scratch(count, n_z):
        return [
            pltpu.SemaphoreType.DMA((count, 2 * n_z)),
            pltpu.SemaphoreType.DMA((count, 2 * n_z)),
            pltpu.SemaphoreType.DMA((count,)),
        ]

    def block(self, a, owner):
        rows = self.shards[a].shape[0]
        return self.wholes[a].at[pl.ds(pl.multiple_of(owner * rows, rows), rows)]

    def along_z(self, a, j):
        net = self.net
        return remote(self.shards[a], self.block(a, net.wide), self.send.at[a, j], self.recv.at[a, net.wide], net.z_peer(j)[1])

    def across(self, a):
        net = self.net
        return remote(self.shards[a], self.block(a, net.wide), self.send.at[a, 0], self.recv.at[a, net.wide], net.sibling)

    def relayed(self, a, j):
        net = self.net
        owner = 2 * net.z_peer(j)[0] + net.core
        here = self.block(a, owner)
        return remote(here, here, self.send.at[a, net.n_z + j], self.recv.at[a, owner], net.sibling)

    def own(self, a):
        return pltpu.make_async_copy(self.shards[a], self.block(a, self.net.wide), self.near.at[a])

    def arrival(self, a, owner):
        here = self.block(a, owner)
        return remote(here, here, self.send.at[a, 0], self.recv.at[a, owner], self.net.sibling)

    def start(self, a):
        for j in range(1, self.net.n_z):
            self.along_z(a, j).start()
        self.across(a).start()
        self.own(a).start()

    def relay(self, a):
        net = self.net
        for j in range(1, net.n_z):
            self.arrival(a, 2 * net.z_peer(j)[0] + net.core).wait_recv()
            self.relayed(a, j).start()

    def finish(self, a):
        net = self.net
        self.own(a).wait()
        self.across(a).wait_send()
        for j in range(1, net.n_z):
            self.along_z(a, j).wait_send()
            self.relayed(a, j).wait_send()
        for z in range(net.n_z):
            self.arrival(a, 2 * z + 1 - net.core).wait_recv()


class SharedGather:
    def __init__(self, net, shards, wholes, send_z, send_dp, send_core, recv_z, recv_dp, recv_core, near):
        self.net, self.shards, self.wholes = net, shards, wholes
        self.send_z, self.send_dp, self.send_core = send_z, send_dp, send_core
        self.recv_z, self.recv_dp, self.recv_core, self.near = recv_z, recv_dp, recv_core, near

    @staticmethod
    def scratch(count, n_dp, n_z):
        sem = pltpu.SemaphoreType.DMA
        return [
            sem((count, n_z)), sem((count, n_z, n_dp)), sem((count, n_z)),
            sem((count, n_z)), sem((count, n_z, n_dp)), sem((count, n_z)), sem((count,)),
        ]

    def block(self, a, owner):
        rows = self.shards[a].shape[0]
        return self.wholes[a].at[pl.ds(pl.multiple_of(owner * rows, rows), rows)]

    def piece(self, a, owner, q):
        rows = self.shards[a].shape[0]
        some = rows // self.net.n_dp
        return self.wholes[a].at[pl.ds(pl.multiple_of(owner * rows + q * some, some), some)]

    def along_z(self, a, j):
        net = self.net
        some = self.shards[a].shape[0] // net.n_dp
        mine = self.shards[a].at[pl.ds(pl.multiple_of(net.dp * some, some), some)]
        return remote(mine, self.piece(a, net.wide, net.dp), self.send_z.at[a, j], self.recv_z.at[a, net.z], net.z_peer(j)[1])

    def from_z(self, a, j):
        net = self.net
        z, peer = net.z_peer(j)
        here = self.piece(a, 2 * z + net.core, net.dp)
        return remote(here, here, self.send_z.at[a, j], self.recv_z.at[a, z], peer)

    def over_dp(self, a, j, i):
        net = self.net
        z = net.z_peer(j)[0]
        here = self.piece(a, 2 * z + net.core, net.dp)
        return remote(here, here, self.send_dp.at[a, j, i], self.recv_dp.at[a, j, net.dp], net.dp_peer(i)[1])

    def from_dp(self, a, j, i):
        net = self.net
        z = net.z_peer(j)[0]
        q, peer = net.dp_peer(i)
        here = self.piece(a, 2 * z + net.core, q)
        return remote(here, here, self.send_dp.at[a, j, i], self.recv_dp.at[a, j, q], peer)

    def across(self, a, j):
        net = self.net
        z = net.z_peer(j)[0]
        here = self.block(a, 2 * z + net.core)
        source = self.shards[a] if j == 0 else here
        return remote(source, here, self.send_core.at[a, j], self.recv_core.at[a, z], net.sibling)

    def from_core(self, a, z):
        net = self.net
        here = self.block(a, 2 * z + 1 - net.core)
        return remote(here, here, self.send_core.at[a, 0], self.recv_core.at[a, z], net.sibling)

    def own(self, a):
        return pltpu.make_async_copy(self.shards[a], self.block(a, self.net.wide), self.near.at[a])

    def start(self):
        for a in range(len(self.shards)):
            for j in range(1, self.net.n_z):
                self.along_z(a, j).start()
        for a in range(len(self.shards)):
            self.across(a, 0).start()
            self.own(a).start()

    def relay(self, a):
        net = self.net
        for j in range(1, net.n_z):
            self.from_z(a, j).wait_recv()
            for i in range(1, net.n_dp):
                self.over_dp(a, j, i).start()

    def pass_on(self, a):
        net = self.net
        for j in range(1, net.n_z):
            for i in range(1, net.n_dp):
                self.from_dp(a, j, i).wait_recv()
            self.across(a, j).start()

    def finish(self, a):
        net = self.net
        self.own(a).wait()
        for j in range(1, net.n_z):
            self.along_z(a, j).wait_send()
            for i in range(1, net.n_dp):
                self.over_dp(a, j, i).wait_send()
        for j in range(net.n_z):
            self.across(a, j).wait_send()
            self.from_core(a, j).wait_recv()


class Exchange:
    def __init__(self, net, out, inbox, send, recv, near):
        self.net, self.out, self.inbox = net, out, inbox
        self.send, self.recv, self.near = send, recv, near

    @staticmethod
    def scratch(n_wide):
        return [pltpu.SemaphoreType.DMA((n_wide,)), pltpu.SemaphoreType.DMA((n_wide,)), pltpu.SemaphoreType.DMA(())]

    def to(self, w):
        net = self.net
        return remote(self.out.at[w], self.inbox.at[net.wide], self.send.at[w], self.recv.at[net.wide], (net.dp, w))

    def arrival(self, w):
        here = self.inbox.at[w]
        return remote(here, here, self.send.at[w], self.recv.at[w], (self.net.dp, w))

    def own(self):
        me = self.net.wide
        return pltpu.make_async_copy(self.out.at[me], self.inbox.at[me], self.near)

    def send_block(self, w):
        @pl.when(w != self.net.wide)
        def _():
            self.to(w).start()

        @pl.when(w == self.net.wide)
        def _():
            self.own().start()

    def send_all(self):
        for j in range(1, self.net.n_wide):
            self.to(self.net.wide_peer(j)[0]).start()
        self.own().start()

    def finish(self):
        for j in range(1, self.net.n_wide):
            w = self.net.wide_peer(j)[0]
            self.to(w).wait_send()
            self.arrival(w).wait_recv()
        self.own().wait()


def slices_of(ref, first, lengths):
    views = []
    for length in lengths:
        views.append(ref.at[:, first : first + length])
        first += length
    return views


def char_vectors(row, width, ff, out):
    return slices_of(row, 0, [width] * 6 + [ff, out])


def word_vectors(row, width, ff):
    return slices_of(row, row.shape[1] - 5 * width - ff, [width] * 5 + [ff])


def char_back_kernel(chars_per, steps, net_sizes, *refs):
    (
        gx_ref, c_ref, cnt_ref, qkv_ref, p_ref, o_ref, h1_ref, h2_ref, m_ref, s_ref, pooled_all, gx_all,
        win, wout, wup, wdn, wpj, vec, *refs
    ) = refs
    if net_sizes:
        word_grads, word_row, *refs = refs
    gc_ref, *refs = refs
    if net_sizes:
        outs, refs = refs[:23], refs[23:]
        accs, refs = refs[:13], refs[13:]
    else:
        accs, refs = refs[:13], refs[13:]
    dga, dsa, dwin, dwout, dgb, dsb, dwup, dub, dwdn, ddb, dqv, dwpj, dpb = accs
    gh1_ref, gm_ref, u_ref, gz_ref, gq_ref, *refs = refs
    rows, width = c_ref.shape
    ga, sa, gb, sb, _, qv, _, _ = char_vectors(vec, width, wup.shape[1], wpj.shape[1])
    phase, step = pl.program_id(0), pl.program_id(1)
    now = phase * steps + step
    factor = width**-0.5
    chunk = min(rows, 256)
    cw = chunk // chars_per

    if net_sizes:
        net = Net(*net_sizes)
        ff_grads, at_grads, row, *refs = refs
        word = Reduce(net, word_grads, *refs[:6], refs[6:8])
        ff = Reduce(net, ff_grads, *refs[8:14], refs[14:16])
        att = Reduce(net, at_grads, *refs[16:22], refs[22:24])
        rowsum = ReduceRows(net, row, *refs[24:27], refs[27:29])

        @pl.when(now == 0)
        def _():
            peers = [net.sibling] + [net.dp_peer(j)[1] for j in range(1, net.n_dp)] + [net.z_peer(j)[1] for j in range(1, net.n_z)]
            net.greet(peers)
            net.met(peers)
            word.start()

        schedule = {
            steps // 4: word.over_dp,
            steps - steps // 8: word.over_z,
            steps: ff.start,
            steps + steps // 8: ff.over_dp,
            steps + steps // 4: word.back_over_dp,
            steps + 3 * steps // 8: ff.over_z,
            steps + 5 * steps // 8: ff.back_over_dp,
        }
        for when, act in schedule.items():
            pl.when(now == when)(act)

    @pl.when(now == 0)
    def _():
        for acc in accs:
            acc[...] = jnp.zeros_like(acc)
        dwpj[...] = tn(pooled_all[...], gx_all[...])
        dpb[...] = column_sum(gx_all[...].astype(F32))

    here = pl.ds(pl.multiple_of(step * rows, rows), rows)

    @pl.when(phase == 0)
    def _():
        gp = nt(gx_ref[...], wpj[...]).astype(BF).astype(F32)
        for t in range(rows // chunk):
            at = slice(t * chunk, (t + 1) * chunk)
            wat = slice(t * cw, (t + 1) * cw)
            h2 = h2_ref[at, :]
            om = pool_weights(h2, qv[...], cnt_ref[wat, :], chars_per)
            gpb = jnp.broadcast_to(gp[wat, :].reshape(cw, 1, width), (cw, chars_per, width)).reshape(chunk, width)
            w = jnp.sum(h2 * gpb, -1, keepdims=True).reshape(cw, chars_per, 1)
            de = om * (w - jnp.sum(om * w, 1, keepdims=True))
            de = de.reshape(chunk, 1) * factor
            gh2 = om.reshape(chunk, 1) * gpb + de * qv[...]
            dqv[...] += column_sum(de * h2)
            gy = gh2.astype(BF)
            ddb[...] += column_sum(gy.astype(F32))
            gm_ref[at, :] = gy
            gz = (nt(gy, wdn[...]) * s_ref[at, :].astype(F32)).astype(BF)
            gz_ref[at, :] = gz
            dub[...] += column_sum(gz.astype(F32))
            du = nt(gz, wup[...])
            n, r = normal_of(h1_ref[at, :])
            dgb[...] += column_sum(du * n)
            dsb[...] += column_sum(du)
            u_ref[at, :] = (n * gb[...] + sb[...]).astype(BF)
            gh1_ref[pl.ds(pl.multiple_of(step * rows + t * chunk, chunk), chunk), :] = gh2 + norm_back(du, n, r, gb[...])
        dwup[...] += tn(u_ref[...], gz_ref[...])
        dwdn[...] += tn(gm_ref[...], m_ref[...])

    if net_sizes:
        n_z, n_wide = net.n_z, net.n_wide

        @pl.when(now == steps - 1)
        def _():
            up, proj = dwup.shape[1], dwpj.shape[1]
            down = dwdn[...].T
            some = width // n_wide
            side = down.shape[0] // n_wide // some
            for owner in range(n_wide):
                z, core = owner // 2, owner % 2
                mine = slice(owner * some, (owner + 1) * some)
                ff_grads[z, core, :, :up] = dwup[mine, :].astype(BF)
                ff_grads[z, core, :, up : up + proj] = dwpj[mine, :].astype(BF)
                for k in range(side):
                    first = (owner * side + k) * some
                    ff_grads[z, core, :, up + proj + k * width : up + proj + (k + 1) * width] = down[first : first + some].astype(BF)

    @pl.when(phase == 1)
    def _():
        g1 = gh1_ref[here, :].astype(BF)
        dwout[...] += tn(o_ref[...], g1)
        gm_ref[...] = nt(g1, wout[...]).astype(BF)
        for g in range(rows // GROUP):
            at = slice(g * GROUP, (g + 1) * GROUP)
            for p in range(width // GROUP):
                q = qkv_ref[at, p * GROUP : (p + 1) * GROUP]
                k = qkv_ref[at, width + p * GROUP : width + (p + 1) * GROUP]
                v = qkv_ref[at, 2 * width + p * GROUP : 2 * width + (p + 1) * GROUP]
                soft = p_ref[at, p * 2 * GROUP : (p + 1) * 2 * GROUP]
                gm = gm_ref[at, p * GROUP : (p + 1) * GROUP]
                dp = nt(gm, two_heads(v))
                gs = jnp.concatenate([softmax_back(soft[:, h * GROUP : (h + 1) * GROUP], dp[:, h * GROUP : (h + 1) * GROUP]) for h in range(2)], 1)
                gq_ref[at, p * GROUP : (p + 1) * GROUP] = (nn(gs, two_heads(k)) * HD**-0.5).astype(BF)
                gq_ref[at, width + p * GROUP : width + (p + 1) * GROUP] = one_of_two(tn(gs, q)).astype(BF)
                gq_ref[at, 2 * width + p * GROUP : 2 * width + (p + 1) * GROUP] = one_of_two(tn(soft, gm)).astype(BF)
        for t in range(rows // chunk):
            at = slice(t * chunk, (t + 1) * chunk)
            n, r = normal_of(c_ref[at, :].astype(F32))
            u_ref[at, :] = (n * ga[...] + sa[...]).astype(BF)
            da = nt(gq_ref[at, :], win[...])
            dga[...] += column_sum(da * n)
            dsa[...] += column_sum(da)
            gc_ref[at, :] = gh1_ref[pl.ds(pl.multiple_of(step * rows + t * chunk, chunk), chunk), :] + norm_back(da, n, r, ga[...])
        dwin[...] += tn(u_ref[...], gq_ref[...])

    if net_sizes:

        @pl.when(now == 2 * steps - 1)
        def _():
            some = width // n_wide
            for owner in range(n_wide):
                z, core = owner // 2, owner % 2
                mine = slice(owner * some, (owner + 1) * some)
                at_grads[z, core, :, : 3 * width] = dwin[mine, :].astype(BF)
                at_grads[z, core, :, 3 * width :] = dwout[mine, :].astype(BF)
            column, places = 0, []
            for acc in (dga, dsa, dgb, dsb, ddb, dqv, dub, dpb):
                row[:, column : column + acc.shape[1]] = acc[...]
                places.append((column, acc.shape[1]))
                column += acc.shape[1]
            row[:, column:] = word_row[...]
            (
                oga, osa, owin, owout, ogb, osb, oup, oub, odn, odb, oqv, opj, opb,
                xga, xsa, xwin, xwout, xgb, xsb, xup, xub, xdn, xdb,
            ) = outs
            for ref in (xga, xsa, xgb, xsb, xdb, xub):
                length = ref.shape[1] * n_wide
                places.append((column, length))
                column += length
            att.start()
            rowsum.start()
            word.finish(columns_of((xwin, xwout, xup), xdn))
            ff.finish(columns_of((oup, opj), odn))
            att.over_dp()
            rowsum.over_dp()
            att.over_z()
            rowsum.over_z()
            att.back_over_dp()
            ordered = (oga, osa, ogb, osb, odb, oqv, oub, opb, xga, xsa, xgb, xsb, xdb, xub)
            rowsum.finish([(ref, *place) for ref, place in zip(ordered, places)])
            att.finish(columns_of((owin, owout), None))


def columns_of(across, down):
    outs, column = [], 0
    for ref in across:
        outs.append((ref, column, ref.shape[1], 1))
        column += ref.shape[1]
    if down is not None:
        outs.append((down, column, down.shape[1], down.shape[0] // across[0].shape[0]))
    return outs


def whole_block(shape):
    return pl.BlockSpec(shape, lambda p, i: (0,) * len(shape))


def char_backward(gx, chars, counts, saved, weights, chars_per, rows, net_sizes=None, word_grads=None, word_row=None):
    total, width = chars.shape
    win, wout, wup, wdn, wpj, vec = weights
    pooled, qkv, soft, mixed, h1, h2, m, s = saved
    words, cw = total // chars_per, rows // chars_per
    ff, out = wup.shape[1], wpj.shape[1]
    steps = total // rows

    def early(count, columns):
        return pl.BlockSpec((count, columns), lambda p, i: (i + p * (steps - 1 - i), 0))

    def late(count, columns):
        return pl.BlockSpec((count, columns), lambda p, i: (i * p, 0))

    accs = [(1, width), (1, width), (width, 3 * width), (width, width), (1, width), (1, width), (width, ff), (1, ff),
            (width, ff), (1, width), (1, width), (width, out), (1, out)]
    in_specs = [early(cw, out), late(rows, width), early(cw, 1), late(rows, 3 * width), late(rows, 2 * width),
                late(rows, width), early(rows, width), early(rows, width), early(rows, ff), early(rows, ff),
                whole_block(pooled.shape), whole_block(gx.shape)] + [whole_block(w.shape) for w in weights]
    operands = [gx, chars, counts, qkv, soft, mixed, h1, h2, m, s, pooled, gx, *weights]
    scratch = [pltpu.VMEM((total, width), F32), pltpu.VMEM((rows, width), BF), pltpu.VMEM((rows, width), BF),
               pltpu.VMEM((rows, ff), BF), pltpu.VMEM((rows, 3 * width), BF)]
    out_shapes = [(total, width)]
    if net_sizes:
        n_dp, n_wide = net_sizes
        n_z, some = n_wide // 2, width // n_wide
        word_rows, word_width = word_grads.shape[2:]
        wide_d = n_wide * word_rows
        word_ff = word_row.shape[1] - 5 * wide_d
        operands += [word_grads, word_row]
        in_specs += [pl.BlockSpec(memory_space=pl.ANY), whole_block(word_row.shape)]
        part = lambda a: (1, a[1] // n_wide) if a[0] == 1 else (a[0] // n_wide, a[1])
        words_accs = [(1, wide_d), (1, wide_d), (wide_d, 3 * wide_d), (wide_d, wide_d), (1, wide_d), (1, wide_d), (wide_d, word_ff),
                      (1, word_ff), (word_ff, wide_d), (1, wide_d)]
        out_shapes += [part(a) for a in accs[:8] + [(ff, width)] + accs[9:] + words_accs]
        ff_width, at_width = ff + out + ff, 4 * width
        row_width = 6 * width + ff + out + word_row.shape[1]
        scratch = (
            [pltpu.VMEM(a, F32) for a in accs]
            + scratch
            + [pltpu.VMEM((n_z, 2, some, ff_width), BF), pltpu.VMEM((n_z, 2, some, at_width), BF), pltpu.VMEM((1, row_width), F32)]
            + Reduce.scratch(n_dp, n_z, word_rows, word_width)
            + Reduce.scratch(n_dp, n_z, some, ff_width)
            + Reduce.scratch(n_dp, n_z, some, at_width)
            + ReduceRows.scratch(n_dp, n_z, row_width)[1:]
        )
        params = pltpu.CompilerParams(vmem_limit_bytes=VMEM_LIMIT, collective_id=3, has_side_effects=True)
    else:
        out_shapes += accs
        params = pltpu.CompilerParams(vmem_limit_bytes=VMEM_LIMIT)
    return pl.pallas_call(
        functools.partial(char_back_kernel, chars_per, steps, net_sizes),
        grid=(2, steps),
        in_specs=in_specs,
        out_specs=[late(rows, width)] + [whole_block(a) for a in out_shapes[1:]],
        out_shape=[jax.ShapeDtypeStruct(a, F32) for a in out_shapes],
        scratch_shapes=scratch,
        compiler_params=params,
        name="char_backward",
    )(*operands)


def char_forward_kernel(chars_per, steps, net_sizes, lengths, *refs):
    c_ref, bias_ref, cnt_ref, *refs = refs
    if net_sizes:
        net = Net(*net_sizes)
        shards, word_shards, refs = refs[:6], refs[6:10], refs[10:]
        inbox, vec, *refs = refs
        char_out, word_out, refs = refs[:5], refs[5:9], refs[9:]
    else:
        win, wout, wup, wdn, wpj, vec, *refs = refs
        x_ref, *refs = refs
    pooled_ref, qkv_ref, p_ref, o_ref, h1_ref, h2_ref, m_ref, s_ref, *refs = refs
    h1_all, *refs = refs
    rows, width = c_ref.shape
    phase, step = pl.program_id(0), pl.program_id(1)
    now = phase * steps + step
    chunk = min(rows, 256)
    cw = chunk // chars_per

    if net_sizes:
        x_out, win, wout, wup, wdn, wpj, pieces, *refs = refs
        gather = Gather(net, shards, [win, wout, wup, wdn, wpj, pieces], *refs[:3])
        shared = SharedGather(net, word_shards, word_out, *refs[3:10])
        exchange = Exchange(net, x_out, inbox, *refs[10:13])
        keep = refs[13]
        first, later = (5, 0, 1), (2, 3, 4)

        @pl.when(now == 0)
        def _():
            peers = [net.wide_peer(j)[1] for j in range(1, net.n_wide)] + [net.dp_peer(j)[1] for j in range(1, net.n_dp)]
            net.greet(peers)
            net.met(peers)
            for a in first + later:
                gather.start(a)
            for a in first:
                gather.relay(a)
            shared.start()
            for a in first:
                gather.finish(a)
            column = 0
            for at, length in lengths:
                some = length // net.n_wide
                row = jnp.concatenate([pieces[w, :, at : at + some] for w in range(net.n_wide)], 1)
                vec[:, column : column + length] = row
                column += length

        @pl.when(now == 3 * steps // 8)
        def _():
            for a in later:
                gather.relay(a)

        @pl.when(now == steps)
        def _():
            for a in later:
                gather.finish(a)
            for a in range(5):
                pltpu.make_async_copy(gather.wholes[a], char_out[a], keep.at[a]).start()

        for a in range(4):

            @pl.when(now == steps - steps // 4 + a * steps // 8)
            def _(a=a):
                shared.relay(a)

            @pl.when(now == 2 * steps - 5 * steps // 8 + a * steps // 8)
            def _(a=a):
                shared.pass_on(a)

    ga, sa, gb, sb, db, qv, ub, pb = char_vectors(vec, width, wup.shape[1], wpj.shape[1])

    def block(t):
        return pl.ds(pl.multiple_of(step * rows + t * chunk, chunk), chunk)

    @pl.when(phase == 0)
    def _():
        n, _ = normal_of(c_ref[...].astype(F32))
        a = (n * ga[...] + sa[...]).astype(BF)
        qkv = nn(a, win[...])
        qkv_ref[:, :width] = (qkv[:, :width] * HD**-0.5).astype(BF)
        qkv_ref[:, width:] = qkv[:, width:].astype(BF)
        ri = lax.broadcasted_iota(jnp.int32, (GROUP, GROUP), 0) // chars_per
        ci = lax.broadcasted_iota(jnp.int32, (GROUP, GROUP), 1) // chars_per
        same = ri == ci
        for g in range(rows // GROUP):
            at = slice(g * GROUP, (g + 1) * GROUP)
            bias = jnp.where(same, jnp.broadcast_to(bias_ref[0, g : g + 1, :], (GROUP, GROUP)), NEG)
            for p in range(width // GROUP):
                q = qkv_ref[at, p * GROUP : (p + 1) * GROUP]
                k = qkv_ref[at, width + p * GROUP : width + (p + 1) * GROUP]
                v = qkv_ref[at, 2 * width + p * GROUP : 2 * width + (p + 1) * GROUP]
                s = nt(q, two_heads(k))
                soft = jnp.concatenate([softmax_low(s[:, h * GROUP : (h + 1) * GROUP] + bias) for h in range(2)], 1)
                p_ref[at, p * 2 * GROUP : (p + 1) * 2 * GROUP] = soft
                o_ref[at, p * GROUP : (p + 1) * GROUP] = nn(soft, two_heads(v)).astype(BF)
        for t in range(rows // chunk):
            at = slice(t * chunk, (t + 1) * chunk)
            h1 = c_ref[at, :].astype(F32) + nn(o_ref[at, :], wout[...])
            h1_ref[at, :] = h1
            h1_all[block(t), :] = h1

    @pl.when(phase == 1)
    def _():
        for t in range(rows // chunk):
            at = slice(t * chunk, (t + 1) * chunk)
            wat = slice(t * cw, (t + 1) * cw)
            h1 = h1_all[block(t), :]
            n, _ = normal_of(h1)
            u = (n * gb[...] + sb[...]).astype(BF)
            m, s = gelu_and_slope(nn(u, wup[...]) + ub[...])
            m_ref[at, :] = m.astype(BF)
            s_ref[at, :] = s.astype(BF)
            h2 = h1 + (nn(m_ref[at, :], wdn[...]) + db[...])
            h2_ref[at, :] = h2
            om = pool_weights(h2, qv[...], cnt_ref[wat, :], chars_per)
            pooled_ref[wat, :] = jnp.sum(om * h2.reshape(cw, chars_per, width), 1).astype(BF)
        x = (nn(pooled_ref[...], wpj[...]) + pb[...]).astype(BF)
        if net_sizes:
            cap = x_out.shape[1]
            words = rows // chars_per
            first_word = step * words
            target = first_word // cap
            x_out[target, pl.ds(pl.multiple_of(lax.rem(first_word, cap), words), words)] = x
            pl.when(lax.rem(first_word + words, cap) == 0)(lambda: exchange.send_block(target))
        else:
            x_ref[...] = x

    if net_sizes:

        @pl.when(now == 2 * steps - 1)
        def _():
            for a in range(4):
                shared.finish(a)
            exchange.finish()
            for a in range(5):
                pltpu.make_async_copy(gather.wholes[a], char_out[a], keep.at[a]).wait()


def char_forward(chars, key_bias, counts, weights, chars_per, rows, net_sizes=None, word_shards=None, lengths=None, cap=None):
    total, width = chars.shape
    words, cw = total // chars_per, rows // chars_per
    ff, out = weights[2].shape[1], weights[4].shape[1]
    steps = total // rows

    def early(count, columns):
        return pl.BlockSpec((count, columns), lambda p, i: (i + p * (steps - 1 - i), 0))

    def late(count, columns):
        return pl.BlockSpec((count, columns), lambda p, i: (i * p, 0))

    saved = [((words, width), BF, cw, late), ((total, 3 * width), BF, rows, early), ((total, 2 * width), BF, rows, early),
             ((total, width), BF, rows, early), ((total, width), F32, rows, early), ((total, width), F32, rows, late),
             ((total, ff), BF, rows, late), ((total, ff), BF, rows, late)]
    saved_specs = [where(count, s[1]) for s, _, count, where in saved]
    saved_shapes = [jax.ShapeDtypeStruct(s, d) for s, d, _, _ in saved]
    groups = rows // GROUP
    bias_spec = pl.BlockSpec((1, groups, GROUP), lambda p, i: (i + p * (steps - 1 - i), 0, 0))
    in_specs = [early(rows, width), bias_spec, late(cw, 1)]
    operands = [chars, key_bias.reshape(steps, groups, GROUP), counts]
    scratch = [pltpu.VMEM((total, width), F32)]
    anywhere = pl.BlockSpec(memory_space=pl.ANY)
    if net_sizes:
        n_dp, n_wide = net_sizes
        n_z = n_wide // 2
        in_specs += [anywhere] * 10
        operands += [*weights, *word_shards]
        vec_shape = jax.ShapeDtypeStruct((1, sum(length for _, length in lengths)), F32)
        grown = lambda a: jax.ShapeDtypeStruct((a.shape[0] * n_wide, a.shape[1]), a.dtype)
        fulls = [grown(a) for a in weights[:5]]
        out_specs = [anywhere, whole_block(vec_shape.shape)] + [anywhere] * 9 + saved_specs
        out_shapes = [jax.ShapeDtypeStruct((n_wide, cap, out), BF), vec_shape, *fulls, *(grown(a) for a in word_shards), *saved_shapes]
        scratch += (
            [pltpu.VMEM((n_wide, cap, out), BF)]
            + [pltpu.VMEM(a.shape, a.dtype) for a in fulls]
            + [pltpu.VMEM((n_wide, *weights[5].shape[1:]), F32)]
            + Gather.scratch(6, n_z)
            + SharedGather.scratch(4, n_dp, n_z)
            + Exchange.scratch(n_wide)
            + [pltpu.SemaphoreType.DMA((5,))]
        )
        params = pltpu.CompilerParams(vmem_limit_bytes=VMEM_LIMIT, collective_id=1, has_side_effects=True)
    else:
        in_specs += [whole_block(w.shape) for w in weights]
        operands += [*weights]
        out_specs = [late(cw, out)] + saved_specs
        out_shapes = [jax.ShapeDtypeStruct((words, out), BF), *saved_shapes]
        params = pltpu.CompilerParams(vmem_limit_bytes=VMEM_LIMIT)
    return pl.pallas_call(
        functools.partial(char_forward_kernel, chars_per, steps, net_sizes, lengths),
        grid=(2, steps),
        in_specs=in_specs,
        out_specs=out_specs,
        out_shape=out_shapes,
        scratch_shapes=scratch,
        compiler_params=params,
        name="char_forward",
    )(*operands)


def word_kernel(slot_cap, net_sizes, *refs):
    arrived, bucket, assign, seg_row, seg_col, grad_ref, win, wout, wup, wdn, vec, out_ref, back_out, *refs = refs
    length, width = grad_ref.shape
    ff = wup.shape[1]
    if net_sizes:
        net = Net(*net_sizes)
        word_grads, word_row, *refs = refs
        dga, dsa, dgb, dsb, ddb, dub = word_vectors(word_row, width, ff)
    else:
        dga, dsa, dwin, dwout, dgb, dsb, dwup, dub, dwdn, ddb, *refs = refs
    qkv_ref, p_ref, mix_ref, h_ref, s_ref, gq_ref, *refs = refs
    ga, sa, gb, sb, db, ub = word_vectors(vec, width, ff)
    owners = assign.shape[1]
    slots = owners * slot_cap
    if net_sizes:
        back_ref, *sems = refs
        exchange = Exchange(net, back_ref, back_out, *sems)
        peers = [net.wide_peer(j)[1] for j in range(1, net.n_wide)]
        net.greet(peers)
    named = jnp.where(bucket[...] == lax.broadcasted_iota(jnp.int32, (length, owners), 1), 1.0, 0.0)
    ri = lax.broadcasted_iota(jnp.int32, (length, length), 0)
    ci = lax.broadcasted_iota(jnp.int32, (length, length), 1)
    earlier = nn(jnp.where(ci < ri, 1.0, 0.0).astype(BF), named.astype(BF))
    slot = jnp.sum(named * (assign[...].astype(F32) * slot_cap + earlier), -1, keepdims=True).astype(jnp.int32)
    hot = jnp.where(lax.broadcasted_iota(jnp.int32, (length, slots), 1) == slot, 1.0, 0.0).astype(BF)
    x = nn(hot, arrived[...].reshape(slots, width))
    n1, r1 = normal_of(x)
    a = (n1 * ga[...] + sa[...]).astype(BF)
    qkv = nn(a, win[...])
    qkv_ref[:, :width] = (qkv[:, :width] * HD**-0.5).astype(BF)
    qkv_ref[:, width:] = qkv[:, width:].astype(BF)
    bias = jnp.where((seg_row[...] == seg_col[...]) & (ci <= ri), 0.0, NEG)

    def pair(p):
        return [qkv_ref[:, i * width + p * GROUP : i * width + (p + 1) * GROUP] for i in range(3)]

    for p in range(width // GROUP):
        q, k, v = pair(p)
        s = nt(q, two_heads(k))
        soft = jnp.concatenate([softmax_low(s[:, h * length : (h + 1) * length] + bias) for h in range(2)], 1)
        p_ref[:, 2 * p * length : (2 * p + 2) * length] = soft
        mix_ref[:, p * GROUP : (p + 1) * GROUP] = nn(soft, two_heads(v)).astype(BF)
    inner = x + nn(mix_ref[...], wout[...])
    n2, r2 = normal_of(inner)
    u = (n2 * gb[...] + sb[...]).astype(BF)
    h, slope = gelu_and_slope(nn(u, wup[...]) + ub[...])
    h_ref[...] = h.astype(BF)
    s_ref[...] = slope
    out_ref[...] = inner + (nn(h_ref[...], wdn[...]) + db[...])
    g = grad_ref[...]
    gz = (nt(g, wdn[...]) * s_ref[...]).astype(BF)
    du = nt(gz, wup[...])
    g1 = g.astype(F32) + norm_back(du, n2, r2, gb[...])
    g1_low = g1.astype(BF)
    gm = nt(g1_low, wout[...]).astype(BF)
    for p in range(width // GROUP):
        q, k, v = pair(p)
        gmp = gm[:, p * GROUP : (p + 1) * GROUP]
        soft = p_ref[:, 2 * p * length : (2 * p + 2) * length]
        dp = nt(gmp, two_heads(v))
        gs = jnp.concatenate([softmax_back(soft[:, h * length : (h + 1) * length], dp[:, h * length : (h + 1) * length]) for h in range(2)], 1)
        gq_ref[:, p * GROUP : (p + 1) * GROUP] = (nn(gs, two_heads(k)) * HD**-0.5).astype(BF)
        gq_ref[:, width + p * GROUP : width + (p + 1) * GROUP] = one_of_two(tn(gs, q)).astype(BF)
        gq_ref[:, 2 * width + p * GROUP : 2 * width + (p + 1) * GROUP] = one_of_two(tn(soft, gmp)).astype(BF)
    da = nt(gq_ref[...], win[...])
    gx = (g1 + norm_back(da, n1, r1, ga[...])).astype(BF)
    back = tn(hot, gx).astype(BF).reshape(owners, slot_cap, width)
    if net_sizes:
        back_ref[...] = back
        net.met(peers)
        exchange.send_all()
        some = width // net.n_wide
        side = ff // width

        def put(value, column):
            value = value.astype(BF)
            for w in range(net.n_wide):
                word_grads[w // 2, w % 2, :, column : column + value.shape[1]] = value[w * some : (w + 1) * some]

        put(tn(a, gq_ref[...]), 0)
        put(tn(mix_ref[...], g1_low), 3 * width)
        put(tn(u, gz), 4 * width)
        down = tn(h_ref[...], g).astype(BF)
        for w in range(net.n_wide):
            for k in range(side):
                first = (w * side + k) * some
                column = 4 * width + ff + k * width
                word_grads[w // 2, w % 2, :, column : column + width] = down[first : first + some]
    else:
        back_out[...] = back
        dwin[...] = tn(a, gq_ref[...])
        dwout[...] = tn(mix_ref[...], g1_low)
        dwup[...] = tn(u, gz)
        dwdn[...] = tn(h_ref[...], g)
    dga[...] = column_sum(da * n1)
    dsa[...] = column_sum(da)
    dgb[...] = column_sum(du * n2)
    dsb[...] = column_sum(du)
    dub[...] = column_sum(gz.astype(F32))
    ddb[...] = column_sum(g.astype(F32))
    if net_sizes:
        exchange.finish()


def word_block(arrived, bucket, assign, segments, grad, weights, slot_cap, net_sizes=None):
    length, width = grad.shape
    ff = weights[2].shape[1]
    owners = assign.shape[1]
    low = lambda *s: jax.ShapeDtypeStruct(s, BF)
    full = lambda *s: jax.ShapeDtypeStruct(s, F32)
    vmem = pl.BlockSpec(memory_space=pltpu.VMEM)
    out_shapes, out_specs = [full(length, width), low(owners, slot_cap, width)], [vmem, vmem]
    scratch = [pltpu.VMEM((length, 3 * width), BF), pltpu.VMEM((length, width // HD * length), BF), pltpu.VMEM((length, width), BF),
               pltpu.VMEM((length, ff), BF), pltpu.VMEM((length, ff), F32), pltpu.VMEM((length, 3 * width), BF)]
    if net_sizes:
        n_dp, n_wide = net_sizes
        out_shapes += [low(n_wide // 2, 2, width // n_wide, 4 * width + 2 * ff), full(1, 5 * width + ff)]
        out_specs = [vmem, pl.BlockSpec(memory_space=pl.ANY), vmem, vmem]
        scratch += [pltpu.VMEM((owners, slot_cap, width), BF)] + Exchange.scratch(n_wide)
        params = pltpu.CompilerParams(vmem_limit_bytes=VMEM_LIMIT, collective_id=2, has_side_effects=True)
    else:
        row = full(1, width)
        out_shapes += [row, row, full(width, 3 * width), full(width, width), row, row, full(width, ff), full(1, ff), full(ff, width), row]
        out_specs += [vmem] * 10
        params = pltpu.CompilerParams(vmem_limit_bytes=VMEM_LIMIT)
    return pl.pallas_call(
        functools.partial(word_kernel, slot_cap, net_sizes),
        in_specs=[vmem] * 11,
        out_specs=out_specs,
        out_shape=out_shapes,
        scratch_shapes=scratch,
        compiler_params=params,
        name="word_block",
    )(arrived, bucket, assign, segments, segments.reshape(length, 1), grad, *weights)


def gathered(shard):
    return lax.all_gather(shard, "wide", axis=0, tiled=True)


def exchanged(blocks):
    return lax.all_to_all(blocks, "wide", split_axis=0, concat_axis=0, tiled=True)


def summed(grad):
    part = lax.psum_scatter(grad.astype(BF), "wide", scatter_dimension=0, tiled=True)
    return lax.psum(part, "dp").astype(F32)


def shards(
    chars, char_counts, buckets, assign, segments,
    char_gain, char_shift, char_inproj, char_outproj, char_gain_mid, char_shift_mid, char_up, char_up_bias, char_down, char_down_bias,
    pool_query, char_proj, char_proj_bias,
    word_gain, word_shift, word_inproj, word_outproj, word_gain_mid, word_shift_mid, word_up, word_up_bias, word_down, word_down_bias,
    out_grad,
):
    n_dp, n_wide = lax.axis_size("dp"), lax.axis_size("wide")
    cap, chars_per, width = chars.shape[2:]
    slots = n_wide * cap
    rows = chars.reshape(slots * chars_per, width)
    counts = char_counts.reshape(slots, 1)
    key_bias = jnp.where(lax.broadcasted_iota(jnp.int32, (slots, chars_per), 1) < counts, 0.0, NEG)
    block = min(512, rows.shape[0])
    char_shards = (char_inproj, char_outproj, char_up, char_down, char_proj)
    word_shards = (word_inproj, word_outproj, word_up, word_down)
    vectors = (char_gain, char_shift, char_gain_mid, char_shift_mid, char_down_bias, pool_query, char_up_bias, char_proj_bias,
               word_gain, word_shift, word_gain_mid, word_shift_mid, word_down_bias, word_up_bias)
    matrices = char_shards + word_shards
    fast = (
        all(m.shape[0] % 16 == 0 for m in char_shards)
        and all(m.shape[0] % (16 * n_dp) == 0 for m in word_shards)
        and cap % (block // chars_per) == 0
        and (4 * width) % (GROUP * n_dp) == 0
        and n_wide % 2 == 0
    )
    bucket, names, seg, upstream = buckets[0], assign[None], segments, out_grad[0]
    if fast:
        sizes = (n_dp, n_wide)
        padded, lengths, at = [], [], 0
        for v in vectors:
            room = -(-v.shape[0] // GROUP) * GROUP
            padded.append(jnp.pad(v.astype(F32), (0, room - v.shape[0])))
            lengths.append((at, v.shape[0] * n_wide))
            at += room
        pieces = jnp.concatenate(padded).reshape(1, 1, at)
        arrived, vec, *rest = char_forward(rows, key_bias, counts, (*char_shards, pieces), chars_per, block, sizes, word_shards, tuple(lengths), cap)
        char_full, word_full, saved = rest[:5], rest[5:9], rest[9:]
        result, returned, word_grads, word_row = word_block(arrived, bucket, names, seg, upstream, (*word_full, vec), cap, sizes)
        incoming = returned.reshape(slots, -1)
        outs = char_backward(incoming, rows, counts, saved, (*char_full, vec), chars_per, block, sizes, word_grads, word_row)
        char_grads, *grads = outs
        grads = [g[0] if g.shape[0] == 1 else g for g in grads]
    else:
        vec = jnp.concatenate([gathered(v) for v in vectors]).astype(F32)[None]
        char_full, word_full = [gathered(m) for m in char_shards], [gathered(m) for m in word_shards]
        outgoing, *saved = char_forward(rows, key_bias, counts, (*char_full, vec), chars_per, block)
        arrived = exchanged(outgoing.reshape(n_wide, cap, -1))
        result, back, *word_grads = word_block(arrived, bucket, names, seg, upstream, (*word_full, vec), cap)
        incoming = exchanged(back).reshape(slots, -1)
        char_grads, *grads = char_backward(incoming, rows, counts, saved, (*char_full, vec), chars_per, block)
        grads[8] = grads[8].T
        grads = [summed(g[0] if g.shape[0] == 1 else g) for g in grads + word_grads]
    return (result[None], char_grads.reshape(chars.shape), *grads)


def solution(mesh):
    whole, split = ("dp", "wide"), "wide"
    row, flat = P(split, None), P(split)
    word = [flat, flat, row, row, flat, flat, row, flat, row, flat]
    char = word + [flat, row, flat]
    chars = P(whole, None, None, None, None)
    three = P(whole, None, None)
    return jax.shard_map(
        shards,
        mesh=mesh,
        in_specs=(chars, three, three, P(), P(whole, None), *char, *word, three),
        out_specs=(three, chars, *char, *word),
        check_vma=False,
    )
```

time: 645 us -> 312 us (0.48); the launches traced: 635 us -> 312 us
  blocking collectives: 201 us -> 0 us
  Pallas kernels: 142 us -> 270 us
  waiting for transfers between devices: 109 us -> 0 us
  other arithmetic: 59 us -> 0.62 us
  matrix products: 36.3 us -> 0 us
  starting transfers between devices: 25 us -> 0 us
  between operations: 17.5 us -> 0.92 us
    pallas_call x2 -> x3, Pallas kernels: 142 us -> 270 us  [the longest x1 148 us: char_backward(): pl.pallas_call(functools.partial(char_back_kernel, chars_per, steps, net_...]
    all_gather x8 -> x0, blocking collectives: 119 us -> none  [the longest x1 18.1 us: shards(): lax.all_gather(word_outproj, 'wide', axis=0, tiled=True)]
    psum x2 -> x0, waiting for transfers between devices: 73.5 us -> none  [the longest x1 39 us: shards(): lax.psum(char_parts[8].astype(jnp.bfloat16), 'dp').astype(jnp.float32)]
    unnamed x2 -> x0, blocking collectives: 61.2 us -> none
    convert_element_type x46 -> x0, other arithmetic: 41 us -> none  [the longest x1 1.78 us: shards(): lax.psum(word_parts[6].astype(jnp.bfloat16), 'dp').astype(jnp.float32)]
    dot_general x18 -> x0, matrix products: 36.3 us -> none  [the longest x4 11.4 us: dense_right(): lax.dot_general(left, right, (((1,), (1,)), ((), ())), preferred_element_...]
    all_to_all x7 -> x0, waiting for transfers between devices: 32.9 us -> none  [the longest x6 32.9 us: sum_at_owner(): lax.all_to_all(parts, axis, split_axis=0, concat_axis=0, tiled=True)]
    all_to_all x7 -> x0, starting transfers between devices: 24.2 us -> none  [the longest x6 20.7 us: sum_at_owner(): lax.all_to_all(parts, axis, split_axis=0, concat_axis=0, tiled=True)]
  transfers between devices with their start and end apart: 16 -> 0, of which waited for: 7 -> 0; matrix products, arithmetic and copies ran while one was open for 19% -> 0% of each run, Pallas kernels for 22% -> 0%
where the time goes in v2:
time: 312 us
  Pallas kernels  270 us (87%)
  local copies, waits for them, and re-layouts  40.4 us (13%)
    pallas_call x1, Pallas kernels, char_backward(): pl.pallas_call(functools.partial(char_back_kernel, chars_per, steps, net_...  148 us
    pallas_call x1, Pallas kernels, char_forward(): pl.pallas_call(functools.partial(char_forward_kernel, chars_per, steps, n...  99.3 us
    unnamed x86, local copies, waits for them, and re-layouts  25.4 us
    pallas_call x1, Pallas kernels, word_block(): pl.pallas_call(functools.partial(word_kernel, slot_cap, net_sizes), in_sp...  22.3 us
    pad x12, local copies, waits for them, and re-layouts, shards(): padded.append(jnp.pad(v.astype(F32), (0, room - v.shape[0])))  7.92 us

profile of v2, /device:TPU:0, one launch (start us, length us, event | category | flops | bytes accessed | tf_op | source)
XLA Modules:
  0.0 312.0 jit_solution(1501602612366364535)
XLA Ops:
  0.7 0.7 pad.50
  1.3 0.7 pad.51
  2.0 0.7 pad.52
  2.6 0.7 pad.53
  3.3 0.7 pad.54
  4.0 0.7 pad.55
  4.6 0.7 pad.56
  5.3 0.7 pad.57
  5.9 0.7 pad.58
  6.6 0.7 pad.59
  7.3 0.7 pad.60
  7.9 0.7 pad.61
  9.8 0.8 dynamic-update-slice.6
  11.8 0.8 dynamic-update-slice.13
  13.3 0.8 lt.13
  14.1 1.5 copy.55.refs_1_
  15.6 1.5 copy.56.refs_4_
  17.3 0.6 compare_select_fusion.refs_1_
  17.9 1.6 reshape.85.refs_2_
  19.5 99.3 %char_forward.1 = (bf16[8,64,512]{2,1,0:T(8,128)(2,1)}, f32[1,7680]{1,0:T(1,128)}, bf16[256,768]{1,0:T(8,128)(2,1)}, bf16[256,256]{1,0:T(8,128)(2,1)}, bf16[256,...) custom-call(bf16[8192,256]{1,0:T(8,128)(2,1)} %bitcast.24, ...), custom_call_target="tpu_custom_call" | custom-call | tf_op jit(solution)/shard_map/char_forward/pallas_call | solution.py:936
  118.8 22.3 %word_block.1 = (f32[256,512]{1,0:T(8,128)}, bf16[8,64,512]{2,1,0:T(8,128)(2,1)}, bf16[4,2,64,6144]{3,2,1,0:T(8,128)(2,1)}, f32[1,4608]{1,0:T(1,128)}) custom-call(bf16[8,64,512]{2,1,0:T(8,128)(2,1)} %get-tuple-element.72.refs_0_, s32[256,1]{1,0:T(8,128)} %copy.55.refs_1_, s32[1,8]{1,0:T(1,128)} %bitcast.34, s32[1,256]{1,0:T(1,128)} %refs_3_.3, ...), custom_call_target="tpu_custom_call" | custom-call | tf_op jit(solution)/shard_map/word_block/pallas_call | solution.py:1073
  141.1 148.4 %char_backward.1 = (f32[8192,256]{1,0:T(8,128)}, f32[1,32]{1,0:T(1,128)}, f32[1,32]{1,0:T(1,128)}, f32[32,768]{1,0:T(8,128)}, f32[32,256]{1,0:T(8,128)}, /*index...) custom-call(bf16[512,512]{1,0:T(8,128)(2,1)} %bitcast.27, ...), custom_call_target="tpu_custom_call" | custom-call | tf_op jit(solution)/shard_map/char_backward/pallas_call | solution.py:739
  289.6 0.8 copy.97
  290.6 7.9 %copy.98 = f32[1,8,64,16,256]{4,3,2,1,0:T(8,128)} copy(f32[1,8,64,16,256]{4,3,2,1,0:T(8,128)} %bitcast.26) | data formatting | bytes 16777216
  299.5 0.6 copy.101
  301.8 0.7 copy.105
  303.0 0.7 copy.107
  304.7 0.6 copy.110
  306.9 0.7 copy.114
  307.6 0.7 copy.115
  309.3 0.8 copy.118
  310.7 0.8 copy.120
  (81 shorter events, 11.3 us)
Async XLA Ops:
  141.1 148.4 %copy-start.2 = (f32[256,512]{1,0:T(8,128)S(1)}, f32[256,512]{1,0:T(8,128)}, u32[]{:S(2)}) copy-start(f32[256,512]{1,0:T(8,128)} %get-tuple-element.78) | copy-start | bytes 1572868
  290.4 8.1 %copy-start.23 = (f32[1,32]{1,0:T(1,128)S(1)}, f32[1,32]{1,0:T(1,128)}, u32[]{:S(2)}) copy-start(f32[1,32]{1,0:T(1,128)} %get-tuple-element.96) | copy-start | bytes 388
  290.4 8.6 %copy-start.22 = (f32[1,32]{1,0:T(1,128)S(1)}, f32[1,32]{1,0:T(1,128)}, u32[]{:S(2)}) copy-start(f32[1,32]{1,0:T(1,128)} %get-tuple-element.97) | copy-start | bytes 388
  290.4 9.2 %copy-start.7 = (f32[32,768]{1,0:T(8,128)S(1)}, f32[32,768]{1,0:T(8,128)}, u32[]{:S(2)}) copy-start(f32[32,768]{1,0:T(8,128)} %get-tuple-element.148) | copy-start | bytes 294916
  290.4 9.8 %copy-start.9 = (f32[32,256]{1,0:T(8,128)S(1)}, f32[32,256]{1,0:T(8,128)}, u32[]{:S(2)}) copy-start(f32[32,256]{1,0:T(8,128)} %get-tuple-element.149) | copy-start | bytes 98308
  290.4 10.4 %copy-start.21 = (f32[1,32]{1,0:T(1,128)S(1)}, f32[1,32]{1,0:T(1,128)}, u32[]{:S(2)}) copy-start(f32[1,32]{1,0:T(1,128)} %get-tuple-element.100) | copy-start | bytes 388
  290.4 10.9 %copy-start.20 = (f32[1,32]{1,0:T(1,128)S(1)}, f32[1,32]{1,0:T(1,128)}, u32[]{:S(2)}) copy-start(f32[1,32]{1,0:T(1,128)} %get-tuple-element.101) | copy-start | bytes 388
  290.4 11.4 %copy-start.6 = (f32[32,1024]{1,0:T(8,128)S(1)}, f32[32,1024]{1,0:T(8,128)}, u32[]{:S(2)}) copy-start(f32[32,1024]{1,0:T(8,128)} %get-tuple-element.152) | copy-start | bytes 393220
  290.4 12.1 %copy-start.19 = (f32[1,128]{1,0:T(1,128)S(1)}, f32[1,128]{1,0:T(1,128)}, u32[]{:S(2)}) copy-start(f32[1,128]{1,0:T(1,128)} %get-tuple-element.103) | copy-start | bytes 1540
  290.4 12.6 %copy-start.5 = (f32[128,256]{1,0:T(8,128)S(1)}, f32[128,256]{1,0:T(8,128)}, u32[]{:S(2)}) copy-start(f32[128,256]{1,0:T(8,128)} %get-tuple-element.154) | copy-start | bytes 393220
  290.4 13.2 %copy-start.18 = (f32[1,32]{1,0:T(1,128)S(1)}, f32[1,32]{1,0:T(1,128)}, u32[]{:S(2)}) copy-start(f32[1,32]{1,0:T(1,128)} %get-tuple-element.105) | copy-start | bytes 388
  290.4 13.7 %copy-start.17 = (f32[1,32]{1,0:T(1,128)S(1)}, f32[1,32]{1,0:T(1,128)}, u32[]{:S(2)}) copy-start(f32[1,32]{1,0:T(1,128)} %get-tuple-element.106) | copy-start | bytes 388
  290.5 14.2 %copy-start.8 = (f32[32,512]{1,0:T(8,128)S(1)}, f32[32,512]{1,0:T(8,128)}, u32[]{:S(2)}) copy-start(f32[32,512]{1,0:T(8,128)} %get-tuple-element.157) | copy-start | bytes 196612
  290.5 14.9 %copy-start.16 = (f32[1,64]{1,0:T(1,128)S(1)}, f32[1,64]{1,0:T(1,128)}, u32[]{:S(2)}) copy-start(f32[1,64]{1,0:T(1,128)} %get-tuple-element.108) | copy-start | bytes 772
  290.5 15.4 %copy-start.15 = (f32[1,64]{1,0:T(1,128)S(1)}, f32[1,64]{1,0:T(1,128)}, u32[]{:S(2)}) copy-start(f32[1,64]{1,0:T(1,128)} %get-tuple-element.109) | copy-start | bytes 772
  290.5 15.9 %copy-start.14 = (f32[1,64]{1,0:T(1,128)S(1)}, f32[1,64]{1,0:T(1,128)}, u32[]{:S(2)}) copy-start(f32[1,64]{1,0:T(1,128)} %get-tuple-element.110) | copy-start | bytes 772
  290.5 16.4 %copy-start.3 = (f32[64,1536]{1,0:T(8,128)S(1)}, f32[64,1536]{1,0:T(8,128)}, u32[]{:S(2)}) copy-start(f32[64,1536]{1,0:T(8,128)} %get-tuple-element.161) | copy-start | bytes 1179652
  290.5 17.1 %copy-start.4 = (f32[64,512]{1,0:T(8,128)S(1)}, f32[64,512]{1,0:T(8,128)}, u32[]{:S(2)}) copy-start(f32[64,512]{1,0:T(8,128)} %get-tuple-element.162) | copy-start | bytes 393220
  290.5 17.8 %copy-start.13 = (f32[1,64]{1,0:T(1,128)S(1)}, f32[1,64]{1,0:T(1,128)}, u32[]{:S(2)}) copy-start(f32[1,64]{1,0:T(1,128)} %get-tuple-element.113) | copy-start | bytes 772
  290.5 18.3 %copy-start.12 = (f32[1,64]{1,0:T(1,128)S(1)}, f32[1,64]{1,0:T(1,128)}, u32[]{:S(2)}) copy-start(f32[1,64]{1,0:T(1,128)} %get-tuple-element.114) | copy-start | bytes 772
  290.5 18.8 %copy-start.1 = (f32[64,2048]{1,0:T(8,128)S(1)}, f32[64,2048]{1,0:T(8,128)}, u32[]{:S(2)}) copy-start(f32[64,2048]{1,0:T(8,128)} %get-tuple-element.165) | copy-start | bytes 1572868
  290.5 19.6 %copy-start.10 = (f32[1,256]{1,0:T(1,128)S(1)}, f32[1,256]{1,0:T(1,128)}, u32[]{:S(2)}) copy-start(f32[1,256]{1,0:T(1,128)} %get-tuple-element.116) | copy-start | bytes 3076
  290.6 20.1 %copy-start = (f32[256,512]{1,0:T(8,128)S(1)}, f32[256,512]{1,0:T(8,128)}, u32[]{:S(2)}) copy-start(f32[256,512]{1,0:T(8,128)} %get-tuple-element.167) | copy-start | bytes 1572868
  290.6 20.9 %copy-start.11 = (f32[1,64]{1,0:T(1,128)S(1)}, f32[1,64]{1,0:T(1,128)}, u32[]{:S(2)}) copy-start(f32[1,64]{1,0:T(1,128)} %get-tuple-element.118) | copy-start | bytes 772

commit v3 on v2

--- a/solution.py
+++ b/solution.py
@@ -31,6 +31,10 @@
     return lax.dot_general(a, b, (((0,), (0,)), ((), ())), preferred_element_type=F32)
 
 
+def padded(lanes):
+    return -(-lanes // GROUP) * GROUP
+
+
 def column_sum(x):
     return jnp.sum(x, 0, keepdims=True)
 
@@ -71,6 +75,21 @@
     half = t.shape[0] // 2
     left = lax.broadcasted_iota(jnp.int32, (half, t.shape[1]), 1) < HD
     return jnp.where(left, t[:half], t[half:])
+
+
+def as_column(row):
+    n = row.shape[1]
+    same = lax.broadcasted_iota(jnp.int32, (n, n), 0) == lax.broadcasted_iota(jnp.int32, (n, n), 1)
+    return jnp.sum(jnp.where(same, jnp.broadcast_to(row, (n, n)), 0.0), -1, keepdims=True)
+
+
+def key_bias(row, chars_per):
+    n = row.shape[1]
+    lanes = n * chars_per
+    of_word = lax.broadcasted_iota(jnp.int32, (n, lanes), 1) // chars_per == lax.broadcasted_iota(jnp.int32, (n, lanes), 0)
+    counts = nn(jnp.broadcast_to(row, (8, n)).astype(BF), jnp.where(of_word, 1.0, 0.0).astype(BF))
+    place = lax.rem(lax.broadcasted_iota(jnp.int32, (8, lanes), 1), chars_per)
+    return jnp.where(place.astype(F32) < counts, 0.0, NEG)
 
 
 def pool_weights(h2, query, counts, chars_per):
@@ -78,7 +97,7 @@
     words = rows // chars_per
     e = jnp.sum(h2 * query, -1, keepdims=True) * (h2.shape[1] ** -0.5)
     e = e.reshape(words, chars_per, 1)
-    place = lax.broadcasted_iota(jnp.int32, (words, chars_per, 1), 1)
+    place = lax.broadcasted_iota(jnp.int32, (words, chars_per, 1), 1).astype(F32)
     e = jnp.where(place < counts.reshape(words, 1, 1), e, NEG)
     ex = jnp.exp(e - jnp.max(e, 1, keepdims=True))
     return ex / jnp.sum(ex, 1, keepdims=True)
@@ -207,17 +226,9 @@
         for j in range(1, net.n_dp):
             self.to_all(j).start()
 
-    def finish(self, outs):
-        net = self.net
-        for j in range(1, net.n_dp):
+    def finish(self):
+        for j in range(1, self.net.n_dp):
             self.to_all(j).wait()
-        rows = self.part.shape[1]
-        for ref, first, columns, side in outs:
-            for k in range(side):
-                for at in range(0, columns, GROUP):
-                    column = first + k * columns + at
-                    q, lane = column // self.span, column % self.span
-                    ref[k * rows : (k + 1) * rows, at : at + GROUP] = self.done[q, :, lane : lane + GROUP].astype(F32)
 
 
 class ReduceRows:
@@ -269,18 +280,20 @@
         for j in range(1, net.n_z):
             self.to_z(j).start()
 
-    def finish(self, outs):
+    def finish(self, out, places):
         net = self.net
         for j in range(1, net.n_z):
             self.to_z(j).wait()
         total = self.of_z[0]
         for z in range(1, net.n_z):
             total = total + self.of_z[z]
-        for ref, first, length in outs:
-            piece = ref.shape[1]
+        at = 0
+        for first, length in places:
+            piece = length // net.n_wide
             vector = jnp.broadcast_to(total[:, first : first + length], (8, length))
             turned = pltpu.roll(vector, lax.rem(length - net.wide * piece, length), 1)
-            ref[...] = turned[:1, :piece]
+            out[:, at : at + piece] = turned[:1, :piece]
+            at += padded(piece)
 
 
 class Gather:
@@ -500,7 +513,7 @@
     return slices_of(row, row.shape[1] - 5 * width - ff, [width] * 5 + [ff])
 
 
-def char_back_kernel(chars_per, steps, net_sizes, *refs):
+def char_back_kernel(chars_per, steps, net_sizes, word_sizes, *refs):
     (
         gx_ref, c_ref, cnt_ref, qkv_ref, p_ref, o_ref, h1_ref, h2_ref, m_ref, s_ref, pooled_all, gx_all,
         win, wout, wup, wdn, wpj, vec, *refs
@@ -509,19 +522,18 @@
         word_grads, word_row, *refs = refs
     gc_ref, *refs = refs
     if net_sizes:
-        outs, refs = refs[:23], refs[23:]
-        accs, refs = refs[:13], refs[13:]
-    else:
-        accs, refs = refs[:13], refs[13:]
+        outs, refs = refs[:4], refs[4:]
+    accs, refs = refs[:13], refs[13:]
     dga, dsa, dwin, dwout, dgb, dsb, dwup, dub, dwdn, ddb, dqv, dwpj, dpb = accs
-    gh1_ref, gm_ref, u_ref, gz_ref, gq_ref, *refs = refs
+    gh1_ref, gm_ref, u_ref, gz_ref, gq_ref, gs_ref, *refs = refs
     rows, width = c_ref.shape
     ga, sa, gb, sb, _, qv, _, _ = char_vectors(vec, width, wup.shape[1], wpj.shape[1])
     phase, step = pl.program_id(0), pl.program_id(1)
     now = phase * steps + step
     factor = width**-0.5
-    chunk = min(rows, 256)
+    chunk = min(rows, 512)
     cw = chunk // chars_per
+    words = rows // chars_per
 
     if net_sizes:
         net = Net(*net_sizes)
@@ -530,6 +542,7 @@
         ff = Reduce(net, ff_grads, *refs[8:14], refs[14:16])
         att = Reduce(net, at_grads, *refs[16:22], refs[22:24])
         rowsum = ReduceRows(net, row, *refs[24:27], refs[27:29])
+        keep = refs[29]
 
         @pl.when(now == 0)
         def _():
@@ -562,11 +575,12 @@
     @pl.when(phase == 0)
     def _():
         gp = nt(gx_ref[...], wpj[...]).astype(BF).astype(F32)
+        counts = as_column(cnt_ref[pl.ds(step, 1), :].astype(F32))
         for t in range(rows // chunk):
             at = slice(t * chunk, (t + 1) * chunk)
             wat = slice(t * cw, (t + 1) * cw)
-            h2 = h2_ref[at, :]
-            om = pool_weights(h2, qv[...], cnt_ref[wat, :], chars_per)
+            h2 = h2_ref[at, :].astype(F32)
+            om = pool_weights(h2, qv[...], counts[wat, :], chars_per)
             gpb = jnp.broadcast_to(gp[wat, :].reshape(cw, 1, width), (cw, chars_per, width)).reshape(chunk, width)
             w = jnp.sum(h2 * gpb, -1, keepdims=True).reshape(cw, chars_per, 1)
             de = om * (w - jnp.sum(om * w, 1, keepdims=True))
@@ -580,11 +594,11 @@
             gz_ref[at, :] = gz
             dub[...] += column_sum(gz.astype(F32))
             du = nt(gz, wup[...])
-            n, r = normal_of(h1_ref[at, :])
+            n, r = normal_of(h1_ref[at, :].astype(F32))
             dgb[...] += column_sum(du * n)
             dsb[...] += column_sum(du)
             u_ref[at, :] = (n * gb[...] + sb[...]).astype(BF)
-            gh1_ref[pl.ds(pl.multiple_of(step * rows + t * chunk, chunk), chunk), :] = gh2 + norm_back(du, n, r, gb[...])
+            gh1_ref[pl.ds(pl.multiple_of(step * rows + t * chunk, chunk), chunk), :] = (gh2 + norm_back(du, n, r, gb[...])).astype(BF)
         dwup[...] += tn(u_ref[...], gz_ref[...])
         dwdn[...] += tn(gm_ref[...], m_ref[...])
 
@@ -608,22 +622,26 @@
 
     @pl.when(phase == 1)
     def _():
-        g1 = gh1_ref[here, :].astype(BF)
+        g1 = gh1_ref[here, :]
         dwout[...] += tn(o_ref[...], g1)
         gm_ref[...] = nt(g1, wout[...]).astype(BF)
-        for g in range(rows // GROUP):
-            at = slice(g * GROUP, (g + 1) * GROUP)
-            for p in range(width // GROUP):
-                q = qkv_ref[at, p * GROUP : (p + 1) * GROUP]
-                k = qkv_ref[at, width + p * GROUP : width + (p + 1) * GROUP]
-                v = qkv_ref[at, 2 * width + p * GROUP : 2 * width + (p + 1) * GROUP]
-                soft = p_ref[at, p * 2 * GROUP : (p + 1) * 2 * GROUP]
-                gm = gm_ref[at, p * GROUP : (p + 1) * GROUP]
-                dp = nt(gm, two_heads(v))
-                gs = jnp.concatenate([softmax_back(soft[:, h * GROUP : (h + 1) * GROUP], dp[:, h * GROUP : (h + 1) * GROUP]) for h in range(2)], 1)
-                gq_ref[at, p * GROUP : (p + 1) * GROUP] = (nn(gs, two_heads(k)) * HD**-0.5).astype(BF)
-                gq_ref[at, width + p * GROUP : width + (p + 1) * GROUP] = one_of_two(tn(gs, q)).astype(BF)
-                gq_ref[at, 2 * width + p * GROUP : 2 * width + (p + 1) * GROUP] = one_of_two(tn(soft, gm)).astype(BF)
+        units = [(slice(g * GROUP, (g + 1) * GROUP), p) for g in range(rows // GROUP) for p in range(width // GROUP)]
+
+        def head_pair(at, p, i):
+            return qkv_ref[at, i * width + p * GROUP : i * width + (p + 1) * GROUP]
+
+        for at, p in units:
+            dp = nt(gm_ref[at, p * GROUP : (p + 1) * GROUP], two_heads(head_pair(at, p, 2)))
+            for h in range(2):
+                lanes = slice((2 * p + h) * GROUP, (2 * p + h + 1) * GROUP)
+                gs_ref[at, lanes] = softmax_back(p_ref[at, lanes], dp[:, h * GROUP : (h + 1) * GROUP])
+        for at, p in units:
+            gs = gs_ref[at, 2 * p * GROUP : 2 * (p + 1) * GROUP]
+            gq_ref[at, p * GROUP : (p + 1) * GROUP] = (nn(gs, two_heads(head_pair(at, p, 1))) * HD**-0.5).astype(BF)
+            gq_ref[at, width + p * GROUP : width + (p + 1) * GROUP] = one_of_two(tn(gs, head_pair(at, p, 0))).astype(BF)
+            soft = p_ref[at, p * 2 * GROUP : (p + 1) * 2 * GROUP]
+            gm = gm_ref[at, p * GROUP : (p + 1) * GROUP]
+            gq_ref[at, 2 * width + p * GROUP : 2 * width + (p + 1) * GROUP] = one_of_two(tn(soft, gm)).astype(BF)
         for t in range(rows // chunk):
             at = slice(t * chunk, (t + 1) * chunk)
             n, r = normal_of(c_ref[at, :].astype(F32))
@@ -631,7 +649,8 @@
             da = nt(gq_ref[at, :], win[...])
             dga[...] += column_sum(da * n)
             dsa[...] += column_sum(da)
-            gc_ref[at, :] = gh1_ref[pl.ds(pl.multiple_of(step * rows + t * chunk, chunk), chunk), :] + norm_back(da, n, r, ga[...])
+            grad = gh1_ref[pl.ds(pl.multiple_of(step * rows + t * chunk, chunk), chunk), :].astype(F32) + norm_back(da, n, r, ga[...])
+            gc_ref[at, :] = grad.astype(gc_ref.dtype)
         dwin[...] += tn(u_ref[...], gq_ref[...])
 
     if net_sizes:
@@ -650,40 +669,33 @@
                 places.append((column, acc.shape[1]))
                 column += acc.shape[1]
             row[:, column:] = word_row[...]
-            (
-                oga, osa, owin, owout, ogb, osb, oup, oub, odn, odb, oqv, opj, opb,
-                xga, xsa, xwin, xwout, xgb, xsb, xup, xub, xdn, xdb,
-            ) = outs
-            for ref in (xga, xsa, xgb, xsb, xdb, xub):
-                length = ref.shape[1] * n_wide
-                places.append((column, length))
-                column += length
+            for ref in word_vectors(row, *word_sizes):
+                places.append((column, ref.shape[1]))
+                column += ref.shape[1]
             att.start()
             rowsum.start()
-            word.finish(columns_of((xwin, xwout, xup), xdn))
-            ff.finish(columns_of((oup, opj), odn))
+            word.finish()
+            ff.finish()
             att.over_dp()
             rowsum.over_dp()
             att.over_z()
             rowsum.over_z()
             att.back_over_dp()
-            ordered = (oga, osa, ogb, osb, odb, oqv, oub, opb, xga, xsa, xgb, xsb, xdb, xub)
-            rowsum.finish([(ref, *place) for ref, place in zip(ordered, places)])
-            att.finish(columns_of((owin, owout), None))
-
-
-def columns_of(across, down):
-    outs, column = [], 0
-    for ref in across:
-        outs.append((ref, column, ref.shape[1], 1))
-        column += ref.shape[1]
-    if down is not None:
-        outs.append((down, column, down.shape[1], down.shape[0] // across[0].shape[0]))
-    return outs
+            rowsum.finish(outs[3], places)
+            att.finish()
+            copies = [pltpu.make_async_copy(piece.done, out, keep.at[i]) for i, (piece, out) in enumerate(zip((word, ff, att), outs))]
+            for copy in copies:
+                copy.start()
+            for copy in copies:
+                copy.wait()
 
 
 def whole_block(shape):
-    return pl.BlockSpec(shape, lambda p, i: (0,) * len(shape))
+    return pl.BlockSpec(shape, lambda *_: (0,) * len(shape), pipeline_mode=pl.Buffered(1))
+
+
+def whole_out(shape):
+    return pl.BlockSpec(shape, lambda *_: (0,) * len(shape))
 
 
 def char_backward(gx, chars, counts, saved, weights, chars_per, rows, net_sizes=None, word_grads=None, word_row=None):
@@ -702,13 +714,12 @@
 
     accs = [(1, width), (1, width), (width, 3 * width), (width, width), (1, width), (1, width), (width, ff), (1, ff),
             (width, ff), (1, width), (1, width), (width, out), (1, out)]
-    in_specs = [early(cw, out), late(rows, width), early(cw, 1), late(rows, 3 * width), late(rows, 2 * width),
+    in_specs = [early(cw, out), late(rows, width), whole_block(counts.shape), late(rows, 3 * width), late(rows, 2 * width),
                 late(rows, width), early(rows, width), early(rows, width), early(rows, ff), early(rows, ff),
                 whole_block(pooled.shape), whole_block(gx.shape)] + [whole_block(w.shape) for w in weights]
     operands = [gx, chars, counts, qkv, soft, mixed, h1, h2, m, s, pooled, gx, *weights]
-    scratch = [pltpu.VMEM((total, width), F32), pltpu.VMEM((rows, width), BF), pltpu.VMEM((rows, width), BF),
-               pltpu.VMEM((rows, ff), BF), pltpu.VMEM((rows, 3 * width), BF)]
-    out_shapes = [(total, width)]
+    scratch = [pltpu.VMEM((total, width), BF), pltpu.VMEM((rows, width), BF), pltpu.VMEM((rows, width), BF),
+               pltpu.VMEM((rows, ff), BF), pltpu.VMEM((rows, 3 * width), BF), pltpu.VMEM((rows, 2 * width), BF)]
     if net_sizes:
         n_dp, n_wide = net_sizes
         n_z, some = n_wide // 2, width // n_wide
@@ -717,12 +728,13 @@
         word_ff = word_row.shape[1] - 5 * wide_d
         operands += [word_grads, word_row]
         in_specs += [pl.BlockSpec(memory_space=pl.ANY), whole_block(word_row.shape)]
-        part = lambda a: (1, a[1] // n_wide) if a[0] == 1 else (a[0] // n_wide, a[1])
-        words_accs = [(1, wide_d), (1, wide_d), (wide_d, 3 * wide_d), (wide_d, wide_d), (1, wide_d), (1, wide_d), (wide_d, word_ff),
-                      (1, word_ff), (word_ff, wide_d), (1, wide_d)]
-        out_shapes += [part(a) for a in accs[:8] + [(ff, width)] + accs[9:] + words_accs]
         ff_width, at_width = ff + out + ff, 4 * width
         row_width = 6 * width + ff + out + word_row.shape[1]
+        word_sizes = (wide_d, word_ff)
+        sums = [(n_dp, word_rows, word_width // n_dp), (n_dp, some, ff_width // n_dp), (n_dp, some, at_width // n_dp)]
+        pieces = sum(padded(n // n_wide) for n in [width] * 6 + [ff, out] + [wide_d] * 5 + [word_ff])
+        out_shapes = [jax.ShapeDtypeStruct((total, width), BF)] + [jax.ShapeDtypeStruct(a, BF) for a in sums] + [jax.ShapeDtypeStruct((1, pieces), F32)]
+        out_specs = [late(rows, width)] + [pl.BlockSpec(memory_space=pl.ANY)] * 3 + [whole_out((1, pieces))]
         scratch = (
             [pltpu.VMEM(a, F32) for a in accs]
             + scratch
@@ -731,28 +743,79 @@
             + Reduce.scratch(n_dp, n_z, some, ff_width)
             + Reduce.scratch(n_dp, n_z, some, at_width)
             + ReduceRows.scratch(n_dp, n_z, row_width)[1:]
+            + [pltpu.SemaphoreType.DMA((3,))]
         )
         params = pltpu.CompilerParams(vmem_limit_bytes=VMEM_LIMIT, collective_id=3, has_side_effects=True)
     else:
-        out_shapes += accs
+        word_sizes = None
+        out_shapes = [jax.ShapeDtypeStruct(a, F32) for a in [(total, width)] + accs]
+        out_specs = [late(rows, width)] + [whole_out(a) for a in accs]
         params = pltpu.CompilerParams(vmem_limit_bytes=VMEM_LIMIT)
     return pl.pallas_call(
-        functools.partial(char_back_kernel, chars_per, steps, net_sizes),
+        functools.partial(char_back_kernel, chars_per, steps, net_sizes, word_sizes),
         grid=(2, steps),
         in_specs=in_specs,
-        out_specs=[late(rows, width)] + [whole_block(a) for a in out_shapes[1:]],
-        out_shape=[jax.ShapeDtypeStruct(a, F32) for a in out_shapes],
+        out_specs=out_specs,
+        out_shape=out_shapes,
         scratch_shapes=scratch,
         compiler_params=params,
         name="char_backward",
     )(*operands)
 
 
+def unpack(done, outs):
+    rows, span = done.shape[1:]
+    for ref, first, columns, side in outs:
+        for k in range(side):
+            for at in range(0, columns, GROUP):
+                column = first + k * columns + at
+                q, lane = column // span, column % span
+                ref[k * rows : (k + 1) * rows, at : at + GROUP] = done[q, :, lane : lane + GROUP].astype(F32)
+
+
+def output_kernel(gc_low, word_done, ff_done, at_done, row, gc_ref, *outs):
+    gc_ref[...] = gc_low[...].astype(F32)
+
+    @pl.when(pl.program_id(0) == 0)
+    def _():
+        (
+            oga, osa, owin, owout, ogb, osb, oup, oub, odn, odb, oqv, opj, opb,
+            xga, xsa, xwin, xwout, xgb, xsb, xup, xub, xdn, xdb,
+        ) = outs
+        for done, across, down in ((word_done, (xwin, xwout, xup), xdn), (ff_done, (oup, opj), odn), (at_done, (owin, owout), None)):
+            places, column = [], 0
+            for ref in across:
+                places.append((ref, column, ref.shape[1], 1))
+                column += ref.shape[1]
+            if down is not None:
+                places.append((down, column, down.shape[1], down.shape[0] // done.shape[1]))
+            unpack(done, places)
+        at = 0
+        for ref in (oga, osa, ogb, osb, odb, oqv, oub, opb, xga, xsa, xgb, xsb, xdb, xub):
+            ref[...] = row[:, at : at + ref.shape[1]]
+            at += padded(ref.shape[1])
+
+
+def outputs_of(gc_low, word_done, ff_done, at_done, row, shapes, rows):
+    total, width = gc_low.shape
+    by_row = pl.BlockSpec((rows, width), lambda i: (i, 0))
+    wholes = [word_done, ff_done, at_done, row]
+    return pl.pallas_call(
+        output_kernel,
+        grid=(total // rows,),
+        in_specs=[by_row] + [whole_block(a.shape) for a in wholes],
+        out_specs=[by_row] + [whole_out(a) for a in shapes],
+        out_shape=[jax.ShapeDtypeStruct(a, F32) for a in [(total, width), *shapes]],
+        compiler_params=pltpu.CompilerParams(vmem_limit_bytes=VMEM_LIMIT),
+        name="outputs",
+    )(gc_low, *wholes)
+
+
 def char_forward_kernel(chars_per, steps, net_sizes, lengths, *refs):
-    c_ref, bias_ref, cnt_ref, *refs = refs
+    c_ref, cnt_ref, *refs = refs
     if net_sizes:
         net = Net(*net_sizes)
-        shards, word_shards, refs = refs[:6], refs[6:10], refs[10:]
+        shards, word_shards, vectors, refs = refs[:5], refs[5:9], refs[9:23], refs[23:]
         inbox, vec, *refs = refs
         char_out, word_out, refs = refs[:5], refs[5:9], refs[9:]
     else:
@@ -763,12 +826,13 @@
     rows, width = c_ref.shape
     phase, step = pl.program_id(0), pl.program_id(1)
     now = phase * steps + step
-    chunk = min(rows, 256)
+    chunk = min(rows, 512)
     cw = chunk // chars_per
-
-    if net_sizes:
-        x_out, win, wout, wup, wdn, wpj, pieces, *refs = refs
-        gather = Gather(net, shards, [win, wout, wup, wdn, wpj, pieces], *refs[:3])
+    words = rows // chars_per
+
+    if net_sizes:
+        x_out, win, wout, wup, wdn, wpj, pieces, piece, *refs = refs
+        gather = Gather(net, (*shards, piece), [win, wout, wup, wdn, wpj, pieces], *refs[:3])
         shared = SharedGather(net, word_shards, word_out, *refs[3:10])
         exchange = Exchange(net, x_out, inbox, *refs[10:13])
         keep = refs[13]
@@ -779,6 +843,9 @@
             peers = [net.wide_peer(j)[1] for j in range(1, net.n_wide)] + [net.dp_peer(j)[1] for j in range(1, net.n_dp)]
             net.greet(peers)
             net.met(peers)
+            for ref, (at, length) in zip(vectors, lengths):
+                some = length // net.n_wide
+                piece[0, :, at : at + some] = ref[...].astype(F32).reshape(1, some)
             for a in first + later:
                 gather.start(a)
             for a in first:
@@ -830,25 +897,28 @@
         ri = lax.broadcasted_iota(jnp.int32, (GROUP, GROUP), 0) // chars_per
         ci = lax.broadcasted_iota(jnp.int32, (GROUP, GROUP), 1) // chars_per
         same = ri == ci
-        for g in range(rows // GROUP):
-            at = slice(g * GROUP, (g + 1) * GROUP)
-            bias = jnp.where(same, jnp.broadcast_to(bias_ref[0, g : g + 1, :], (GROUP, GROUP)), NEG)
-            for p in range(width // GROUP):
-                q = qkv_ref[at, p * GROUP : (p + 1) * GROUP]
-                k = qkv_ref[at, width + p * GROUP : width + (p + 1) * GROUP]
-                v = qkv_ref[at, 2 * width + p * GROUP : 2 * width + (p + 1) * GROUP]
-                s = nt(q, two_heads(k))
-                soft = jnp.concatenate([softmax_low(s[:, h * GROUP : (h + 1) * GROUP] + bias) for h in range(2)], 1)
-                p_ref[at, p * 2 * GROUP : (p + 1) * 2 * GROUP] = soft
-                o_ref[at, p * GROUP : (p + 1) * GROUP] = nn(soft, two_heads(v)).astype(BF)
+        units = [(g, slice(g * GROUP, (g + 1) * GROUP), p) for g in range(rows // GROUP) for p in range(width // GROUP)]
+
+        def head_pair(at, p, i):
+            return qkv_ref[at, i * width + p * GROUP : i * width + (p + 1) * GROUP]
+
+        valid = key_bias(cnt_ref[pl.ds(step, 1), :].astype(F32), chars_per)
+        for g, at, p in units:
+            bias = jnp.where(same, jnp.broadcast_to(valid[:1, g * GROUP : (g + 1) * GROUP], (GROUP, GROUP)), NEG)
+            s = nt(head_pair(at, p, 0), two_heads(head_pair(at, p, 1)))
+            for h in range(2):
+                p_ref[at, (2 * p + h) * GROUP : (2 * p + h + 1) * GROUP] = softmax_low(s[:, h * GROUP : (h + 1) * GROUP] + bias)
+        for _, at, p in units:
+            o_ref[at, p * GROUP : (p + 1) * GROUP] = nn(p_ref[at, 2 * p * GROUP : 2 * (p + 1) * GROUP], two_heads(head_pair(at, p, 2))).astype(BF)
         for t in range(rows // chunk):
             at = slice(t * chunk, (t + 1) * chunk)
             h1 = c_ref[at, :].astype(F32) + nn(o_ref[at, :], wout[...])
-            h1_ref[at, :] = h1
+            h1_ref[at, :] = h1.astype(BF)
             h1_all[block(t), :] = h1
 
     @pl.when(phase == 1)
     def _():
+        counts = as_column(cnt_ref[pl.ds(step, 1), :].astype(F32))
         for t in range(rows // chunk):
             at = slice(t * chunk, (t + 1) * chunk)
             wat = slice(t * cw, (t + 1) * cw)
@@ -859,13 +929,12 @@
             m_ref[at, :] = m.astype(BF)
             s_ref[at, :] = s.astype(BF)
             h2 = h1 + (nn(m_ref[at, :], wdn[...]) + db[...])
-            h2_ref[at, :] = h2
-            om = pool_weights(h2, qv[...], cnt_ref[wat, :], chars_per)
+            h2_ref[at, :] = h2.astype(BF)
+            om = pool_weights(h2, qv[...], counts[wat, :], chars_per)
             pooled_ref[wat, :] = jnp.sum(om * h2.reshape(cw, chars_per, width), 1).astype(BF)
         x = (nn(pooled_ref[...], wpj[...]) + pb[...]).astype(BF)
         if net_sizes:
             cap = x_out.shape[1]
-            words = rows // chars_per
             first_word = step * words
             target = first_word // cap
             x_out[target, pl.ds(pl.multiple_of(lax.rem(first_word, cap), words), words)] = x
@@ -884,7 +953,7 @@
                 pltpu.make_async_copy(gather.wholes[a], char_out[a], keep.at[a]).wait()
 
 
-def char_forward(chars, key_bias, counts, weights, chars_per, rows, net_sizes=None, word_shards=None, lengths=None, cap=None):
+def char_forward(chars, counts, weights, chars_per, rows, net_sizes=None, word_shards=None, vectors=None, cap=None):
     total, width = chars.shape
     words, cw = total // chars_per, rows // chars_per
     ff, out = weights[2].shape[1], weights[4].shape[1]
@@ -897,30 +966,32 @@
         return pl.BlockSpec((count, columns), lambda p, i: (i * p, 0))
 
     saved = [((words, width), BF, cw, late), ((total, 3 * width), BF, rows, early), ((total, 2 * width), BF, rows, early),
-             ((total, width), BF, rows, early), ((total, width), F32, rows, early), ((total, width), F32, rows, late),
+             ((total, width), BF, rows, early), ((total, width), BF, rows, early), ((total, width), BF, rows, late),
              ((total, ff), BF, rows, late), ((total, ff), BF, rows, late)]
     saved_specs = [where(count, s[1]) for s, _, count, where in saved]
     saved_shapes = [jax.ShapeDtypeStruct(s, d) for s, d, _, _ in saved]
-    groups = rows // GROUP
-    bias_spec = pl.BlockSpec((1, groups, GROUP), lambda p, i: (i + p * (steps - 1 - i), 0, 0))
-    in_specs = [early(rows, width), bias_spec, late(cw, 1)]
-    operands = [chars, key_bias.reshape(steps, groups, GROUP), counts]
+    in_specs = [early(rows, width), whole_block(counts.shape)]
+    operands = [chars, counts]
     scratch = [pltpu.VMEM((total, width), F32)]
     anywhere = pl.BlockSpec(memory_space=pl.ANY)
     if net_sizes:
         n_dp, n_wide = net_sizes
         n_z = n_wide // 2
-        in_specs += [anywhere] * 10
-        operands += [*weights, *word_shards]
+        lengths, room = [], 0
+        for v in vectors:
+            lengths.append((room, v.shape[0] * n_wide))
+            room += padded(v.shape[0])
+        in_specs += [anywhere] * 9 + [whole_block(v.shape) for v in vectors]
+        operands += [*weights, *word_shards, *vectors]
         vec_shape = jax.ShapeDtypeStruct((1, sum(length for _, length in lengths)), F32)
         grown = lambda a: jax.ShapeDtypeStruct((a.shape[0] * n_wide, a.shape[1]), a.dtype)
-        fulls = [grown(a) for a in weights[:5]]
-        out_specs = [anywhere, whole_block(vec_shape.shape)] + [anywhere] * 9 + saved_specs
+        fulls = [grown(a) for a in weights]
+        out_specs = [anywhere, whole_out(vec_shape.shape)] + [anywhere] * 9 + saved_specs
         out_shapes = [jax.ShapeDtypeStruct((n_wide, cap, out), BF), vec_shape, *fulls, *(grown(a) for a in word_shards), *saved_shapes]
         scratch += (
             [pltpu.VMEM((n_wide, cap, out), BF)]
             + [pltpu.VMEM(a.shape, a.dtype) for a in fulls]
-            + [pltpu.VMEM((n_wide, *weights[5].shape[1:]), F32)]
+            + [pltpu.VMEM((n_wide, 1, room), F32), pltpu.VMEM((1, 1, room), F32)]
             + Gather.scratch(6, n_z)
             + SharedGather.scratch(4, n_dp, n_z)
             + Exchange.scratch(n_wide)
@@ -928,6 +999,7 @@
         )
         params = pltpu.CompilerParams(vmem_limit_bytes=VMEM_LIMIT, collective_id=1, has_side_effects=True)
     else:
+        lengths = None
         in_specs += [whole_block(w.shape) for w in weights]
         operands += [*weights]
         out_specs = [late(cw, out)] + saved_specs
@@ -946,7 +1018,7 @@
 
 
 def word_kernel(slot_cap, net_sizes, *refs):
-    arrived, bucket, assign, seg_row, seg_col, grad_ref, win, wout, wup, wdn, vec, out_ref, back_out, *refs = refs
+    arrived, bucket, assign, segment, grad_ref, win, wout, wup, wdn, vec, out_ref, back_out, *refs = refs
     length, width = grad_ref.shape
     ff = wup.shape[1]
     if net_sizes:
@@ -964,19 +1036,21 @@
         exchange = Exchange(net, back_ref, back_out, *sems)
         peers = [net.wide_peer(j)[1] for j in range(1, net.n_wide)]
         net.greet(peers)
-    named = jnp.where(bucket[...] == lax.broadcasted_iota(jnp.int32, (length, owners), 1), 1.0, 0.0)
+    named = jnp.where(bucket[...] == lax.broadcasted_iota(jnp.int32, (owners, length), 0), 1.0, 0.0)
     ri = lax.broadcasted_iota(jnp.int32, (length, length), 0)
     ci = lax.broadcasted_iota(jnp.int32, (length, length), 1)
-    earlier = nn(jnp.where(ci < ri, 1.0, 0.0).astype(BF), named.astype(BF))
-    slot = jnp.sum(named * (assign[...].astype(F32) * slot_cap + earlier), -1, keepdims=True).astype(jnp.int32)
-    hot = jnp.where(lax.broadcasted_iota(jnp.int32, (length, slots), 1) == slot, 1.0, 0.0).astype(BF)
-    x = nn(hot, arrived[...].reshape(slots, width))
+    earlier = nn(named.astype(BF), jnp.where(ri < ci, 1.0, 0.0).astype(BF))
+    served = as_column(assign[...].astype(F32)) * slot_cap
+    slot = jnp.sum(named * (served + earlier), 0, keepdims=True).astype(jnp.int32)
+    hot = jnp.where(lax.broadcasted_iota(jnp.int32, (slots, length), 0) == slot, 1.0, 0.0).astype(BF)
+    x = tn(hot, arrived[...].reshape(slots, width))
     n1, r1 = normal_of(x)
     a = (n1 * ga[...] + sa[...]).astype(BF)
     qkv = nn(a, win[...])
     qkv_ref[:, :width] = (qkv[:, :width] * HD**-0.5).astype(BF)
     qkv_ref[:, width:] = qkv[:, width:].astype(BF)
-    bias = jnp.where((seg_row[...] == seg_col[...]) & (ci <= ri), 0.0, NEG)
+    seg = segment[...].astype(F32)
+    bias = jnp.where((seg == as_column(seg)) & (ci <= ri), 0.0, NEG)
 
     def pair(p):
         return [qkv_ref[:, i * width + p * GROUP : i * width + (p + 1) * GROUP] for i in range(3)]
@@ -1011,7 +1085,7 @@
         gq_ref[:, 2 * width + p * GROUP : 2 * width + (p + 1) * GROUP] = one_of_two(tn(soft, gmp)).astype(BF)
     da = nt(gq_ref[...], win[...])
     gx = (g1 + norm_back(da, n1, r1, ga[...])).astype(BF)
-    back = tn(hot, gx).astype(BF).reshape(owners, slot_cap, width)
+    back = nn(hot, gx).astype(BF).reshape(owners, slot_cap, width)
     if net_sizes:
         back_ref[...] = back
         net.met(peers)
@@ -1072,13 +1146,13 @@
         params = pltpu.CompilerParams(vmem_limit_bytes=VMEM_LIMIT)
     return pl.pallas_call(
         functools.partial(word_kernel, slot_cap, net_sizes),
-        in_specs=[vmem] * 11,
+        in_specs=[vmem] * 10,
         out_specs=out_specs,
         out_shape=out_shapes,
         scratch_shapes=scratch,
         compiler_params=params,
         name="word_block",
-    )(arrived, bucket, assign, segments, segments.reshape(length, 1), grad, *weights)
+    )(arrived, bucket, assign, segments, grad, *weights)
 
 
 def gathered(shard):
@@ -1105,14 +1179,12 @@
     cap, chars_per, width = chars.shape[2:]
     slots = n_wide * cap
     rows = chars.reshape(slots * chars_per, width)
-    counts = char_counts.reshape(slots, 1)
-    key_bias = jnp.where(lax.broadcasted_iota(jnp.int32, (slots, chars_per), 1) < counts, 0.0, NEG)
-    block = min(512, rows.shape[0])
+    block = min(1024, rows.shape[0])
+    counts = char_counts.reshape(-1, block // chars_per)
     char_shards = (char_inproj, char_outproj, char_up, char_down, char_proj)
     word_shards = (word_inproj, word_outproj, word_up, word_down)
     vectors = (char_gain, char_shift, char_gain_mid, char_shift_mid, char_down_bias, pool_query, char_up_bias, char_proj_bias,
                word_gain, word_shift, word_gain_mid, word_shift_mid, word_down_bias, word_up_bias)
-    matrices = char_shards + word_shards
     fast = (
         all(m.shape[0] % 16 == 0 for m in char_shards)
         and all(m.shape[0] % (16 * n_dp) == 0 for m in word_shards)
@@ -1120,29 +1192,26 @@
         and (4 * width) % (GROUP * n_dp) == 0
         and n_wide % 2 == 0
     )
-    bucket, names, seg, upstream = buckets[0], assign[None], segments, out_grad[0]
+    bucket, names, upstream = buckets.reshape(1, -1), assign[None], out_grad[0]
     if fast:
         sizes = (n_dp, n_wide)
-        padded, lengths, at = [], [], 0
-        for v in vectors:
-            room = -(-v.shape[0] // GROUP) * GROUP
-            padded.append(jnp.pad(v.astype(F32), (0, room - v.shape[0])))
-            lengths.append((at, v.shape[0] * n_wide))
-            at += room
-        pieces = jnp.concatenate(padded).reshape(1, 1, at)
-        arrived, vec, *rest = char_forward(rows, key_bias, counts, (*char_shards, pieces), chars_per, block, sizes, word_shards, tuple(lengths), cap)
+        arrived, vec, *rest = char_forward(rows, counts, char_shards, chars_per, block, sizes, word_shards, vectors, cap)
         char_full, word_full, saved = rest[:5], rest[5:9], rest[9:]
-        result, returned, word_grads, word_row = word_block(arrived, bucket, names, seg, upstream, (*word_full, vec), cap, sizes)
+        result, returned, word_grads, word_row = word_block(arrived, bucket, names, segments, upstream, (*word_full, vec), cap, sizes)
         incoming = returned.reshape(slots, -1)
-        outs = char_backward(incoming, rows, counts, saved, (*char_full, vec), chars_per, block, sizes, word_grads, word_row)
-        char_grads, *grads = outs
+        sums = char_backward(incoming, rows, counts, saved, (*char_full, vec), chars_per, block, sizes, word_grads, word_row)
+        params = (char_gain, char_shift, char_inproj, char_outproj, char_gain_mid, char_shift_mid, char_up, char_up_bias, char_down,
+                  char_down_bias, pool_query, char_proj, char_proj_bias, word_gain, word_shift, word_inproj, word_outproj, word_gain_mid,
+                  word_shift_mid, word_up, word_up_bias, word_down, word_down_bias)
+        shapes = [p.shape if p.ndim == 2 else (1, *p.shape) for p in params]
+        char_grads, *grads = outputs_of(*sums, shapes, block)
         grads = [g[0] if g.shape[0] == 1 else g for g in grads]
     else:
         vec = jnp.concatenate([gathered(v) for v in vectors]).astype(F32)[None]
         char_full, word_full = [gathered(m) for m in char_shards], [gathered(m) for m in word_shards]
-        outgoing, *saved = char_forward(rows, key_bias, counts, (*char_full, vec), chars_per, block)
+        outgoing, *saved = char_forward(rows, counts, (*char_full, vec), chars_per, block)
         arrived = exchanged(outgoing.reshape(n_wide, cap, -1))
-        result, back, *word_grads = word_block(arrived, bucket, names, seg, upstream, (*word_full, vec), cap)
+        result, back, *word_grads = word_block(arrived, bucket, names, segments, upstream, (*word_full, vec), cap)
         incoming = exchanged(back).reshape(slots, -1)
         char_grads, *grads = char_backward(incoming, rows, counts, saved, (*char_full, vec), chars_per, block)
         grads[8] = grads[8].T

time: 312 us -> 237 us (0.76)
  local copies, waits for them, and re-layouts: 40.4 us -> 0.8 us
  Pallas kernels: 270 us -> 235 us
    pallas_call x1, Pallas kernels: 148 us -> 117 us  [char_backward(): pl.pallas_call(functools.partial(char_back_kernel, chars_per, steps, net_...]
    unnamed x86 -> x3, local copies, waits for them, and re-layouts: 25.4 us -> 0.8 us
    pallas_call x1, Pallas kernels: 99.3 us -> 87.7 us  [char_forward(): pl.pallas_call(functools.partial(char_forward_kernel, chars_per, steps, n...]
    pallas_call x0 -> x1, Pallas kernels: none -> 8.6 us  [outputs_of(): pl.pallas_call(output_kernel, grid=(total // rows,), in_specs=[by_row] +...]
    pad x12 -> x0, local copies, waits for them, and re-layouts: 7.92 us -> none  [shards(): padded.append(jnp.pad(v.astype(F32), (0, room - v.shape[0])))]
    reshape x3 -> x0, local copies, waits for them, and re-layouts: 3.66 us -> none  [the longest x1 1.59 us: shards(): counts = char_counts.reshape(slots, 1)]
where the time goes in v3:
time: 237 us
  Pallas kernels  235 us (99%)
    pallas_call x1, Pallas kernels, char_backward(): pl.pallas_call(functools.partial(char_back_kernel, chars_per, steps, net_...  117 us
    pallas_call x1, Pallas kernels, char_forward(): pl.pallas_call(functools.partial(char_forward_kernel, chars_per, steps, n...  87.7 us
    pallas_call x1, Pallas kernels, word_block(): pl.pallas_call(functools.partial(word_kernel, slot_cap, net_sizes), in_sp...  22.1 us
    pallas_call x1, Pallas kernels, outputs_of(): pl.pallas_call(output_kernel, grid=(total // rows,), in_specs=[by_row] +...  8.6 us

profile of v3, /device:TPU:0, one launch (start us, length us, event | category | flops | bytes accessed | tf_op | source)
XLA Modules:
  0.0 236.8 jit_solution(9827517006025185108)
XLA Ops:
  0.7 87.7 %char_forward.1 = (bf16[8,64,512]{2,1,0:T(8,128)(2,1)}, f32[1,7680]{1,0:T(1,128)}, bf16[256,768]{1,0:T(8,128)(2,1)}, bf16[256,256]{1,0:T(8,128)(2,1)}, bf16[256,...) custom-call(bf16[8192,256]{1,0:T(8,128)(2,1)} %bitcast.22, ...), custom_call_target="tpu_custom_call" | custom-call | tf_op jit(solution)/shard_map/char_forward/pallas_call | solution.py:1008
  88.4 22.1 %word_block.1 = (f32[256,512]{1,0:T(8,128)}, bf16[8,64,512]{2,1,0:T(8,128)(2,1)}, bf16[4,2,64,6144]{3,2,1,0:T(8,128)(2,1)}, f32[1,4608]{1,0:T(1,128)}) custom-call(bf16[8,64,512]{2,1,0:T(8,128)(2,1)} %get-tuple-element.77.refs_0_, s32[1,256]{1,0:T(1,128)} %bitcast.30, s32[1,8]{1,0:T(1,128)} %bitcast.31, s32[1,256]{1,0:T(1,128)} %refs_3_.3, ...), custom_call_target="tpu_custom_call" | custom-call | tf_op jit(solution)/shard_map/word_block/pallas_call | solution.py:1147
  110.5 116.8 %char_backward.1 = (bf16[8192,256]{1,0:T(8,128)(2,1)}, bf16[4,64,1536]{2,1,0:T(8,128)(2,1)}, bf16[4,32,640]{2,1,0:T(8,128)(2,1)}, bf16[4,32,256]{2,1,0:T(8,128)(2,1)}, f32[1,1920]{1,0:T(1,128)}) custom-call(bf16[512,512]{1,0:T(8,128)(2,1)} %bitcast.24, bf16[8192,256]{1,0:T(8,128)(2,1)} %bitcast.23, s32[8,64]{1,0:T(8,128)} %bitcast.29, ...), custom_call_target="tpu_custom_call" | custom-call | tf_op jit(solution)/shard_map/char_backward/pallas_call | solution.py:754
  227.4 0.0 copy-start
  227.4 8.6 %outputs.1 = (f32[8192,256]{1,0:T(8,128)}, f32[1,32]{1,0:T(1,128)}, f32[1,32]{1,0:T(1,128)}, f32[32,768]{1,0:T(8,128)}, f32[32,256]{1,0:T(8,128)}, /*index=5*/f3...) custom-call(bf16[8192,256]{1,0:T(8,128)(2,1)} %get-tuple-element.100, ...), custom_call_target="tpu_custom_call" | custom-call | tf_op jit(solution)/shard_map/outputs/pallas_call | solution.py:803
  236.0 0.0 copy-done
  236.0 0.8 copy.55
Async XLA Ops:
  227.4 8.6 %copy-start = (f32[256,512]{1,0:T(8,128)S(1)}, f32[256,512]{1,0:T(8,128)}, u32[]{:S(2)}) copy-start(f32[256,512]{1,0:T(8,128)} %get-tuple-element.83) | copy-start | bytes 1572868

commit v4 on v3

--- a/solution.py
+++ b/solution.py
@@ -17,6 +17,7 @@
 BF = jnp.bfloat16
 MESH = pl.DeviceIdType.MESH
 VMEM_LIMIT = 60 << 20
+WORD_PARTS = 3
 
 
 def nn(a, b):
@@ -136,8 +137,9 @@
 
 
 class Reduce:
-    def __init__(self, net, grads, kept, from_core, part, from_dp, from_z, done, sems):
+    def __init__(self, net, grads, first, kept, from_core, part, from_dp, from_z, done, sems):
         self.net, self.grads = net, grads
+        self.columns = pl.ds(first, kept.shape[-1])
         self.kept, self.from_core, self.part = kept, from_core, part
         self.from_dp, self.from_z, self.done = from_dp, from_z, done
         self.send, self.recv = sems
@@ -163,10 +165,10 @@
 
     def to_core(self):
         net = self.net
-        return remote(self.grads.at[:, 1 - net.core], self.from_core, self.send.at[0], self.recv.at[0], net.sibling)
+        return remote(self.grads.at[:, 1 - net.core, :, self.columns], self.from_core, self.send.at[0], self.recv.at[0], net.sibling)
 
     def own(self):
-        return pltpu.make_async_copy(self.grads.at[:, self.net.core], self.kept, self.recv.at[1])
+        return pltpu.make_async_copy(self.grads.at[:, self.net.core, :, self.columns], self.kept, self.recv.at[1])
 
     def to_dp(self, j):
         q, peer = self.net.dp_peer(j)
@@ -229,6 +231,86 @@
     def finish(self):
         for j in range(1, self.net.n_dp):
             self.to_all(j).wait()
+
+
+class TwoWayReduce(Reduce):
+    @staticmethod
+    def scratch(n_dp, n_z, rows, width):
+        count = 2 + 2 * n_dp + n_z
+        return [
+            pltpu.VMEM((n_z, rows, width), BF),
+            pltpu.VMEM((n_z, rows, width), BF),
+            pltpu.VMEM((n_z, rows, width // n_dp), BF),
+            pltpu.VMEM((2, n_z, rows, width // 4), BF),
+            pltpu.VMEM((2, n_z, rows, width // 8), BF),
+            pltpu.VMEM((n_z - 1, rows, width // n_dp), BF),
+            pltpu.VMEM((n_dp, rows, width // n_dp), BF),
+            pltpu.SemaphoreType.DMA((count,)),
+            pltpu.SemaphoreType.DMA((count,)),
+        ]
+
+    def __init__(self, net, grads, first, kept, from_core, part, half, quarter, from_z, done, sems):
+        super().__init__(net, grads, first, kept, from_core, part, None, from_z, done, sems)
+        self.half, self.quarter = half, quarter
+        x, y = lax.rem(net.dp, 2), net.dp // 2
+        along_x, along_y = (net.dp + 1 - 2 * x, net.wide), (lax.rem(net.dp + 2, 4), net.wide)
+        self.order = ((x, y, along_x, along_y), (y, x, along_y, along_x))
+
+    def window(self, h, a, b=None):
+        eighth = self.span // 2
+        at = h * 4 * eighth + a * 2 * eighth
+        if b is None:
+            return pl.ds(pl.multiple_of(at, GROUP), 2 * eighth)
+        return pl.ds(pl.multiple_of(at + b * eighth, GROUP), eighth)
+
+    def first_step(self, h):
+        a, _, peer, _ = self.order[h]
+        return remote(self.kept.at[:, :, self.window(h, 1 - a)], self.half.at[h], self.send.at[2 + h], self.recv.at[2 + h], peer)
+
+    def second_step(self, h):
+        a, b, _, peer = self.order[h]
+        return remote(self.kept.at[:, :, self.window(h, a, 1 - b)], self.quarter.at[h], self.send.at[4 + h], self.recv.at[4 + h], peer)
+
+    def over_dp(self):
+        self.own().wait()
+        self.to_core().wait()
+
+        @pl.loop(0, self.net.n_z)
+        def _(z):
+            self.kept[z] = (self.kept[z].astype(F32) + self.from_core[z].astype(F32)).astype(BF)
+
+        for h in range(2):
+            self.first_step(h).start()
+
+    def over_dp_again(self):
+        for h in range(2):
+            self.first_step(h).wait()
+        for h in range(2):
+            mine = self.window(h, self.order[h][0])
+
+            @pl.loop(0, self.net.n_z)
+            def _(z):
+                self.kept[z, :, mine] = (self.kept[z, :, mine].astype(F32) + self.half[h, z].astype(F32)).astype(BF)
+
+        for h in range(2):
+            self.second_step(h).start()
+
+    def over_z(self):
+        net = self.net
+        for h in range(2):
+            self.second_step(h).wait()
+        eighth = self.span // 2
+        for h in range(2):
+            a, b, _, _ = self.order[h]
+            mine = self.window(h, a, b)
+
+            @pl.loop(0, net.n_z)
+            def _(z):
+                total = self.kept[z, :, mine].astype(F32) + self.quarter[h, z].astype(F32)
+                self.part[z, :, h * eighth : (h + 1) * eighth] = total.astype(BF)
+
+        for j in range(1, net.n_z):
+            self.to_z(j).start()
 
 
 class ReduceRows:
@@ -375,15 +457,24 @@
         rows = self.shards[a].shape[0]
         return self.wholes[a].at[pl.ds(pl.multiple_of(owner * rows, rows), rows)]
 
+    def part(self, a, q):
+        rows, columns = self.shards[a].shape
+        n_dp = self.net.n_dp
+        if rows % (16 * n_dp) == 0:
+            some = rows // n_dp
+            return pl.multiple_of(q * some, some), some, 0, columns
+        some = columns // n_dp
+        return 0, rows, pl.multiple_of(q * some, some), some
+
     def piece(self, a, owner, q):
         rows = self.shards[a].shape[0]
-        some = rows // self.net.n_dp
-        return self.wholes[a].at[pl.ds(pl.multiple_of(owner * rows + q * some, some), some)]
+        row, height, column, width = self.part(a, q)
+        return self.wholes[a].at[pl.ds(pl.multiple_of(owner * rows + row, height), height), pl.ds(column, width)]
 
     def along_z(self, a, j):
         net = self.net
-        some = self.shards[a].shape[0] // net.n_dp
-        mine = self.shards[a].at[pl.ds(pl.multiple_of(net.dp * some, some), some)]
+        row, height, column, width = self.part(a, net.dp)
+        mine = self.shards[a].at[pl.ds(row, height), pl.ds(column, width)]
         return remote(mine, self.piece(a, net.wide, net.dp), self.send_z.at[a, j], self.recv_z.at[a, net.z], net.z_peer(j)[1])
 
     def from_z(self, a, j):
@@ -420,13 +511,11 @@
     def own(self, a):
         return pltpu.make_async_copy(self.shards[a], self.block(a, self.net.wide), self.near.at[a])
 
-    def start(self):
-        for a in range(len(self.shards)):
-            for j in range(1, self.net.n_z):
-                self.along_z(a, j).start()
-        for a in range(len(self.shards)):
-            self.across(a, 0).start()
-            self.own(a).start()
+    def start(self, a):
+        for j in range(1, self.net.n_z):
+            self.along_z(a, j).start()
+        self.across(a, 0).start()
+        self.own(a).start()
 
     def relay(self, a):
         net = self.net
@@ -522,7 +611,7 @@
         word_grads, word_row, *refs = refs
     gc_ref, *refs = refs
     if net_sizes:
-        outs, refs = refs[:4], refs[4:]
+        outs, refs = refs[: WORD_PARTS + 3], refs[WORD_PARTS + 3 :]
     accs, refs = refs[:13], refs[13:]
     dga, dsa, dwin, dwout, dgb, dsb, dwup, dub, dwdn, ddb, dqv, dwpj, dpb = accs
     gh1_ref, gm_ref, u_ref, gz_ref, gq_ref, gs_ref, *refs = refs
@@ -538,30 +627,45 @@
     if net_sizes:
         net = Net(*net_sizes)
         ff_grads, at_grads, row, *refs = refs
-        word = Reduce(net, word_grads, *refs[:6], refs[6:8])
-        ff = Reduce(net, ff_grads, *refs[8:14], refs[14:16])
-        att = Reduce(net, at_grads, *refs[16:22], refs[22:24])
-        rowsum = ReduceRows(net, row, *refs[24:27], refs[27:29])
-        keep = refs[29]
+        each = word_grads.shape[-1] // WORD_PARTS
+        words_of = []
+        for part in range(WORD_PARTS):
+            words_of.append(TwoWayReduce(net, word_grads, part * each, *refs[:7], refs[7:9]))
+            refs = refs[9:]
+        ff = Reduce(net, ff_grads, 0, *refs[:6], refs[6:8])
+        att = Reduce(net, at_grads, 0, *refs[8:14], refs[14:16])
+        rowsum = ReduceRows(net, row, *refs[16:19], refs[19:21])
+        keep = refs[21]
 
         @pl.when(now == 0)
         def _():
             peers = [net.sibling] + [net.dp_peer(j)[1] for j in range(1, net.n_dp)] + [net.z_peer(j)[1] for j in range(1, net.n_z)]
             net.greet(peers)
             net.met(peers)
-            word.start()
-
-        schedule = {
-            steps // 4: word.over_dp,
-            steps - steps // 8: word.over_z,
-            steps: ff.start,
-            steps + steps // 8: ff.over_dp,
-            steps + steps // 4: word.back_over_dp,
-            steps + 3 * steps // 8: ff.over_z,
-            steps + 5 * steps // 8: ff.back_over_dp,
-        }
-        for when, act in schedule.items():
-            pl.when(now == when)(act)
+            for part in words_of:
+                part.start()
+
+        one, two, three = words_of
+        schedule = (
+            (2, one.over_dp),
+            (4, one.over_dp_again),
+            (4, two.over_dp),
+            (6, one.over_z),
+            (6, two.over_dp_again),
+            (6, three.over_dp),
+            (8, one.back_over_dp),
+            (8, two.over_z),
+            (8, three.over_dp_again),
+            (8, ff.start),
+            (9, ff.over_dp),
+            (10, two.back_over_dp),
+            (10, three.over_z),
+            (12, three.back_over_dp),
+            (12, ff.over_z),
+            (14, ff.back_over_dp),
+        )
+        for when, act in schedule:
+            pl.when(now == when * steps // 8)(act)
 
     @pl.when(now == 0)
     def _():
@@ -674,16 +778,17 @@
                 column += ref.shape[1]
             att.start()
             rowsum.start()
-            word.finish()
+            for part in words_of:
+                part.finish()
             ff.finish()
             att.over_dp()
             rowsum.over_dp()
             att.over_z()
             rowsum.over_z()
             att.back_over_dp()
-            rowsum.finish(outs[3], places)
+            rowsum.finish(outs[-1], places)
             att.finish()
-            copies = [pltpu.make_async_copy(piece.done, out, keep.at[i]) for i, (piece, out) in enumerate(zip((word, ff, att), outs))]
+            copies = [pltpu.make_async_copy(piece.done, out, keep.at[i]) for i, (piece, out) in enumerate(zip((*words_of, ff, att), outs))]
             for copy in copies:
                 copy.start()
             for copy in copies:
@@ -731,19 +836,19 @@
         ff_width, at_width = ff + out + ff, 4 * width
         row_width = 6 * width + ff + out + word_row.shape[1]
         word_sizes = (wide_d, word_ff)
-        sums = [(n_dp, word_rows, word_width // n_dp), (n_dp, some, ff_width // n_dp), (n_dp, some, at_width // n_dp)]
+        sums = [(n_dp, word_rows, word_width // WORD_PARTS // n_dp)] * WORD_PARTS + [(n_dp, some, ff_width // n_dp), (n_dp, some, at_width // n_dp)]
         pieces = sum(padded(n // n_wide) for n in [width] * 6 + [ff, out] + [wide_d] * 5 + [word_ff])
         out_shapes = [jax.ShapeDtypeStruct((total, width), BF)] + [jax.ShapeDtypeStruct(a, BF) for a in sums] + [jax.ShapeDtypeStruct((1, pieces), F32)]
-        out_specs = [late(rows, width)] + [pl.BlockSpec(memory_space=pl.ANY)] * 3 + [whole_out((1, pieces))]
+        out_specs = [late(rows, width)] + [pl.BlockSpec(memory_space=pl.ANY)] * len(sums) + [whole_out((1, pieces))]
         scratch = (
             [pltpu.VMEM(a, F32) for a in accs]
             + scratch
             + [pltpu.VMEM((n_z, 2, some, ff_width), BF), pltpu.VMEM((n_z, 2, some, at_width), BF), pltpu.VMEM((1, row_width), F32)]
-            + Reduce.scratch(n_dp, n_z, word_rows, word_width)
+            + TwoWayReduce.scratch(n_dp, n_z, word_rows, word_width // WORD_PARTS) * WORD_PARTS
             + Reduce.scratch(n_dp, n_z, some, ff_width)
             + Reduce.scratch(n_dp, n_z, some, at_width)
             + ReduceRows.scratch(n_dp, n_z, row_width)[1:]
-            + [pltpu.SemaphoreType.DMA((3,))]
+            + [pltpu.SemaphoreType.DMA((len(sums),))]
         )
         params = pltpu.CompilerParams(vmem_limit_bytes=VMEM_LIMIT, collective_id=3, has_side_effects=True)
     else:
@@ -763,17 +868,25 @@
     )(*operands)
 
 
-def unpack(done, outs):
-    rows, span = done.shape[1:]
+def unpack(parts, outs, two_way):
+    n_dp, rows, span = parts[0].shape
     for ref, first, columns, side in outs:
         for k in range(side):
             for at in range(0, columns, GROUP):
                 column = first + k * columns + at
-                q, lane = column // span, column % span
-                ref[k * rows : (k + 1) * rows, at : at + GROUP] = done[q, :, lane : lane + GROUP].astype(F32)
-
-
-def output_kernel(gc_low, word_done, ff_done, at_done, row, gc_ref, *outs):
+                part, column = column // (n_dp * span), column % (n_dp * span)
+                if two_way:
+                    eighth = span // 2
+                    h, place, lane = column // (4 * eighth), column // eighth % 4, column % eighth
+                    q = place if h else place // 2 + place % 2 * 2
+                    lane += h * eighth
+                else:
+                    q, lane = column // span, column % span
+                ref[k * rows : (k + 1) * rows, at : at + GROUP] = parts[part][q, :, lane : lane + GROUP].astype(F32)
+
+
+def output_kernel(gc_low, *refs):
+    word_done, (ff_done, at_done, row, gc_ref, *outs) = refs[:WORD_PARTS], refs[WORD_PARTS:]
     gc_ref[...] = gc_low[...].astype(F32)
 
     @pl.when(pl.program_id(0) == 0)
@@ -782,24 +895,23 @@
             oga, osa, owin, owout, ogb, osb, oup, oub, odn, odb, oqv, opj, opb,
             xga, xsa, xwin, xwout, xgb, xsb, xup, xub, xdn, xdb,
         ) = outs
-        for done, across, down in ((word_done, (xwin, xwout, xup), xdn), (ff_done, (oup, opj), odn), (at_done, (owin, owout), None)):
+        for done, across, down in ((word_done, (xwin, xwout, xup), xdn), ([ff_done], (oup, opj), odn), ([at_done], (owin, owout), None)):
             places, column = [], 0
             for ref in across:
                 places.append((ref, column, ref.shape[1], 1))
                 column += ref.shape[1]
             if down is not None:
-                places.append((down, column, down.shape[1], down.shape[0] // done.shape[1]))
-            unpack(done, places)
+                places.append((down, column, down.shape[1], down.shape[0] // done[0].shape[1]))
+            unpack(done, places, len(done) > 1)
         at = 0
         for ref in (oga, osa, ogb, osb, odb, oqv, oub, opb, xga, xsa, xgb, xsb, xdb, xub):
             ref[...] = row[:, at : at + ref.shape[1]]
             at += padded(ref.shape[1])
 
 
-def outputs_of(gc_low, word_done, ff_done, at_done, row, shapes, rows):
+def outputs_of(gc_low, *wholes, shapes, rows):
     total, width = gc_low.shape
     by_row = pl.BlockSpec((rows, width), lambda i: (i, 0))
-    wholes = [word_done, ff_done, at_done, row]
     return pl.pallas_call(
         output_kernel,
         grid=(total // rows,),
@@ -809,6 +921,12 @@
         compiler_params=pltpu.CompilerParams(vmem_limit_bytes=VMEM_LIMIT),
         name="outputs",
     )(gc_low, *wholes)
+
+
+def late_place(net_sizes, steps, step):
+    if not net_sizes:
+        return step
+    return lax.rem((lax.axis_index("wide") + 1) * (steps // net_sizes[1]) + step, steps)
 
 
 def char_forward_kernel(chars_per, steps, net_sizes, lengths, *refs):
@@ -829,63 +947,68 @@
     chunk = min(rows, 512)
     cw = chunk // chars_per
     words = rows // chars_per
+    place = late_place(net_sizes, steps, step)
 
     if net_sizes:
         x_out, win, wout, wup, wdn, wpj, pieces, piece, *refs = refs
-        gather = Gather(net, (*shards, piece), [win, wout, wup, wdn, wpj, pieces], *refs[:3])
-        shared = SharedGather(net, word_shards, word_out, *refs[3:10])
+        gather = Gather(net, (shards[0], shards[1], piece), [win, wout, pieces], *refs[:3])
+        shared = SharedGather(net, (*shards[2:], *word_shards), [wup, wdn, wpj, *word_out], *refs[3:10])
         exchange = Exchange(net, x_out, inbox, *refs[10:13])
         keep = refs[13]
-        first, later = (5, 0, 1), (2, 3, 4)
+        char_weights = (win, wout, wup, wdn, wpj)
 
         @pl.when(now == 0)
         def _():
             peers = [net.wide_peer(j)[1] for j in range(1, net.n_wide)] + [net.dp_peer(j)[1] for j in range(1, net.n_dp)]
             net.greet(peers)
-            net.met(peers)
             for ref, (at, length) in zip(vectors, lengths):
                 some = length // net.n_wide
                 piece[0, :, at : at + some] = ref[...].astype(F32).reshape(1, some)
-            for a in first + later:
+            net.met(peers)
+            for a in (2, 0, 1):
                 gather.start(a)
-            for a in first:
+            for a in (2, 0, 1):
                 gather.relay(a)
-            shared.start()
-            for a in first:
-                gather.finish(a)
+            for a in range(3):
+                shared.start(a)
+            gather.finish(2)
             column = 0
             for at, length in lengths:
                 some = length // net.n_wide
                 row = jnp.concatenate([pieces[w, :, at : at + some] for w in range(net.n_wide)], 1)
                 vec[:, column : column + length] = row
                 column += length
-
-        @pl.when(now == 3 * steps // 8)
-        def _():
-            for a in later:
-                gather.relay(a)
-
-        @pl.when(now == steps)
-        def _():
-            for a in later:
-                gather.finish(a)
-            for a in range(5):
-                pltpu.make_async_copy(gather.wholes[a], char_out[a], keep.at[a]).start()
-
-        for a in range(4):
-
-            @pl.when(now == steps - steps // 4 + a * steps // 8)
-            def _(a=a):
+            gather.finish(0)
+            gather.finish(1)
+
+        def start_words():
+            for a in range(3, 7):
+                shared.start(a)
+
+        def relay_chars():
+            for a in range(3):
                 shared.relay(a)
 
-            @pl.when(now == 2 * steps - 5 * steps // 8 + a * steps // 8)
-            def _(a=a):
+        def pass_on_chars():
+            for a in range(3):
                 shared.pass_on(a)
 
+        def finish_chars():
+            for a in range(3):
+                shared.finish(a)
+            for a, weight in enumerate(char_weights):
+                pltpu.make_async_copy(weight, char_out[a], keep.at[a]).start()
+
+        schedule = [(1, start_words), (2, relay_chars), (5, pass_on_chars), (8, finish_chars)]
+        schedule += [(6 + i, functools.partial(shared.relay, 3 + i)) for i in range(4)]
+        schedule += [(12 + i, functools.partial(shared.pass_on, 3 + i)) for i in range(4)]
+        for when, act in schedule:
+            pl.when(now == when * steps // 8)(act)
+
     ga, sa, gb, sb, db, qv, ub, pb = char_vectors(vec, width, wup.shape[1], wpj.shape[1])
 
     def block(t):
-        return pl.ds(pl.multiple_of(step * rows + t * chunk, chunk), chunk)
+        return pl.ds(pl.multiple_of(place * rows + t * chunk, chunk), chunk)
 
     @pl.when(phase == 0)
     def _():
@@ -914,11 +1037,11 @@
             at = slice(t * chunk, (t + 1) * chunk)
             h1 = c_ref[at, :].astype(F32) + nn(o_ref[at, :], wout[...])
             h1_ref[at, :] = h1.astype(BF)
-            h1_all[block(t), :] = h1
+            h1_all[pl.ds(pl.multiple_of(step * rows + t * chunk, chunk), chunk), :] = h1
 
     @pl.when(phase == 1)
     def _():
-        counts = as_column(cnt_ref[pl.ds(step, 1), :].astype(F32))
+        counts = as_column(cnt_ref[pl.ds(place, 1), :].astype(F32))
         for t in range(rows // chunk):
             at = slice(t * chunk, (t + 1) * chunk)
             wat = slice(t * cw, (t + 1) * cw)
@@ -935,7 +1058,7 @@
         x = (nn(pooled_ref[...], wpj[...]) + pb[...]).astype(BF)
         if net_sizes:
             cap = x_out.shape[1]
-            first_word = step * words
+            first_word = place * words
             target = first_word // cap
             x_out[target, pl.ds(pl.multiple_of(lax.rem(first_word, cap), words), words)] = x
             pl.when(lax.rem(first_word + words, cap) == 0)(lambda: exchange.send_block(target))
@@ -946,11 +1069,11 @@
 
         @pl.when(now == 2 * steps - 1)
         def _():
-            for a in range(4):
+            for a in range(3, 7):
                 shared.finish(a)
             exchange.finish()
-            for a in range(5):
-                pltpu.make_async_copy(gather.wholes[a], char_out[a], keep.at[a]).wait()
+            for a, weight in enumerate(char_weights):
+                pltpu.make_async_copy(weight, char_out[a], keep.at[a]).wait()
 
 
 def char_forward(chars, counts, weights, chars_per, rows, net_sizes=None, word_shards=None, vectors=None, cap=None):
@@ -963,7 +1086,7 @@
         return pl.BlockSpec((count, columns), lambda p, i: (i + p * (steps - 1 - i), 0))
 
     def late(count, columns):
-        return pl.BlockSpec((count, columns), lambda p, i: (i * p, 0))
+        return pl.BlockSpec((count, columns), lambda p, i: (late_place(net_sizes, steps, i * p), 0))
 
     saved = [((words, width), BF, cw, late), ((total, 3 * width), BF, rows, early), ((total, 2 * width), BF, rows, early),
              ((total, width), BF, rows, early), ((total, width), BF, rows, early), ((total, width), BF, rows, late),
@@ -992,8 +1115,8 @@
             [pltpu.VMEM((n_wide, cap, out), BF)]
             + [pltpu.VMEM(a.shape, a.dtype) for a in fulls]
             + [pltpu.VMEM((n_wide, 1, room), F32), pltpu.VMEM((1, 1, room), F32)]
-            + Gather.scratch(6, n_z)
-            + SharedGather.scratch(4, n_dp, n_z)
+            + Gather.scratch(3, n_z)
+            + SharedGather.scratch(7, n_dp, n_z)
             + Exchange.scratch(n_wide)
             + [pltpu.SemaphoreType.DMA((5,))]
         )
@@ -1023,7 +1146,13 @@
     ff = wup.shape[1]
     if net_sizes:
         net = Net(*net_sizes)
-        word_grads, word_row, *refs = refs
+        grads_out, word_row, *refs = refs
+        *held, word_grads, load_sem, store_sem = refs[-7:]
+        refs = refs[:-7]
+        loads = [pltpu.make_async_copy(src, dst, load_sem.at[i]) for i, (src, dst) in enumerate(zip((win, wout, wup, wdn), held))]
+        for load in loads:
+            load.start()
+        win, wout, wup, wdn = held
         dga, dsa, dgb, dsb, ddb, dub = word_vectors(word_row, width, ff)
     else:
         dga, dsa, dwin, dwout, dgb, dsb, dwup, dub, dwdn, ddb, *refs = refs
@@ -1036,6 +1165,10 @@
         exchange = Exchange(net, back_ref, back_out, *sems)
         peers = [net.wide_peer(j)[1] for j in range(1, net.n_wide)]
         net.greet(peers)
+    def ready(i):
+        if net_sizes:
+            loads[i].wait()
+
     named = jnp.where(bucket[...] == lax.broadcasted_iota(jnp.int32, (owners, length), 0), 1.0, 0.0)
     ri = lax.broadcasted_iota(jnp.int32, (length, length), 0)
     ci = lax.broadcasted_iota(jnp.int32, (length, length), 1)
@@ -1046,6 +1179,7 @@
     x = tn(hot, arrived[...].reshape(slots, width))
     n1, r1 = normal_of(x)
     a = (n1 * ga[...] + sa[...]).astype(BF)
+    ready(0)
     qkv = nn(a, win[...])
     qkv_ref[:, :width] = (qkv[:, :width] * HD**-0.5).astype(BF)
     qkv_ref[:, width:] = qkv[:, width:].astype(BF)
@@ -1061,12 +1195,15 @@
         soft = jnp.concatenate([softmax_low(s[:, h * length : (h + 1) * length] + bias) for h in range(2)], 1)
         p_ref[:, 2 * p * length : (2 * p + 2) * length] = soft
         mix_ref[:, p * GROUP : (p + 1) * GROUP] = nn(soft, two_heads(v)).astype(BF)
+    ready(1)
     inner = x + nn(mix_ref[...], wout[...])
     n2, r2 = normal_of(inner)
     u = (n2 * gb[...] + sb[...]).astype(BF)
+    ready(2)
     h, slope = gelu_and_slope(nn(u, wup[...]) + ub[...])
     h_ref[...] = h.astype(BF)
     s_ref[...] = slope
+    ready(3)
     out_ref[...] = inner + (nn(h_ref[...], wdn[...]) + db[...])
     g = grad_ref[...]
     gz = (nt(g, wdn[...]) * s_ref[...]).astype(BF)
@@ -1098,15 +1235,22 @@
             for w in range(net.n_wide):
                 word_grads[w // 2, w % 2, :, column : column + value.shape[1]] = value[w * some : (w + 1) * some]
 
+        def store(i, first, columns):
+            window = pl.ds(first, columns)
+            return pltpu.make_async_copy(word_grads.at[:, :, :, window], grads_out.at[:, :, :, window], store_sem.at[i])
+
         put(tn(a, gq_ref[...]), 0)
         put(tn(mix_ref[...], g1_low), 3 * width)
+        store(0, 0, 4 * width).start()
         put(tn(u, gz), 4 * width)
+        store(1, 4 * width, ff).start()
         down = tn(h_ref[...], g).astype(BF)
         for w in range(net.n_wide):
             for k in range(side):
                 first = (w * side + k) * some
                 column = 4 * width + ff + k * width
                 word_grads[w // 2, w % 2, :, column : column + width] = down[first : first + some]
+        store(2, 4 * width + ff, ff).start()
     else:
         back_out[...] = back
         dwin[...] = tn(a, gq_ref[...])
@@ -1121,6 +1265,8 @@
     ddb[...] = column_sum(g.astype(F32))
     if net_sizes:
         exchange.finish()
+        for i, (first, columns) in enumerate(((0, 4 * width), (4 * width, ff), (4 * width + ff, ff))):
+            store(i, first, columns).wait()
 
 
 def word_block(arrived, bucket, assign, segments, grad, weights, slot_cap, net_sizes=None):
@@ -1136,17 +1282,22 @@
     if net_sizes:
         n_dp, n_wide = net_sizes
         out_shapes += [low(n_wide // 2, 2, width // n_wide, 4 * width + 2 * ff), full(1, 5 * width + ff)]
-        out_specs = [vmem, pl.BlockSpec(memory_space=pl.ANY), vmem, vmem]
+        anywhere = pl.BlockSpec(memory_space=pl.ANY)
+        out_specs = [vmem, anywhere, anywhere, vmem]
+        in_specs = [vmem] * 5 + [anywhere] * 4 + [vmem]
         scratch += [pltpu.VMEM((owners, slot_cap, width), BF)] + Exchange.scratch(n_wide)
+        scratch += [pltpu.VMEM(w.shape, BF) for w in weights[:4]] + [pltpu.VMEM(out_shapes[2].shape, BF)]
+        scratch += [pltpu.SemaphoreType.DMA((4,)), pltpu.SemaphoreType.DMA((3,))]
         params = pltpu.CompilerParams(vmem_limit_bytes=VMEM_LIMIT, collective_id=2, has_side_effects=True)
     else:
         row = full(1, width)
         out_shapes += [row, row, full(width, 3 * width), full(width, width), row, row, full(width, ff), full(1, ff), full(ff, width), row]
         out_specs += [vmem] * 10
+        in_specs = [vmem] * 10
         params = pltpu.CompilerParams(vmem_limit_bytes=VMEM_LIMIT)
     return pl.pallas_call(
         functools.partial(word_kernel, slot_cap, net_sizes),
-        in_specs=[vmem] * 10,
+        in_specs=in_specs,
         out_specs=out_specs,
         out_shape=out_shapes,
         scratch_shapes=scratch,
@@ -1191,6 +1342,8 @@
         and cap % (block // chars_per) == 0
         and (4 * width) % (GROUP * n_dp) == 0
         and n_wide % 2 == 0
+        and n_dp == 4
+        and (4 * word_up.shape[0] * n_wide + 2 * word_up.shape[1]) % (8 * GROUP * WORD_PARTS) == 0
     )
     bucket, names, upstream = buckets.reshape(1, -1), assign[None], out_grad[0]
     if fast:
@@ -1204,7 +1357,7 @@
                   char_down_bias, pool_query, char_proj, char_proj_bias, word_gain, word_shift, word_inproj, word_outproj, word_gain_mid,
                   word_shift_mid, word_up, word_up_bias, word_down, word_down_bias)
         shapes = [p.shape if p.ndim == 2 else (1, *p.shape) for p in params]
-        char_grads, *grads = outputs_of(*sums, shapes, block)
+        char_grads, *grads = outputs_of(*sums, shapes=shapes, rows=block)
         grads = [g[0] if g.shape[0] == 1 else g for g in grads]
     else:
         vec = jnp.concatenate([gathered(v) for v in vectors]).astype(F32)[None]

time: 237 us -> 205 us (0.86)
  Pallas kernels: 235 us -> 203 us
    pallas_call x1, Pallas kernels: 117 us -> 96.6 us  [char_backward(): pl.pallas_call(functools.partial(char_back_kernel, chars_per, steps, net_...]
    pallas_call x1, Pallas kernels: 87.7 us -> 75.2 us  [char_forward(): pl.pallas_call(functools.partial(char_forward_kernel, chars_per, steps, n...]
where the time goes in v4:
time: 205 us
  Pallas kernels  203 us (99%)
    pallas_call x1, Pallas kernels, char_backward(): pl.pallas_call(functools.partial(char_back_kernel, chars_per, steps, net_...  96.6 us
    pallas_call x1, Pallas kernels, char_forward(): pl.pallas_call(functools.partial(char_forward_kernel, chars_per, steps, n...  75.2 us
    pallas_call x1, Pallas kernels, word_block(): pl.pallas_call(functools.partial(word_kernel, slot_cap, net_sizes), in_sp...  22.7 us
    pallas_call x1, Pallas kernels, outputs_of(): pl.pallas_call(output_kernel, grid=(total // rows,), in_specs=[by_row] +...  8.63 us

profile of v4, /device:TPU:0, one launch (start us, length us, event | category | flops | bytes accessed | tf_op | source)
XLA Modules:
  0.0 204.6 jit_solution(18005929663462544867)
XLA Ops:
  0.7 75.2 %char_forward.1 = (bf16[8,64,512]{2,1,0:T(8,128)(2,1)}, f32[1,7680]{1,0:T(1,128)}, bf16[256,768]{1,0:T(8,128)(2,1)}, bf16[256,256]{1,0:T(8,128)(2,1)}, bf16[256,...) custom-call(bf16[8192,256]{1,0:T(8,128)(2,1)} %bitcast.22, ...), custom_call_target="tpu_custom_call" | custom-call | tf_op jit(solution)/shard_map/char_forward/pallas_call | solution.py:1131
  75.9 22.7 %word_block.1 = (f32[256,512]{1,0:T(8,128)}, bf16[8,64,512]{2,1,0:T(8,128)(2,1)}, bf16[4,2,64,6144]{3,2,1,0:T(8,128)(2,1)}, f32[1,4608]{1,0:T(1,128)}) custom-call(bf16[8,64,512]{2,1,0:T(8,128)(2,1)} %get-tuple-element.79.refs_0_, s32[1,256]{1,0:T(1,128)} %bitcast.30, s32[1,8]{1,0:T(1,128)} %bitcast.31, s32[1,256]{1,0:T(1,128)} %refs_3_.3, ...), custom_call_target="tpu_custom_call" | custom-call | tf_op jit(solution)/shard_map/word_block/pallas_call | solution.py:1298
  98.6 96.6 %char_backward.1 = (bf16[8192,256]{1,0:T(8,128)(2,1)}, bf16[4,64,512]{2,1,0:T(8,128)(2,1)}, bf16[4,64,512]{2,1,0:T(8,128)(2,1)}, bf16[4,64,512]{2,1,0:T(8,128)(2...) custom-call(bf16[512,512]{1,0:T(8,128)(2,1)} %bitcast.24, ...), custom_call_target="tpu_custom_call" | custom-call | tf_op jit(solution)/shard_map/char_backward/pallas_call | solution.py:859
  195.2 0.0 copy-start
  195.2 8.6 %outputs.1 = (f32[8192,256]{1,0:T(8,128)}, f32[1,32]{1,0:T(1,128)}, f32[1,32]{1,0:T(1,128)}, f32[32,768]{1,0:T(8,128)}, f32[32,256]{1,0:T(8,128)}, /*index=5*/f3...) custom-call(bf16[8192,256]{1,0:T(8,128)(2,1)} %get-tuple-element.102, ...), custom_call_target="tpu_custom_call" | custom-call | tf_op jit(solution)/shard_map/outputs/pallas_call | solution.py:915
  203.8 0.0 copy-done
  203.8 0.8 copy.55
Async XLA Ops:
  195.2 8.7 %copy-start = (f32[256,512]{1,0:T(8,128)S(1)}, f32[256,512]{1,0:T(8,128)}, u32[]{:S(2)}) copy-start(f32[256,512]{1,0:T(8,128)} %get-tuple-element.85) | copy-start | bytes 1572868

commit v5 on v4

--- a/solution.py
+++ b/solution.py
@@ -11,6 +11,7 @@
 NEG = -1e30
 ROOT_HALF = 0.7071067811865476
 INV_ROOT_TWO_PI = 0.3989422804014327
+LOG2_E = 1.4426950408889634
 HD = 64
 GROUP = 128
 F32 = jnp.float32
@@ -52,8 +53,9 @@
 
 
 def gelu_and_slope(z):
-    cdf = 0.5 * (1.0 + lax.erf(z * ROOT_HALF))
-    return z * cdf, cdf + z * jnp.exp(-0.5 * z * z) * INV_ROOT_TWO_PI
+    w = z * ROOT_HALF
+    cdf = 0.5 + 0.5 * lax.erf(w)
+    return z * cdf, cdf + (z * INV_ROOT_TWO_PI) * jnp.exp2((w * w) * -LOG2_E)
 
 
 def softmax_low(s):
@@ -647,22 +649,22 @@
 
         one, two, three = words_of
         schedule = (
-            (2, one.over_dp),
-            (4, one.over_dp_again),
-            (4, two.over_dp),
+            (1, one.over_dp),
+            (2, two.over_dp),
+            (3, one.over_dp_again),
+            (4, three.over_dp),
+            (5, two.over_dp_again),
             (6, one.over_z),
-            (6, two.over_dp_again),
-            (6, three.over_dp),
-            (8, one.back_over_dp),
+            (7, three.over_dp_again),
             (8, two.over_z),
-            (8, three.over_dp_again),
             (8, ff.start),
-            (9, ff.over_dp),
-            (10, two.back_over_dp),
+            (9, one.back_over_dp),
             (10, three.over_z),
-            (12, three.back_over_dp),
-            (12, ff.over_z),
-            (14, ff.back_over_dp),
+            (10, ff.over_dp),
+            (11, two.back_over_dp),
+            (13, three.back_over_dp),
+            (13, ff.over_z),
+            (15, ff.back_over_dp),
         )
         for when, act in schedule:
             pl.when(now == when * steps // 8)(act)
@@ -1156,7 +1158,7 @@
         dga, dsa, dgb, dsb, ddb, dub = word_vectors(word_row, width, ff)
     else:
         dga, dsa, dwin, dwout, dgb, dsb, dwup, dub, dwdn, ddb, *refs = refs
-    qkv_ref, p_ref, mix_ref, h_ref, s_ref, gq_ref, *refs = refs
+    qkv_ref, p_ref, mix_ref, h_ref, s_ref, gq_ref, gs_ref, *refs = refs
     ga, sa, gb, sb, db, ub = word_vectors(vec, width, ff)
     owners = assign.shape[1]
     slots = owners * slot_cap
@@ -1189,12 +1191,18 @@
     def pair(p):
         return [qkv_ref[:, i * width + p * GROUP : i * width + (p + 1) * GROUP] for i in range(3)]
 
-    for p in range(width // GROUP):
-        q, k, v = pair(p)
+    pairs = range(width // GROUP)
+
+    def both(p):
+        return slice(2 * p * length, (2 * p + 2) * length)
+
+    for p in pairs:
+        q, k, _ = pair(p)
         s = nt(q, two_heads(k))
-        soft = jnp.concatenate([softmax_low(s[:, h * length : (h + 1) * length] + bias) for h in range(2)], 1)
-        p_ref[:, 2 * p * length : (2 * p + 2) * length] = soft
-        mix_ref[:, p * GROUP : (p + 1) * GROUP] = nn(soft, two_heads(v)).astype(BF)
+        for h in range(2):
+            p_ref[:, (2 * p + h) * length : (2 * p + h + 1) * length] = softmax_low(s[:, h * length : (h + 1) * length] + bias)
+    for p in pairs:
+        mix_ref[:, p * GROUP : (p + 1) * GROUP] = nn(p_ref[:, both(p)], two_heads(pair(p)[2])).astype(BF)
     ready(1)
     inner = x + nn(mix_ref[...], wout[...])
     n2, r2 = normal_of(inner)
@@ -1211,15 +1219,18 @@
     g1 = g.astype(F32) + norm_back(du, n2, r2, gb[...])
     g1_low = g1.astype(BF)
     gm = nt(g1_low, wout[...]).astype(BF)
-    for p in range(width // GROUP):
-        q, k, v = pair(p)
-        gmp = gm[:, p * GROUP : (p + 1) * GROUP]
-        soft = p_ref[:, 2 * p * length : (2 * p + 2) * length]
-        dp = nt(gmp, two_heads(v))
-        gs = jnp.concatenate([softmax_back(soft[:, h * length : (h + 1) * length], dp[:, h * length : (h + 1) * length]) for h in range(2)], 1)
+    for p in pairs:
+        dp = nt(gm[:, p * GROUP : (p + 1) * GROUP], two_heads(pair(p)[2]))
+        for h in range(2):
+            lanes = slice((2 * p + h) * length, (2 * p + h + 1) * length)
+            gs_ref[:, lanes] = softmax_back(p_ref[:, lanes], dp[:, h * length : (h + 1) * length])
+    for p in pairs:
+        q, k, _ = pair(p)
+        gs = gs_ref[:, both(p)]
         gq_ref[:, p * GROUP : (p + 1) * GROUP] = (nn(gs, two_heads(k)) * HD**-0.5).astype(BF)
         gq_ref[:, width + p * GROUP : width + (p + 1) * GROUP] = one_of_two(tn(gs, q)).astype(BF)
-        gq_ref[:, 2 * width + p * GROUP : 2 * width + (p + 1) * GROUP] = one_of_two(tn(soft, gmp)).astype(BF)
+        gmp = gm[:, p * GROUP : (p + 1) * GROUP]
+        gq_ref[:, 2 * width + p * GROUP : 2 * width + (p + 1) * GROUP] = one_of_two(tn(p_ref[:, both(p)], gmp)).astype(BF)
     da = nt(gq_ref[...], win[...])
     gx = (g1 + norm_back(da, n1, r1, ga[...])).astype(BF)
     back = nn(hot, gx).astype(BF).reshape(owners, slot_cap, width)
@@ -1278,7 +1289,8 @@
     vmem = pl.BlockSpec(memory_space=pltpu.VMEM)
     out_shapes, out_specs = [full(length, width), low(owners, slot_cap, width)], [vmem, vmem]
     scratch = [pltpu.VMEM((length, 3 * width), BF), pltpu.VMEM((length, width // HD * length), BF), pltpu.VMEM((length, width), BF),
-               pltpu.VMEM((length, ff), BF), pltpu.VMEM((length, ff), F32), pltpu.VMEM((length, 3 * width), BF)]
+               pltpu.VMEM((length, ff), BF), pltpu.VMEM((length, ff), F32), pltpu.VMEM((length, 3 * width), BF),
+               pltpu.VMEM((length, width // HD * length), BF)]
     if net_sizes:
         n_dp, n_wide = net_sizes
         out_shapes += [low(n_wide // 2, 2, width // n_wide, 4 * width + 2 * ff), full(1, 5 * width + ff)]
@@ -1357,7 +1369,7 @@
                   char_down_bias, pool_query, char_proj, char_proj_bias, word_gain, word_shift, word_inproj, word_outproj, word_gain_mid,
                   word_shift_mid, word_up, word_up_bias, word_down, word_down_bias)
         shapes = [p.shape if p.ndim == 2 else (1, *p.shape) for p in params]
-        char_grads, *grads = outputs_of(*sums, shapes=shapes, rows=block)
+        char_grads, *grads = outputs_of(*sums, shapes=shapes, rows=min(2048, rows.shape[0]))
         grads = [g[0] if g.shape[0] == 1 else g for g in grads]
     else:
         vec = jnp.concatenate([gathered(v) for v in vectors]).astype(F32)[None]

time: 205 us -> 196 us (0.956)
  Pallas kernels: 203 us -> 194 us
    pallas_call x1, Pallas kernels: 96.6 us -> 91.5 us  [char_backward(): pl.pallas_call(functools.partial(char_back_kernel, chars_per, steps, net_...]
where the time goes in v5:
time: 196 us
  Pallas kernels  194 us (99%)
    pallas_call x1, Pallas kernels, char_backward(): pl.pallas_call(functools.partial(char_back_kernel, chars_per, steps, net_...  91.5 us
    pallas_call x1, Pallas kernels, char_forward(): pl.pallas_call(functools.partial(char_forward_kernel, chars_per, steps, n...  74.4 us
    pallas_call x1, Pallas kernels, word_block(): pl.pallas_call(functools.partial(word_kernel, slot_cap, net_sizes), in_sp...  21.3 us
    pallas_call x1, Pallas kernels, outputs_of(): pl.pallas_call(output_kernel, grid=(total // rows,), in_specs=[by_row] +...  7.2 us

profile of v5, /device:TPU:0, one launch (start us, length us, event | category | flops | bytes accessed | tf_op | source)
XLA Modules:
  0.0 195.9 jit_solution(7366884060850613361)
XLA Ops:
  0.7 74.4 %char_forward.1 = (bf16[8,64,512]{2,1,0:T(8,128)(2,1)}, f32[1,7680]{1,0:T(1,128)}, bf16[256,768]{1,0:T(8,128)(2,1)}, bf16[256,256]{1,0:T(8,128)(2,1)}, bf16[256,...) custom-call(bf16[8192,256]{1,0:T(8,128)(2,1)} %bitcast.22, ...), custom_call_target="tpu_custom_call" | custom-call | tf_op jit(solution)/shard_map/char_forward/pallas_call | solution.py:1133
  75.0 21.3 %word_block.1 = (f32[256,512]{1,0:T(8,128)}, bf16[8,64,512]{2,1,0:T(8,128)(2,1)}, bf16[4,2,64,6144]{3,2,1,0:T(8,128)(2,1)}, f32[1,4608]{1,0:T(1,128)}) custom-call(bf16[8,64,512]{2,1,0:T(8,128)(2,1)} %get-tuple-element.79.refs_0_, s32[1,256]{1,0:T(1,128)} %bitcast.30, s32[1,8]{1,0:T(1,128)} %bitcast.31, s32[1,256]{1,0:T(1,128)} %refs_3_.3, ...), custom_call_target="tpu_custom_call" | custom-call | tf_op jit(solution)/shard_map/word_block/pallas_call | solution.py:1310
  96.3 91.5 %char_backward.1 = (bf16[8192,256]{1,0:T(8,128)(2,1)}, bf16[4,64,512]{2,1,0:T(8,128)(2,1)}, bf16[4,64,512]{2,1,0:T(8,128)(2,1)}, bf16[4,64,512]{2,1,0:T(8,128)(2...) custom-call(bf16[512,512]{1,0:T(8,128)(2,1)} %bitcast.24, ...), custom_call_target="tpu_custom_call" | custom-call | tf_op jit(solution)/shard_map/char_backward/pallas_call | solution.py:861
  187.9 0.0 copy-start
  187.9 7.2 %outputs.1 = (f32[8192,256]{1,0:T(8,128)}, f32[1,32]{1,0:T(1,128)}, f32[1,32]{1,0:T(1,128)}, f32[32,768]{1,0:T(8,128)}, f32[32,256]{1,0:T(8,128)}, /*index=5*/f3...) custom-call(bf16[8192,256]{1,0:T(8,128)(2,1)} %get-tuple-element.102, ...), custom_call_target="tpu_custom_call" | custom-call | tf_op jit(solution)/shard_map/outputs/pallas_call | solution.py:917
  195.1 0.0 copy-done
  195.1 0.8 copy.55
Async XLA Ops:
  187.9 7.2 %copy-start = (f32[256,512]{1,0:T(8,128)S(1)}, f32[256,512]{1,0:T(8,128)}, u32[]{:S(2)}) copy-start(f32[256,512]{1,0:T(8,128)} %get-tuple-element.85) | copy-start | bytes 1572868

commit v6 on v5

--- a/solution.py
+++ b/solution.py
@@ -696,7 +696,7 @@
             gy = gh2.astype(BF)
             ddb[...] += column_sum(gy.astype(F32))
             gm_ref[at, :] = gy
-            gz = (nt(gy, wdn[...]) * s_ref[at, :].astype(F32)).astype(BF)
+            gz = nt(gy, wdn[...]).astype(BF) * s_ref[at, :]
             gz_ref[at, :] = gz
             dub[...] += column_sum(gz.astype(F32))
             du = nt(gz, wup[...])
@@ -942,14 +942,25 @@
         win, wout, wup, wdn, wpj, vec, *refs = refs
         x_ref, *refs = refs
     pooled_ref, qkv_ref, p_ref, o_ref, h1_ref, h2_ref, m_ref, s_ref, *refs = refs
-    h1_all, *refs = refs
-    rows, width = c_ref.shape
+    h1_all, c_all, n_all, c_sem, *refs = refs
+    rows, width = c_ref.shape[0] // steps, c_ref.shape[1]
     phase, step = pl.program_id(0), pl.program_id(1)
     now = phase * steps + step
     chunk = min(rows, 512)
     cw = chunk // chars_per
     words = rows // chars_per
     place = late_place(net_sizes, steps, step)
+    load = pltpu.make_async_copy(c_ref, c_all, c_sem)
+
+    def normalize():
+        load.wait()
+
+        @pl.loop(0, steps * rows // chunk)
+        def _(t):
+            at = pl.ds(pl.multiple_of(t * chunk, chunk), chunk)
+            n_all[at, :], _ = normal_of(c_all[at, :].astype(F32))
+
+    pl.when(now == 0)(load.start)
 
     if net_sizes:
         x_out, win, wout, wup, wdn, wpj, pieces, piece, *refs = refs
@@ -969,6 +980,7 @@
             net.met(peers)
             for a in (2, 0, 1):
                 gather.start(a)
+            normalize()
             for a in (2, 0, 1):
                 gather.relay(a)
             for a in range(3):
@@ -1007,6 +1019,9 @@
         for when, act in schedule:
             pl.when(now == when * steps // 8)(act)
 
+    else:
+        pl.when(now == 0)(normalize)
+
     ga, sa, gb, sb, db, qv, ub, pb = char_vectors(vec, width, wup.shape[1], wpj.shape[1])
 
     def block(t):
@@ -1014,8 +1029,7 @@
 
     @pl.when(phase == 0)
     def _():
-        n, _ = normal_of(c_ref[...].astype(F32))
-        a = (n * ga[...] + sa[...]).astype(BF)
+        a = (n_all[pl.ds(pl.multiple_of(step * rows, rows), rows), :] * ga[...] + sa[...]).astype(BF)
         qkv = nn(a, win[...])
         qkv_ref[:, :width] = (qkv[:, :width] * HD**-0.5).astype(BF)
         qkv_ref[:, width:] = qkv[:, width:].astype(BF)
@@ -1037,9 +1051,10 @@
             o_ref[at, p * GROUP : (p + 1) * GROUP] = nn(p_ref[at, 2 * p * GROUP : 2 * (p + 1) * GROUP], two_heads(head_pair(at, p, 2))).astype(BF)
         for t in range(rows // chunk):
             at = slice(t * chunk, (t + 1) * chunk)
-            h1 = c_ref[at, :].astype(F32) + nn(o_ref[at, :], wout[...])
+            here = pl.ds(pl.multiple_of(step * rows + t * chunk, chunk), chunk)
+            h1 = c_all[here, :].astype(F32) + nn(o_ref[at, :], wout[...])
             h1_ref[at, :] = h1.astype(BF)
-            h1_all[pl.ds(pl.multiple_of(step * rows + t * chunk, chunk), chunk), :] = h1
+            h1_all[here, :] = h1
 
     @pl.when(phase == 1)
     def _():
@@ -1095,10 +1110,10 @@
              ((total, ff), BF, rows, late), ((total, ff), BF, rows, late)]
     saved_specs = [where(count, s[1]) for s, _, count, where in saved]
     saved_shapes = [jax.ShapeDtypeStruct(s, d) for s, d, _, _ in saved]
-    in_specs = [early(rows, width), whole_block(counts.shape)]
+    anywhere = pl.BlockSpec(memory_space=pl.ANY)
+    in_specs = [anywhere, whole_block(counts.shape)]
     operands = [chars, counts]
-    scratch = [pltpu.VMEM((total, width), F32)]
-    anywhere = pl.BlockSpec(memory_space=pl.ANY)
+    scratch = [pltpu.VMEM((total, width), F32), pltpu.VMEM((total, width), BF), pltpu.VMEM((total, width), F32), pltpu.SemaphoreType.DMA(())]
     if net_sizes:
         n_dp, n_wide = net_sizes
         n_z = n_wide // 2

time: 196 us -> 193 us (0.985)
  Pallas kernels: 194 us -> 192 us
where the time goes in v6:
time: 193 us
  Pallas kernels  192 us (99%)
    pallas_call x1, Pallas kernels, char_backward(): pl.pallas_call(functools.partial(char_back_kernel, chars_per, steps, net_...  90.2 us
    pallas_call x1, Pallas kernels, char_forward(): pl.pallas_call(functools.partial(char_forward_kernel, chars_per, steps, n...  72.6 us
    pallas_call x1, Pallas kernels, word_block(): pl.pallas_call(functools.partial(word_kernel, slot_cap, net_sizes), in_sp...  21.8 us
    pallas_call x1, Pallas kernels, outputs_of(): pl.pallas_call(output_kernel, grid=(total // rows,), in_specs=[by_row] +...  7.2 us

profile of v6, /device:TPU:0, one launch (start us, length us, event | category | flops | bytes accessed | tf_op | source)
XLA Modules:
  0.0 193.2 jit_solution(4584160943403956875)
XLA Ops:
  0.7 72.6 %char_forward.1 = (bf16[8,64,512]{2,1,0:T(8,128)(2,1)}, f32[1,7680]{1,0:T(1,128)}, bf16[256,768]{1,0:T(8,128)(2,1)}, bf16[256,256]{1,0:T(8,128)(2,1)}, bf16[256,...) custom-call(bf16[8192,256]{1,0:T(8,128)(2,1)} %bitcast.22, ...), custom_call_target="tpu_custom_call" | custom-call | tf_op jit(solution)/shard_map/char_forward/pallas_call | solution.py:1148
  73.3 21.8 %word_block.1 = (f32[256,512]{1,0:T(8,128)}, bf16[8,64,512]{2,1,0:T(8,128)(2,1)}, bf16[4,2,64,6144]{3,2,1,0:T(8,128)(2,1)}, f32[1,4608]{1,0:T(1,128)}) custom-call(bf16[8,64,512]{2,1,0:T(8,128)(2,1)} %get-tuple-element.79.refs_0_, s32[1,256]{1,0:T(1,128)} %bitcast.30, s32[1,8]{1,0:T(1,128)} %bitcast.31, s32[1,256]{1,0:T(1,128)} %refs_3_.3, ...), custom_call_target="tpu_custom_call" | custom-call | tf_op jit(solution)/shard_map/word_block/pallas_call | solution.py:1325
  95.0 90.2 %char_backward.1 = (bf16[8192,256]{1,0:T(8,128)(2,1)}, bf16[4,64,512]{2,1,0:T(8,128)(2,1)}, bf16[4,64,512]{2,1,0:T(8,128)(2,1)}, bf16[4,64,512]{2,1,0:T(8,128)(2...) custom-call(bf16[512,512]{1,0:T(8,128)(2,1)} %bitcast.24, ...), custom_call_target="tpu_custom_call" | custom-call | tf_op jit(solution)/shard_map/char_backward/pallas_call | solution.py:861
  185.2 0.0 copy-start
  185.2 7.2 %outputs.1 = (f32[8192,256]{1,0:T(8,128)}, f32[1,32]{1,0:T(1,128)}, f32[1,32]{1,0:T(1,128)}, f32[32,768]{1,0:T(8,128)}, f32[32,256]{1,0:T(8,128)}, /*index=5*/f3...) custom-call(bf16[8192,256]{1,0:T(8,128)(2,1)} %get-tuple-element.102, ...), custom_call_target="tpu_custom_call" | custom-call | tf_op jit(solution)/shard_map/outputs/pallas_call | solution.py:917
  192.4 0.0 copy-done
  192.4 0.8 copy.55
Async XLA Ops:
  185.2 7.2 %copy-start = (f32[256,512]{1,0:T(8,128)S(1)}, f32[256,512]{1,0:T(8,128)}, u32[]{:S(2)}) copy-start(f32[256,512]{1,0:T(8,128)} %get-tuple-element.85) | copy-start | bytes 1572868

commit v7 on v6

--- a/solution.py
+++ b/solution.py
@@ -56,6 +56,19 @@
     w = z * ROOT_HALF
     cdf = 0.5 + 0.5 * lax.erf(w)
     return z * cdf, cdf + (z * INV_ROOT_TWO_PI) * jnp.exp2((w * w) * -LOG2_E)
+
+
+def two_terms(x):
+    high = x.astype(BF)
+    return high, (x - high.astype(F32)).astype(BF)
+
+
+def norm_vector_grads(weight, weight_grad, upstream_sum, gain, shift):
+    shift_grad = sum(nt(jnp.broadcast_to(part, (8, part.shape[1])), weight) for part in two_terms(upstream_sum))[:1]
+    product = weight.astype(F32) * weight_grad
+    ones = jnp.ones((8, weight.shape[1]), BF)
+    both = sum(nt(ones, part) for part in two_terms(product))[:1]
+    return (both - shift * shift_grad) / gain, shift_grad
 
 
 def softmax_low(s):
@@ -701,12 +714,14 @@
             dub[...] += column_sum(gz.astype(F32))
             du = nt(gz, wup[...])
             n, r = normal_of(h1_ref[at, :].astype(F32))
-            dgb[...] += column_sum(du * n)
-            dsb[...] += column_sum(du)
             u_ref[at, :] = (n * gb[...] + sb[...]).astype(BF)
             gh1_ref[pl.ds(pl.multiple_of(step * rows + t * chunk, chunk), chunk), :] = (gh2 + norm_back(du, n, r, gb[...])).astype(BF)
         dwup[...] += tn(u_ref[...], gz_ref[...])
         dwdn[...] += tn(gm_ref[...], m_ref[...])
+
+    @pl.when(now == steps - 1)
+    def _():
+        dgb[...], dsb[...] = norm_vector_grads(wup[...], dwup[...], dub[...], gb[...], sb[...])
 
     if net_sizes:
         n_z, n_wide = net.n_z, net.n_wide
@@ -780,19 +795,18 @@
                 column += ref.shape[1]
             att.start()
             rowsum.start()
-            for part in words_of:
-                part.finish()
-            ff.finish()
             att.over_dp()
             rowsum.over_dp()
+            copies = [pltpu.make_async_copy(piece.done, out, keep.at[i]) for i, (piece, out) in enumerate(zip((*words_of, ff, att), outs))]
+            for piece, copy in zip((*words_of, ff), copies):
+                piece.finish()
+                copy.start()
             att.over_z()
             rowsum.over_z()
             att.back_over_dp()
             rowsum.finish(outs[-1], places)
             att.finish()
-            copies = [pltpu.make_async_copy(piece.done, out, keep.at[i]) for i, (piece, out) in enumerate(zip((*words_of, ff, att), outs))]
-            for copy in copies:
-                copy.start()
+            copies[-1].start()
             for copy in copies:
                 copy.wait()
 

time: 193 us -> 193 us (level)
  no operation moved by 1% of the time
where the time goes in v7:
time: 193 us
  Pallas kernels  192 us (99%)
    pallas_call x1, Pallas kernels, char_backward(): pl.pallas_call(functools.partial(char_back_kernel, chars_per, steps, net_...  90.1 us
    pallas_call x1, Pallas kernels, char_forward(): pl.pallas_call(functools.partial(char_forward_kernel, chars_per, steps, n...  72.6 us
    pallas_call x1, Pallas kernels, word_block(): pl.pallas_call(functools.partial(word_kernel, slot_cap, net_sizes), in_sp...  21.8 us
    pallas_call x1, Pallas kernels, outputs_of(): pl.pallas_call(output_kernel, grid=(total // rows,), in_specs=[by_row] +...  7.2 us

profile of v7, /device:TPU:0, one launch (start us, length us, event | category | flops | bytes accessed | tf_op | source)
XLA Modules:
  0.0 193.1 jit_solution(4343208580139978339)
XLA Ops:
  0.7 72.6 %char_forward.1 = (bf16[8,64,512]{2,1,0:T(8,128)(2,1)}, f32[1,7680]{1,0:T(1,128)}, bf16[256,768]{1,0:T(8,128)(2,1)}, bf16[256,256]{1,0:T(8,128)(2,1)}, bf16[256,...) custom-call(bf16[8192,256]{1,0:T(8,128)(2,1)} %bitcast.22, ...), custom_call_target="tpu_custom_call" | custom-call | tf_op jit(solution)/shard_map/char_forward/pallas_call | solution.py:1162
  73.3 21.8 %word_block.1 = (f32[256,512]{1,0:T(8,128)}, bf16[8,64,512]{2,1,0:T(8,128)(2,1)}, bf16[4,2,64,6144]{3,2,1,0:T(8,128)(2,1)}, f32[1,4608]{1,0:T(1,128)}) custom-call(bf16[8,64,512]{2,1,0:T(8,128)(2,1)} %get-tuple-element.79.refs_0_, s32[1,256]{1,0:T(1,128)} %bitcast.30, s32[1,8]{1,0:T(1,128)} %bitcast.31, s32[1,256]{1,0:T(1,128)} %refs_3_.3, ...), custom_call_target="tpu_custom_call" | custom-call | tf_op jit(solution)/shard_map/word_block/pallas_call | solution.py:1339
  95.0 90.1 %char_backward.1 = (bf16[8192,256]{1,0:T(8,128)(2,1)}, bf16[4,64,512]{2,1,0:T(8,128)(2,1)}, bf16[4,64,512]{2,1,0:T(8,128)(2,1)}, bf16[4,64,512]{2,1,0:T(8,128)(2...) custom-call(bf16[512,512]{1,0:T(8,128)(2,1)} %bitcast.24, ...), custom_call_target="tpu_custom_call" | custom-call | tf_op jit(solution)/shard_map/char_backward/pallas_call | solution.py:875
  185.1 0.0 copy-start
  185.1 7.2 %outputs.1 = (f32[8192,256]{1,0:T(8,128)}, f32[1,32]{1,0:T(1,128)}, f32[1,32]{1,0:T(1,128)}, f32[32,768]{1,0:T(8,128)}, f32[32,256]{1,0:T(8,128)}, /*index=5*/f3...) custom-call(bf16[8192,256]{1,0:T(8,128)(2,1)} %get-tuple-element.102, ...), custom_call_target="tpu_custom_call" | custom-call | tf_op jit(solution)/shard_map/outputs/pallas_call | solution.py:931
  192.3 0.0 copy-done
  192.3 0.8 copy.55
Async XLA Ops:
  185.1 7.2 %copy-start = (f32[256,512]{1,0:T(8,128)S(1)}, f32[256,512]{1,0:T(8,128)}, u32[]{:S(2)}) copy-start(f32[256,512]{1,0:T(8,128)} %get-tuple-element.85) | copy-start | bytes 1572868
